TPU v7x, 128 devices: a whole 4x4x4 slice. The times are simulated.
128 devices in a mesh: dom: 32 (over x, z, core), sub: 4 (over y).
Axes of the slice: x: 4, y: 4, z: 4, core: 2. Of those that a mesh axis runs over, the one named last changes fastest.
Arguments:
- dofs: float32 [9, 20, 65536], P(None, None, ('dom', 'sub')), may hold values from -6 to 6
- star: float32 [3, 9, 9, 65536], P(None, None, None, ('dom', 'sub')), may hold values from -1.25 to 1.25
- stiff: float32 [3, 20, 20], replicated, may hold values from -1.25 to 1.25
- flux_local: float32 [4, 20, 20], replicated, may hold values from -1.25 to 1.25
- flux_neighbor: float32 [4, 12, 20, 20], replicated, may hold values from -1.25 to 1.25
- solver_minus: float32 [4, 9, 9, 65536], P(None, None, None, ('dom', 'sub')), may hold values from -1 to 1
- solver_plus: float32 [4, 9, 9, 65536], P(None, None, None, ('dom', 'sub')), may hold values from -1 to 1
- neighbor: int32 [4, 65536], P(None, ('dom', 'sub')), may hold values from 0 to 767
- orientation: int32 [4, 65536], P(None, ('dom', 'sub')), may hold values from 0 to 11
- copy_list: int32 [2, 16384], P(None, ('dom', 'sub')), may hold values from 0 to 511
- face_lift: float32 [4, 10, 20], replicated, may hold values from -1.25 to 1.25
- face_eval: float32 [25, 10], replicated, may hold values from -2 to 2
- face_weight: float32 [10, 25], replicated, may hold values from -1.25 to 1.25
- side_owner: int32 [65536, 2], P(('dom', 'sub')), may hold values from 0 to 127, as said below
- side_face: int32 [65536, 2], P(('dom', 'sub')), may hold values from 0 to 2047
- impedance: float32 [4, 65536], P(None, ('dom', 'sub')), may hold values from 0.5 to 2
- normal_initial: float32 [25, 65536], P(None, ('dom', 'sub')), may hold values from -3 to -1
- shear_initial: float32 [2, 25, 65536], P(None, None, ('dom', 'sub')), may hold values from -6 to 6
- slip: float32 [25, 65536], P(None, ('dom', 'sub')), may hold values from 0 to 1
- static_friction: float32 [25, 65536], P(None, ('dom', 'sub')), may hold values from 0.5 to 0.8
- friction_drop: float32 [25, 65536], P(None, ('dom', 'sub')), may hold values from 0.1 to 0.4
- slip_scale: float32 [25, 65536], P(None, ('dom', 'sub')), may hold values from 0.2 to 0.8
Outputs:
- new_dofs: float32 [9, 20, 65536], P(None, None, ('dom', 'sub'))
- new_slip: float32 [25, 65536], P(None, ('dom', 'sub'))
- traction: float32 [2, 25, 65536], P(None, None, ('dom', 'sub'))
Inputs may be any that keep to these rules, and one draw needn't show every extreme that they name: `side_owner`: the two sides of a fault face lie on devices whose indices differ by one; among the 512 faces of one device, no device holds more than 24 sides, and in every such block some device holds exactly 24.
All inputs are finite; a program needn't handle non-finite values.
Results may differ from a plain program's by a relative error of at most 0.0001.
Values sent between devices are 32-bit elements; how exact they have to be, the bound alone decides.
No kernel may reach another device: no remote copies, remote signals or barrier semaphores. Data moves between devices by JAX's collectives and lax.ppermute only.
A program may use at most 256 MiB of HBM per device.

v0:
```python
import jax
import jax.numpy as jnp
from jax import lax
from jax.sharding import PartitionSpec as P

time_step = 0.8
trace_rows = (0, 3, 5, 6, 7, 8)


def from_behind(block, axis, distance):
    devices = range(lax.axis_size(axis))
    route = [(i - distance, i) for i in devices if i - distance in devices]
    return lax.ppermute(block, axis, route)


def predictor(dofs, star, stiff):
    highest = lax.Precision.HIGHEST
    current = dofs
    integral = time_step * dofs
    factor = time_step
    for order in range(1, 4):
        moved = jnp.einsum("dbc,qce->dqbe", stiff, current, precision=highest)
        current = -jnp.einsum("dqpe,dqbe->pbe", star, moved, precision=highest)
        factor = factor * time_step / (order + 1)
        integral = integral + factor * current
    return integral


def friction(
    minus,
    plus,
    impedance,
    normal_initial,
    shear_initial,
    slip,
    static_friction,
    friction_drop,
    slip_scale,
):
    pwave_minus = impedance[0][None, :]
    pwave_plus = impedance[1][None, :]
    swave_minus = impedance[2][None, :]
    swave_plus = impedance[3][None, :]
    normal = (
        pwave_plus * minus[0]
        + pwave_minus * plus[0]
        + pwave_minus * pwave_plus * (plus[3] - minus[3])
    ) / (pwave_minus + pwave_plus)
    swave_sum = swave_minus + swave_plus
    viscous = swave_minus * swave_plus / swave_sum
    shear = (
        swave_plus * minus[1:3]
        + swave_minus * plus[1:3]
        + swave_minus * swave_plus * (plus[4:6] - minus[4:6])
    ) / swave_sum + shear_initial
    weakened = jnp.minimum(slip / slip_scale, 1.0)
    coefficient = static_friction - friction_drop * weakened
    strength = coefficient * jnp.maximum(-(normal + normal_initial), 0.0)
    magnitude = jnp.sqrt(shear[0] * shear[0] + shear[1] * shear[1])
    ratio = jnp.minimum(1.0, strength / jnp.maximum(magnitude, 1.0))
    final = shear * ratio
    rates = (shear - final) / viscous
    new_slip = slip + time_step * jnp.sqrt(rates[0] * rates[0] + rates[1] * rates[1])
    imposed = final - shear_initial
    jump_minus = normal - minus[0]
    jump_plus = normal - plus[0]
    delta_minus = jnp.stack(
        [
            jump_minus,
            imposed[0] - minus[1],
            imposed[1] - minus[2],
            jump_minus / pwave_minus,
            (imposed[0] - minus[1]) / swave_minus,
            (imposed[1] - minus[2]) / swave_minus,
        ]
    )
    delta_plus = jnp.stack(
        [
            jump_plus,
            imposed[0] - plus[1],
            imposed[1] - plus[2],
            -jump_plus / pwave_plus,
            -(imposed[0] - plus[1]) / swave_plus,
            -(imposed[1] - plus[2]) / swave_plus,
        ]
    )
    return (new_slip, final, delta_minus, delta_plus)


def per_device(
    dofs,
    star,
    stiff,
    flux_local,
    flux_neighbor,
    solver_minus,
    solver_plus,
    neighbor,
    orientation,
    copy_list,
    face_lift,
    face_eval,
    face_weight,
    side_owner,
    side_face,
    impedance,
    normal_initial,
    shear_initial,
    slip,
    static_friction,
    friction_drop,
    slip_scale,
):
    highest = lax.Precision.HIGHEST
    count = dofs.shape[2]
    points = face_eval.shape[0]
    devices = lax.axis_size(("dom", "sub"))
    faults = side_owner.shape[0]
    capacity = max(2, 6 * faults // devices)
    total_slots = devices * capacity
    owners = jnp.transpose(side_owner).reshape(-1)
    wanted = jnp.transpose(side_face).reshape(-1)
    onehot = (owners[:, None] == jnp.arange(devices, dtype=jnp.int32)[None, :]).astype(jnp.int32)
    before = jnp.cumsum(onehot, axis=0) - onehot
    position = jnp.sum(before * onehot, axis=1)
    slots = owners * capacity + position
    request = (
        jnp.full((total_slots,), -1, jnp.int32).at[slots].set(wanted).reshape(devices, capacity)
    )
    source = (
        jnp.zeros((total_slots,), jnp.int32).at[slots].set(jnp.arange(2 * faults, dtype=jnp.int32))
    )
    filled = jnp.zeros((total_slots,), jnp.float32).at[slots].set(1.0)
    asked = lax.all_to_all(request, ("dom", "sub"), split_axis=0, concat_axis=0, tiled=True)
    asked = asked.reshape(-1)
    integral = predictor(dofs, star, stiff)
    to_lower = jnp.take(integral, copy_list[0], axis=2)
    to_upper = jnp.take(integral, copy_list[1], axis=2)
    from_lower = from_behind(to_upper, ("dom", "sub"), 1)
    from_upper = from_behind(to_lower, ("dom", "sub"), -1)
    present = asked >= 0
    safe = jnp.where(present, asked, 0)
    element = safe % count
    face_index = safe // count
    select = (face_index[None, :] == jnp.arange(4, dtype=jnp.int32)[:, None]).astype(jnp.float32)
    rows = jnp.array(trace_rows, dtype=jnp.int32)
    columns = jnp.take(jnp.take(integral, rows, axis=0), element, axis=2)
    every_face = jnp.einsum("fmc,kcn->fkmn", face_lift, columns, precision=highest)
    modal = jnp.einsum("fkmn,fn->kmn", every_face, select, precision=highest)
    payload = jnp.einsum("gm,kmn->kgn", face_eval, modal, precision=highest) / time_step
    inner = payload.shape[1]
    arrived = lax.all_to_all(
        payload.reshape(6 * inner, devices, capacity),
        ("dom", "sub"),
        split_axis=1,
        concat_axis=1,
        tiled=True,
    )
    arrived = arrived.reshape(6, inner, total_slots)
    moved = jnp.einsum("dcb,qce->dqbe", stiff, integral, precision=highest)
    volume = jnp.einsum("dqpe,dqbe->pbe", star, moved, precision=highest)
    projected = jnp.einsum("fbc,qce->fqbe", flux_local, integral, precision=highest)
    local = jnp.einsum("fqpe,fqbe->pbe", solver_minus, projected, precision=highest)
    received = jnp.take(arrived, slots, axis=2)
    sides = received.reshape(6, points, 2, faults)
    new_slip, traction, delta_minus, delta_plus = friction(
        sides[:, :, 0],
        sides[:, :, 1],
        impedance,
        normal_initial,
        shear_initial,
        slip,
        static_friction,
        friction_drop,
        slip_scale,
    )
    outgoing = jnp.concatenate([delta_minus, delta_plus], axis=2)
    reply = jnp.take(outgoing, source, axis=2) * filled[None, None, :]
    returned = lax.all_to_all(
        reply.reshape(6 * inner, devices, capacity),
        ("dom", "sub"),
        split_axis=1,
        concat_axis=1,
        tiled=True,
    )
    returned = returned.reshape(6, inner, total_slots)
    extended = jnp.concatenate([integral, from_lower, from_upper], axis=2)
    combos = jnp.arange(flux_neighbor.shape[1], dtype=jnp.int32)[:, None]
    neighbour = jnp.zeros_like(dofs)
    for face in range(4):
        gathered = jnp.take(extended, neighbor[face], axis=2)
        every_combo = jnp.einsum("abc,qce->aqbe", flux_neighbor[face], gathered, precision=highest)
        picked = (orientation[face][None, :] == combos).astype(jnp.float32)
        chosen = jnp.einsum("aqbe,ae->qbe", every_combo, picked, precision=highest)
        neighbour = neighbour + jnp.einsum(
            "qpe,qbe->pbe", solver_plus[face], chosen, precision=highest
        )
    weighted = jnp.einsum("mg,kgn->kmn", face_weight, returned, precision=highest)
    every_lift = jnp.einsum("fmc,kmn->fkcn", face_lift, weighted, precision=highest)
    masked = select * present.astype(jnp.float32)[None, :]
    contrib = jnp.einsum("fkcn,fn->kcn", every_lift, masked, precision=highest)
    placing = (element[:, None] == jnp.arange(count, dtype=jnp.int32)[None, :]).astype(jnp.float32)
    fault_sum = jnp.einsum("kcn,ne->kce", contrib, placing, precision=highest)
    empty_row = jnp.zeros_like(dofs[0])
    fault = jnp.stack(
        [
            fault_sum[0],
            empty_row,
            empty_row,
            fault_sum[1],
            empty_row,
            fault_sum[2],
            fault_sum[3],
            fault_sum[4],
            fault_sum[5],
        ]
    )
    new_dofs = dofs + volume - local - neighbour + fault
    return (new_dofs, new_slip, traction)


def solution(mesh):
    in_specs = (
        P(None, None, ("dom", "sub")),
        P(None, None, None, ("dom", "sub")),
        P(),
        P(),
        P(),
        P(None, None, None, ("dom", "sub")),
        P(None, None, None, ("dom", "sub")),
        P(None, ("dom", "sub")),
        P(None, ("dom", "sub")),
        P(None, ("dom", "sub")),
        P(),
        P(),
        P(),
        P(("dom", "sub"), None),
        P(("dom", "sub"), None),
        P(None, ("dom", "sub")),
        P(None, ("dom", "sub")),
        P(None, None, ("dom", "sub")),
        P(None, ("dom", "sub")),
        P(None, ("dom", "sub")),
        P(None, ("dom", "sub")),
        P(None, ("dom", "sub")),
    )
    out_specs = (
        P(None, None, ("dom", "sub")),
        P(None, ("dom", "sub")),
        P(None, None, ("dom", "sub")),
    )
    return jax.shard_map(
        per_device, mesh=mesh, in_specs=in_specs, out_specs=out_specs, check_vma=False
    )
```

profile of v0, /device:TPU:1, one launch (start us, length us, event | category | flops | bytes accessed | tf_op | source)
XLA Modules:
  0.0 640.3 jit_solution(16754944353800740470)
XLA Ops:
  4.3 4.3 scatter_custom_fusion
  9.4 11.9 %all-to-all-start = ((s32[128,1,24]{2,1,0:T(1,128)}), s32[128,1,24]{2,1,0:T(1,128)S(1)}, u32[]{:S(2)}, u32[]{:S(2)}) async-start(s32[128,1,24]{2,1,0:T(1,128)} %bitcast.96), calls=%async_computation | async-start | bytes 131072 | tf_op jit(solution)/shard_map/all_to_all | solution.py:134
  24.3 9.0 %copy.442 = f32[3,9,20,512]{2,1,0,3:T(8,128)} copy(f32[3,9,20,512]{3,2,0,1:T(8,128)S(1)} %convolution_bitcast_fusion.8) | data formatting | bytes 2211840 | tf_op jit(solution)/shard_map/dbc,qce->dqbe/transpose | solution.py:22
  33.3 7.6 %copy.443 = f32[3,9,9,512]{1,2,0,3:T(8,128)} copy(f32[3,9,9,512]{3,0,2,1:T(4,128)S(1)} %copy-done.8) | data formatting | bytes 995328 | tf_op args[1]
  40.9 20.3 %convolution_bitcast_fusion.3 = f32[512,20,9]{1,2,0:T(8,128)} fusion(f32[3,9,20,512]{2,1,0,3:T(8,128)} %copy.442, f32[3,9,9,512]{1,2,0,3:T(8,128)} %copy.443), kind=kOutput, calls=%fused_computation.62 | convolution fusion | flops 29859840 | bytes 1972224 | tf_op jit(solution)/shard_map/dqpe,dqbe->pbe/dot_general | solution.py:23
  65.2 9.0 %copy.445 = f32[3,9,20,512]{2,1,0,3:T(8,128)} copy(f32[3,9,20,512]{3,2,0,1:T(8,128)S(1)} %convolution_bitcast_fusion.7) | data formatting | bytes 2211840 | tf_op jit(solution)/shard_map/dbc,qce->dqbe/transpose | solution.py:22
  74.2 20.8 %convolution_bitcast_fusion.2 = f32[512,20,9]{1,2,0:T(8,128)} fusion(f32[3,9,20,512]{2,1,0,3:T(8,128)} %copy.445, f32[3,9,9,512]{1,2,0,3:T(8,128)} %copy.443), kind=kOutput, calls=%fused_computation.61 | convolution fusion | flops 29859840 | bytes 1972224 | tf_op jit(solution)/shard_map/dqpe,dqbe->pbe/dot_general | solution.py:23
  99.0 9.0 %copy.448 = f32[3,9,20,512]{2,1,0,3:T(8,128)} copy(f32[3,9,20,512]{3,2,0,1:T(8,128)S(1)} %convolution_bitcast_fusion.6) | data formatting | bytes 2211840 | tf_op jit(solution)/shard_map/dbc,qce->dqbe/transpose | solution.py:22
  108.0 20.4 %convolution_bitcast_fusion.1 = f32[512,20,9]{1,2,0:T(8,128)} fusion(f32[3,9,20,512]{2,1,0,3:T(8,128)} %copy.448, f32[3,9,9,512]{1,2,0,3:T(8,128)} %copy.443), kind=kOutput, calls=%fused_computation.60 | convolution fusion | flops 29859840 | bytes 1972224 | tf_op jit(solution)/shard_map/dqpe,dqbe->pbe/dot_general | solution.py:23
  139.2 4.9 collective-permute-start.1
  152.3 4.5 scatter_custom_fusion.1
  169.9 9.0 %copy.452 = f32[3,9,20,512]{2,1,0,3:T(8,128)} copy(f32[3,9,20,512]{3,2,0,1:T(8,128)S(1)} %convolution_bitcast_fusion.5) | data formatting | bytes 2211840 | tf_op jit(solution)/shard_map/dcb,qce->dqbe/transpose | solution.py:160
  178.8 20.3 %fusion.123 = f32[512,20,9,1]{1,2,3,0:T(8,128)} fusion(f32[3,9,20,512]{2,1,0,3:T(8,128)} %copy.452, f32[3,9,9,512]{1,2,0,3:T(8,128)} %copy.443), kind=kOutput, calls=%fused_computation.269 | convolution fusion | flops 29859840 | bytes 1972224 | tf_op jit(solution)/shard_map/dqpe,dqbe->pbe/dot_general | solution.py:161
  204.7 4.3 scatter_custom_fusion.2
  225.7 14.7 %copy.456 = f32[4,9,20,512]{2,1,0,3:T(8,128)} copy(f32[4,9,20,512]{3,2,0,1:T(8,128)} %convolution_bitcast_fusion.4) | data formatting | bytes 2949120 | tf_op jit(solution)/shard_map/fbc,qce->fqbe/transpose | solution.py:162
  240.4 14.0 %copy.457 = f32[4,9,9,512]{1,2,0,3:T(8,128)} copy(f32[4,9,9,512]{3,0,2,1:T(4,128)S(1)} %copy-done.7) | data formatting | bytes 1327104 | tf_op args[5]
  257.3 26.0 %gather_fusion.1 = f32[3072,6,20]{2,1,0:T(8,128)} fusion(f32[6,20,512]{1,0,2:T(8,128)S(1)} %copy.481, s32[3072]{0:T(1024)S(1)} %broadcast_clamp_fusion), kind=kCustom, calls=%fused_computation.7 | custom fusion | bytes 2961408 | tf_op jit(solution)/shard_map/jit(_take)/gather | solution.py:147
  283.4 12.2 %select_bitcast_fusion = f32[6,20,3072,1]{1,0,2,3:T(8,128)S(1)} fusion(f32[3072,6,20]{2,1,0:T(8,128)} %gather_fusion.1, pred[3072]{0:T(1024)(128)(4,1)S(1)} %get-tuple-element.46), kind=kLoop, calls=%fused_computation.13 | loop fusion | flops 368640 | bytes 2952192 | tf_op jit(solution)/shard_map/jit(_take)/select_n | solution.py:147
  295.7 12.8 %fusion.10 = f32[3072,6,10]{0,2,1:T(8,128)S(1)} fusion(f32[6,20,3072,1]{1,0,2,3:T(8,128)S(1)} %select_bitcast_fusion, f32[3072,4]{0,1:T(4,128)S(1)} %fusion.82, f32[4,10,20]{2,0,1:T(4,128)S(1)} %copy-done.23), kind=kOutput, calls=%fused_computation.31 | convolution fusion | flops 178237440 | bytes 2264192 | tf_op jit(solution)/shard_map/fmc,kcn->fkmn/dot_general | solution.py:148
  310.6 8.9 %reshape.855 = f32[150,128,24]{2,1,0:T(8,128)} reshape(f32[6,25,3072]{2,1,0:T(8,128)S(1)} %fusion.27) | data formatting | bytes 3686400 | tf_op jit(solution)/shard_map/reshape | solution.py:153
  319.5 9.2 %copy.484 = f32[150,128,24]{0,2,1:T(8,128)} copy(f32[150,128,24]{2,1,0:T(8,128)} %reshape.855) | data formatting | bytes 3686400 | tf_op jit(solution)/shard_map/reshape | solution.py:153
  328.7 13.1 %all-to-all-start.1 = ((f32[150,128,24]{0,2,1:T(8,128)}), f32[150,128,24]{0,2,1:T(8,128)}, u32[]{:S(2)}, u32[]{:S(2)}) async-start(f32[150,128,24]{0,2,1:T(8,128)} %copy.484), calls=%async_computation.1 | async-start | bytes 6291456 | tf_op jit(solution)/shard_map/all_to_all | solution.py:152
  342.9 4.9 copy.462
  347.8 5.7 gather_fusion.9
  357.5 5.3 fusion.6
  366.5 5.7 gather_fusion.8
  376.6 5.3 fusion.7
  385.7 5.7 gather_fusion.7
  391.4 5.7 gather_fusion.6
  401.3 5.3 fusion.8
  414.2 5.3 fusion.9
  423.4 10.2 %fusion.15 = f32[512,20,9]{1,2,0:T(8,128)} fusion(f32[1,9,9,512]{1,2,3,0:T(8,128)} %copy.599, f32[512,9,20]{2,1,0:T(8,128)} %copy.554), kind=kOutput, calls=%fused_computation.36 | convolution fusion | flops 9953280 | bytes 903168 | tf_op jit(solution)/shard_map/qpe,qbe->pbe/dot_general | solution.py:195
  433.6 8.5 %reshape.1020 = f32[6,25,3072]{1,0,2:T(8,128)} reshape(f32[150,128,24]{0,2,1:T(8,128)} %all-to-all-done.1) | data formatting | bytes 3686400 | tf_op jit(solution)/shard_map/reshape | solution.py:159
  442.1 12.8 %gather_fusion.2 = f32[1024,6,25]{2,1,0:T(8,128)} fusion(f32[6,25,3072]{1,0,2:T(8,128)} %reshape.1020, s32[1024]{0:T(1024)S(1)} %broadcast_clamp_fusion.1), kind=kCustom, calls=%fused_computation.8 | custom fusion | bytes 1232896 | tf_op jit(solution)/shard_map/jit(_take)/gather | solution.py:164
  463.1 25.5 %gather_fusion.3 = f32[3072,6,25]{2,1,0:T(8,128)} fusion(f32[6,25,1024]{1,0,2:T(8,128)} %copy.506, s32[3072]{0:T(1024)S(1)} %copy-done.25), kind=kCustom, calls=%fused_computation.9 | custom fusion | bytes 3698688 | tf_op jit(solution)/shard_map/jit(_take)/gather | solution.py:178
  488.6 7.6 %reshape.1021 = f32[150,128,24]{0,2,1:T(8,128)S(1)} reshape(f32[6,25,3072]{1,0,2:T(8,128)} %bitcast.448) | data formatting | bytes 3686400 | tf_op jit(solution)/shard_map/jit(_take)/gather | solution.py:178
  496.3 7.7 %copy.582 = f32[150,128,24]{2,1,0:T(8,128)} copy(f32[150,128,24]{0,2,1:T(8,128)S(1)} %reshape.1021) | data formatting | bytes 3686400 | tf_op jit(solution)/shard_map/jit(_take)/gather | solution.py:178
  503.9 9.8 %select_multiply_fusion = f32[150,128,24]{2,1,0:T(8,128)} fusion(f32[150,128,24]{2,1,0:T(8,128)} %copy.582, f32[128,24]{1,0:T(8,128)S(1)} %mul.290, pred[128,24]{1,0:T(8,128)(4,1)S(1)} %copy-done.21), kind=kLoop, calls=%fused_computation.14 | loop fusion | flops 921600 | bytes 3701760 | tf_op jit(solution)/shard_map/mul | solution.py:178
  513.7 9.6 %copy.508 = f32[150,128,24]{0,2,1:T(8,128)} copy(f32[150,128,24]{2,1,0:T(8,128)} %select_multiply_fusion) | data formatting | bytes 3686400 | tf_op jit(solution)/shard_map/mul | solution.py:178
  523.4 9.8 %all-to-all-start.2 = ((f32[150,128,24]{0,2,1:T(8,128)}), f32[150,128,24]{0,2,1:T(8,128)S(1)}, u32[]{:S(2)}, u32[]{:S(2)}) async-start(f32[150,128,24]{0,2,1:T(8,128)} %copy.508), calls=%async_computation.2 | async-start | bytes 6291456 | tf_op jit(solution)/shard_map/all_to_all | solution.py:179
  533.2 10.3 %fusion.18 = f32[512,20,9]{1,2,0:T(8,128)} fusion(f32[1,9,9,512]{1,2,3,0:T(8,128)} %copy.597, f32[512,9,20]{2,1,0:T(8,128)} %copy.546), kind=kOutput, calls=%fused_computation.39 | convolution fusion | flops 9953280 | bytes 903168 | tf_op jit(solution)/shard_map/qpe,qbe->pbe/dot_general | solution.py:195
  543.5 5.7 fusion.21
  549.2 5.8 fusion.24
  555.8 19.5 %all-to-all-done.2 = f32[150,128,24]{0,2,1:T(8,128)S(1)} async-done(((f32[150,128,24]{0,2,1:T(8,128)}), f32[150,128,24]{0,2,1:T(8,128)S(1)}, u32[]{:S(2)}, u32[]{:S(2)}) %all-to-all-start.2) | async-done | bytes 1843232 | tf_op jit(solution)/shard_map/all_to_all | solution.py:179
  575.4 7.7 %copy.509 = f32[150,128,24]{2,1,0:T(8,128)} copy(f32[150,128,24]{0,2,1:T(8,128)S(1)} %all-to-all-done.2) | data formatting | bytes 3686400 | tf_op jit(solution)/shard_map/all_to_all | solution.py:179
  583.0 9.5 %reshape.857 = f32[6,25,3072]{2,1,0:T(8,128)S(1)} reshape(f32[150,128,24]{2,1,0:T(8,128)} %copy.509) | data formatting | bytes 3686400 | tf_op jit(solution)/shard_map/reshape | solution.py:186
  594.4 6.3 fusion.2
  606.9 29.7 %fusion.14 = f32[9,20,512]{1,0,2:T(8,128)} fusion(f32[9,20,512]{1,0,2:T(8,128)} %copy.511, f32[9,20,512]{1,0,2:T(8,128)} %copy.454, f32[512,20,9,1]{1,2,3,0:T(8,128)} %fusion.123, f32[512,20,9]{1,2,0:T(8,128)} %fusion.15, f32[512,20,9]{1,2,0:T(8,128)} %fusion.18, f32[512,20,9]{1,2,0:T(8,128)} %fusion.24, f32[512,20,9]{1,2,0:T(8,128)} %fusion.21, ...), kind=kOutput, calls=%fused_computation.34 | convolution fusion | flops 40458240 | bytes 5087232 | tf_op jit(solution)/shard_map/fqpe,fqbe->pbe/dot_general | solution.py:163
  (220 shorter events, 127.1 us)
Async XLA Ops:
  0.6 21.4 %copy-start = (f32[3,20,20]{2,1,0:T(8,128)S(1)}, f32[3,20,20]{2,1,0:T(8,128)}, u32[]{:S(2)}) copy-start(f32[3,20,20]{2,1,0:T(8,128)} %param.29) | copy-start | bytes 14404
  9.4 245.1 %all-to-all-start = ((s32[128,1,24]{2,1,0:T(1,128)}), s32[128,1,24]{2,1,0:T(1,128)S(1)}, u32[]{:S(2)}, u32[]{:S(2)}) async-start(s32[128,1,24]{2,1,0:T(1,128)} %bitcast.96), calls=%async_computation | async-start | bytes 131072 | tf_op jit(solution)/shard_map/all_to_all | solution.py:134
  24.3 9.0 %copy-start.8 = (f32[3,9,9,512]{3,0,2,1:T(4,128)S(1)}, f32[3,9,9,512]{3,0,2,1:T(4,128)}, u32[]{:S(2)}) copy-start(f32[3,9,9,512]{3,0,2,1:T(4,128)} %param.28) | copy-start | bytes 1492996
  135.2 15.0 %copy-start.38 = (s32[4,512]{1,0:T(4,128)S(1)}, s32[4,512]{1,0:T(4,128)}, u32[]{:S(2)}) copy-start(s32[4,512]{1,0:T(4,128)} %param.34) | copy-start | bytes 24580
  138.0 20.7 %copy-start.39 = (s32[4,512]{1,0:T(4,128)S(1)}, s32[4,512]{1,0:T(4,128)}, u32[]{:S(2)}) copy-start(s32[4,512]{1,0:T(4,128)} %param.35) | copy-start | bytes 24580
  138.0 20.7 %copy-start.40 = (f32[4,512]{1,0:T(4,128)S(1)}, f32[4,512]{1,0:T(4,128)}, u32[]{:S(2)}) copy-start(f32[4,512]{1,0:T(4,128)} %param.42) | copy-start | bytes 24580
  138.0 22.6 %copy-start.20 = (s32[512,2]{0,1:T(2,128)S(1)}, s32[512,2]{0,1:T(2,128)}, u32[]{:S(2)}) copy-start(s32[512,2]{0,1:T(2,128)} %param.40) | copy-start | bytes 12292
  139.2 27.8 %copy-start.22 = (f32[4,20,20]{2,0,1:T(4,128)S(1)}, f32[4,20,20]{2,0,1:T(4,128)}, u32[]{:S(2)}) copy-start(f32[4,20,20]{2,0,1:T(4,128)} %param.30) | copy-start | bytes 19204
  139.2 202.6 %collective-permute-start.1 = (f32[9,20,128]{2,1,0:T(8,128)}, f32[9,20,128]{2,1,0:T(8,128)}, u32[]{:S(2)}, u32[]{:S(2)}) collective-permute-start(f32[9,20,128]{2,1,0:T(8,128)} %copy.461), channel_id=1, source_target_pairs={{1,0},{2,1},{3,2},{4,3},{5,4},{6,5},{7,6},{8,7},{9,8},{10,9},{11,1... | collective-permute-start | bytes 276488 | tf_op jit(solution)/shard_map/ppermute | solution.py:13
  148.2 193.7 %collective-permute-start = (f32[9,20,128]{2,1,0:T(8,128)}, f32[9,20,128]{2,1,0:T(8,128)}, u32[]{:S(2)}, u32[]{:S(2)}) collective-permute-start(f32[9,20,128]{2,1,0:T(8,128)} %copy.459), channel_id=1, source_target_pairs={{0,1},{1,2},{2,3},{3,4},{4,5},{5,6},{6,7},{7,8},{8,9},{9,10},{10,1... | collective-permute-start | bytes 276488 | tf_op jit(solution)/shard_map/ppermute | solution.py:13
  178.8 21.5 %copy-start.45 = (s32[6]{0:T(128)S(1)}, s32[6]{0:T(128)}, u32[]{:S(2)}) copy-start(s32[6]{0:T(128)} %constant.147) | copy-start | bytes 76
  225.7 14.7 %copy-start.7 = (f32[4,9,9,512]{3,0,2,1:T(4,128)S(1)}, f32[4,9,9,512]{3,0,2,1:T(4,128)}, u32[]{:S(2)}) copy-start(f32[4,9,9,512]{3,0,2,1:T(4,128)} %param.32) | copy-start | bytes 1990660
  283.4 12.2 %copy-start.23 = (f32[4,10,20]{2,0,1:T(4,128)S(1)}, f32[4,10,20]{2,0,1:T(4,128)}, u32[]{:S(2)}) copy-start(f32[4,10,20]{2,0,1:T(4,128)} %param.37) | copy-start | bytes 9604
  295.6 12.8 %copy-start.32 = (f32[25,10]{0,1:T(8,128)S(1)}, f32[25,10]{0,1:T(8,128)}, u32[]{:S(2)}) copy-start(f32[25,10]{0,1:T(8,128)} %param.38) | copy-start | bytes 3004
  328.7 104.9 %all-to-all-start.1 = ((f32[150,128,24]{0,2,1:T(8,128)}), f32[150,128,24]{0,2,1:T(8,128)}, u32[]{:S(2)}, u32[]{:S(2)}) async-start(f32[150,128,24]{0,2,1:T(8,128)} %copy.484), calls=%async_computation.1 | async-start | bytes 6291456 | tf_op jit(solution)/shard_map/all_to_all | solution.py:152
  342.9 10.7 %copy-start.44 = (pred[512]{0:T(512)(128)(4,1)S(1)}, pred[512]{0:T(512)(128)(4,1)}, u32[]{:S(2)}) copy-start(pred[512]{0:T(512)(128)(4,1)} %compare_and_fusion.3) | copy-start | bytes 1540
  353.6 4.0 copy-start.15
  353.6 4.0 copy-start.27
  357.5 9.1 %copy-start.31 = (s32[1024]{0:T(1024)S(1)}, s32[1024]{0:T(1024)}, u32[]{:S(2)}) copy-start(s32[1024]{0:T(1024)} %get-tuple-element.94) | copy-start | bytes 12292
  357.5 14.8 %copy-start.43 = (pred[512]{0:T(512)(128)(4,1)S(1)}, pred[512]{0:T(512)(128)(4,1)}, u32[]{:S(2)}) copy-start(pred[512]{0:T(512)(128)(4,1)} %compare_and_fusion.4) | copy-start | bytes 1540
  372.3 4.3 copy-start.14
  372.3 4.3 copy-start.26
  376.6 9.1 %copy-start.30 = (s32[1024]{0:T(1024)S(1)}, s32[1024]{0:T(1024)}, u32[]{:S(2)}) copy-start(s32[1024]{0:T(1024)} %get-tuple-element.95) | copy-start | bytes 12292
  376.6 14.8 %copy-start.29 = (s32[1024]{0:T(1024)S(1)}, s32[1024]{0:T(1024)}, u32[]{:S(2)}) copy-start(s32[1024]{0:T(1024)} %get-tuple-element.96) | copy-start | bytes 12292
  376.6 20.5 %copy-start.42 = (pred[512]{0:T(512)(128)(4,1)S(1)}, pred[512]{0:T(512)(128)(4,1)}, u32[]{:S(2)}) copy-start(pred[512]{0:T(512)(128)(4,1)} %compare_and_fusion.5) | copy-start | bytes 1540
  397.2 4.1 copy-start.13
  401.3 9.0 %copy-start.41 = (pred[512]{0:T(512)(128)(4,1)S(1)}, pred[512]{0:T(512)(128)(4,1)}, u32[]{:S(2)}) copy-start(pred[512]{0:T(512)(128)(4,1)} %compare_and_fusion.6) | copy-start | bytes 1540
  410.3 3.9 copy-start.12
  442.1 16.3 %copy-start.34 = (pred[2,512]{1,0:T(4,128)(4,1)S(1)}, pred[2,512]{1,0:T(4,128)(4,1)}, u32[]{:S(2)}) copy-start(pred[2,512]{1,0:T(4,128)(4,1)} %compare_and_fusion.2) | copy-start | bytes 3076
  442.1 17.0 %copy-start.9 = (f32[2,25,512]{2,0,1:T(2,128)S(1)}, f32[2,25,512]{2,0,1:T(2,128)}, u32[]{:S(2)}) copy-start(f32[2,25,512]{2,0,1:T(2,128)} %param.44) | copy-start | bytes 307204
  442.1 17.0 %copy-start.36 = (f32[1,512]{1,0:T(1,128)S(1)}, f32[1,512]{1,0:T(1,128)}, u32[]{:S(2)}) copy-start(f32[1,512]{1,0:T(1,128)} %get-tuple-element.85) | copy-start | bytes 6148
  442.1 17.0 %copy-start.37 = (f32[1,512]{1,0:T(1,128)S(1)}, f32[1,512]{1,0:T(1,128)}, u32[]{:S(2)}) copy-start(f32[1,512]{1,0:T(1,128)} %get-tuple-element.86) | copy-start | bytes 6148
  454.9 4.7 copy-start.11
  454.9 4.7 copy-start.16
  454.9 4.7 copy-start.17
  454.9 4.7 copy-start.18
  454.9 4.7 copy-start.19
  454.9 4.8 copy-start.35
  496.2 7.7 %copy-start.21 = (pred[128,24]{1,0:T(8,128)(4,1)S(1)}, pred[128,24]{1,0:T(8,128)(4,1)}, u32[]{:S(2)}) copy-start(pred[128,24]{1,0:T(8,128)(4,1)} %broadcast_in_dim.91) | copy-start | bytes 9220
  523.4 52.0 %all-to-all-start.2 = ((f32[150,128,24]{0,2,1:T(8,128)}), f32[150,128,24]{0,2,1:T(8,128)S(1)}, u32[]{:S(2)}, u32[]{:S(2)}) async-start(f32[150,128,24]{0,2,1:T(8,128)} %copy.508), calls=%async_computation.2 | async-start | bytes 6291456 | tf_op jit(solution)/shard_map/all_to_all | solution.py:179
  533.1 10.3 %copy-start.2 = (f32[1,9,9,512]{1,2,3,0:T(8,128)S(1)}, f32[1,9,9,512]{1,2,3,0:T(8,128)}, u32[]{:S(2)}) copy-start(f32[1,9,9,512]{1,2,3,0:T(8,128)} %copy.595) | copy-start | bytes 497668
  533.1 10.3 %copy-start.4 = (f32[512,9,20]{2,1,0:T(8,128)S(1)}, f32[512,9,20]{2,1,0:T(8,128)}, u32[]{:S(2)}) copy-start(f32[512,9,20]{2,1,0:T(8,128)} %copy.538) | copy-start | bytes 1105924
  543.5 5.8 copy-start.3
  543.5 5.8 copy-start.5
  583.0 9.6 %copy-start.33 = (f32[10,25]{1,0:T(8,128)S(1)}, f32[10,25]{1,0:T(8,128)}, u32[]{:S(2)}) copy-start(f32[10,25]{1,0:T(8,128)} %param.39) | copy-start | bytes 3004
  583.0 11.3 %copy-start.24 = (f32[3072,4]{0,1:T(4,128)S(1)}, f32[3072,4]{0,1:T(4,128)}, u32[]{:S(2)}) copy-start(f32[3072,4]{0,1:T(4,128)} %select_bitcast_fusion.7) | copy-start | bytes 147460
  592.6 8.1 %copy-start.28 = (s32[3072]{0:T(1024)S(1)}, s32[3072]{0:T(1024)}, u32[]{:S(2)}) copy-start(s32[3072]{0:T(1024)} %get-tuple-element.47) | copy-start | bytes 36868
  606.9 33.2 %copy-start.1 = (f32[3,20,20]{2,1,0:T(8,128)S(1)}, f32[3,20,20]{2,1,0:T(8,128)}, u32[]{:S(2)}) copy-start(f32[3,20,20]{2,1,0:T(8,128)} %param.29) | copy-start | bytes 14404
  (3 other events, 9.2 us)
where the time goes:
time: 644 us; the launch traced here: 640 us
  local copies, waits for them, and re-layouts  325 us (50%)
  matrix products  199 us (31%)
  other arithmetic  52.7 us (8%)
  starting transfers between devices  41.6 us (6%)
  waiting for transfers between devices  19.6 us (3%)
    dot_general x3, matrix products, predictor(): current = -jnp.einsum('dqpe,dqbe->pbe', star, moved, precision=highest)  61.5 us
    unnamed x113, local copies, waits for them, and re-layouts  45.6 us
    gather x3, local copies, waits for them, and re-layouts, per_device(): reply = jnp.take(outgoing, source, axis=2) * filled[None, None, :]  40.8 us
    dot_general x4, matrix products, per_device(): jnp.einsum('qpe,qbe->pbe', solver_plus[face], chosen, precision=highest)  32 us
    dot_general x1, matrix products, per_device(): jnp.einsum('fqpe,fqbe->pbe', solver_minus, projected, precision=highest)  29.7 us
    gather x3, local copies, waits for them, and re-layouts, per_device(): columns = jnp.take(jnp.take(integral, rows, axis=0), element, axis=2)  27.4 us
    transpose x3, local copies, waits for them, and re-layouts, predictor(): moved = jnp.einsum('dbc,qce->dqbe', stiff, current, precision=highest)  27 us
    gather x4, local copies, waits for them, and re-layouts, per_device(): gathered = jnp.take(extended, neighbor[face], axis=2)  23 us
  transfers between devices with their start and end apart: 5, of which 1 were waited for; matrix products, arithmetic and copies ran while one was open for 65% of the time, Pallas kernels for 0%

commit v1 on v0

v1 whole, which is shorter than its diff:
```python
import jax
import jax.numpy as jnp
from jax import lax
from jax.experimental import pallas as pl
from jax.experimental.pallas import tpu as pltpu
from jax.sharding import PartitionSpec as P

time_step = 0.8
trace_rows = (0, 3, 5, 6, 7, 8)
both = ("dom", "sub")
f32 = jnp.float32
bf16 = jnp.bfloat16
vmem = pl.BlockSpec(memory_space=pltpu.VMEM)


def from_behind(block, axis, distance):
    devices = range(lax.axis_size(axis))
    route = [(i - distance, i) for i in devices if i - distance in devices]
    return lax.ppermute(block, axis, route)


def iota(shape, axis):
    return lax.broadcasted_iota(jnp.int32, shape, axis)


def product(a, b, left=1, right=0):
    return lax.dot_general(a, b, (((left,), (right,)), ((), ())), preferred_element_type=f32)


def product_full(a, b, left=1, right=0):
    return lax.dot_general(
        a,
        b,
        (((left,), (right,)), ((), ())),
        precision=lax.Precision.HIGHEST,
        preferred_element_type=f32,
    )


def halves(x):
    high = x.astype(bf16)
    low = (x - high.astype(f32)).astype(bf16)
    return high, low


def flags(condition):
    return jnp.where(condition, 1.0, 0.0).astype(f32)


def pack_left(a):
    repeat = flags((iota((128, 128), 1) & 31) == iota((128, 128), 0))
    wide = product_full(a, repeat)
    high = wide.astype(bf16).astype(f32)
    return jnp.where(iota(wide.shape, 1) < 64, high, wide - high).astype(bf16)


def pack_right(x):
    high, low = halves(x)
    return jnp.concatenate([high, low, high, low], axis=0)


def thirds(t):
    return jnp.where(t >= 10, 1, 0) + jnp.where(t >= 20, 1, 0)


def owner_flags(owner_ref):
    owner = jnp.concatenate([owner_ref[0:1, :], owner_ref[1:2, :]], axis=1)
    return flags(iota((128, owner.shape[1]), 0) == owner)


def request_kernel(owner_ref, face_ref, impedance_ref, request_ref, position_ref):
    owned = owner_flags(owner_ref)
    owned_half = owned.astype(bf16)
    sides = owned.shape[1]
    block = 256
    ahead = flags(iota((block, block), 0) < iota((block, block), 1)).astype(bf16)
    carry = jnp.zeros((128, 1), f32)
    positions = []
    for start in range(0, sides, block):
        part = owned[:, start : start + block]
        before = product(owned_half[:, start : start + block], ahead) + carry
        positions.append(jnp.sum(part * before, axis=0, keepdims=True))
        carry = carry + jnp.sum(part, axis=1, keepdims=True)
    position = jnp.concatenate(positions, axis=1)
    position_ref[...] = jnp.broadcast_to(position, position_ref.shape)
    wanted = jnp.concatenate([face_ref[0:1, :], face_ref[1:2, :]], axis=1).astype(f32) + 1.0
    zp = jnp.concatenate([impedance_ref[0:1, :], -impedance_ref[1:2, :]], axis=1)
    zs = jnp.concatenate([impedance_ref[2:3, :], -impedance_ref[3:4, :]], axis=1)
    row = iota((128, sides), 0)
    channel = jnp.where(row >= 24, 1, 0) + jnp.where(row >= 48, 1, 0)
    slot = (row - 24 * channel).astype(f32)
    value = jnp.where(row < 24, wanted, jnp.where(row < 48, zp, zs))
    value = jnp.where((slot == position) & (row < 72), value, 0.0)
    high = value.astype(bf16)
    rest = value - high.astype(f32)
    middle, low = halves(rest)
    request_ref[...] = (
        product(owned_half, high, 1, 1)
        + product(owned_half, middle, 1, 1)
        + product(owned_half, low, 1, 1)
    )


def lift_expand(lift_ref, lift_pad):
    lift_pad[...] = jnp.zeros_like(lift_pad)
    for face in range(4):
        lift_pad[face * 16 : face * 16 + 10, 0:20] = lift_ref[:, face, :]
    row = iota((256, 64), 0)
    inner = row & 31
    third = thirds(inner)
    source = (row >> 6) * 16 + inner - 10 * third
    pick = flags((source == iota((256, 64), 1)) & (inner < 30))
    rows = product_full(pick, lift_pad[...])
    spread = flags((iota((128, 192), 1) & 31) == iota((128, 192), 0))
    wide = product_full(rows, spread)
    row = iota((256, 192), 0)
    want = ((row >> 5) & 1) * 3 + thirds(row & 31)
    return jnp.where((iota((256, 192), 1) >> 5) == want, wide, 0.0)


def predictor_kernel(
    dofs_ref,
    star_ref,
    stiff_ref,
    lift_ref,
    copy_ref,
    integral_ref,
    modal_ref,
    table_ref,
    lift_out_ref,
    low_ref,
    up_ref,
    current,
    moved,
    left,
    lift_pad,
):
    count = dofs_ref.shape[2]
    left[...] = jnp.zeros_like(left)
    for d in range(3):
        left[d * 32 : d * 32 + 20, 0:20] = stiff_ref[d]
    packed = pack_left(left[...])
    current[...] = jnp.zeros_like(current)
    for q in range(9):
        current[q, 0:20, :] = dofs_ref[q]
        integral_ref[q, :, :] = time_step * current[q, 0:24, :]
    factor = time_step
    for order in range(1, 4):
        factor = factor * time_step / (order + 1)
        for q in range(9):
            moved[q] = product(packed, pack_right(current[q]))

        def tile(i, carry):
            lanes = pl.ds(pl.multiple_of(i * 128, 128), 128)
            total = [jnp.zeros((24, 128), f32) for _ in range(9)]
            for q in range(9):
                for d in range(3):
                    part = moved[q, d * 32 : d * 32 + 24, lanes]
                    for p in range(9):
                        total[p] = total[p] - star_ref[q, p, d : d + 1, lanes] * part
            for p in range(9):
                current[p, 0:24, lanes] = total[p]
                integral_ref[p, :, lanes] += factor * total[p]
            return carry

        lax.fori_loop(0, count // 128, tile, 0)
    whole = integral_ref[...].reshape(216, count)
    high, low = halves(whole)
    for index, out in ((0, low_ref), (1, up_ref)):
        pick = flags(iota((count, 128), 0) == copy_ref[index : index + 1, :]).astype(bf16)
        out[...] = product(high, pick) + product(low, pick)
    spread = lift_expand(lift_ref, lift_pad)
    lift_out_ref[...] = spread
    for p in range(9):
        current[p, 0:24, :] = integral_ref[p]
    rows = jnp.concatenate([current[r] for r in trace_rows], axis=0)
    rows_high, rows_low = halves(rows)
    spread_high, spread_low = halves(spread)
    modal = (
        product(spread_high, rows_high)
        + product(spread_high, rows_low)
        + product(spread_low, rows_high)
    )
    modal_ref[...] = modal
    table_ref[...] = modal.T


def slots_of(request):
    wanted = (request + 0.5).astype(jnp.int32) - 1
    element = jnp.where(wanted < 0, -1, wanted & 511)
    return element, wanted >> 9


def slot_flags(element, first, many, count):
    lane = iota((128, count), 1)
    return jnp.concatenate(
        [
            flags(element[:, k : k + 1] == lane).astype(bf16)
            for k in range(first, first + many)
        ],
        axis=0,
    )


def gather_kernel(request_ref, table_ref, out_ref):
    request = request_ref[...]
    element, face = slots_of(request)
    table = jnp.concatenate(halves(table_ref[...]), axis=1)
    lane = iota((128, 128), 1)
    for r in range(6):
        pick = slot_flags(element, 4 * r, 4, table_ref.shape[0])
        both_halves = product(pick, table)
        found = both_halves[:, 0:256] + both_halves[:, 256:512]
        block = jnp.zeros((128, 128), f32)
        for j in range(4):
            k = 4 * r + j
            mine = found[j * 128 : j * 128 + 128]
            side = face[:, k : k + 1]
            mine = jnp.where(side >= 2, mine[:, 128:256], mine[:, 0:128])
            mine = jnp.where((side & 1) == 1, pltpu.roll(mine, 64, 1), mine)
            velocity = pltpu.roll(mine, 96, 1)
            z = jnp.where(lane < 10, request[:, 24 + k : 25 + k], request[:, 48 + k : 49 + k])
            wave = jnp.where(lane < 32, mine - z * velocity, 0.0)
            if j:
                wave = pltpu.roll(wave, 32 * j, 1)
            block = block + wave
        out_ref[pl.ds(r, 128, stride=8), :] = block
    for r in range(6, 8):
        out_ref[pl.ds(r, 128, stride=8), :] = jnp.zeros((128, 128), f32)


def inner_kernel(integral_ref, star_ref, minus_ref, stiff_ref, local_ref, out_ref, left, square, moved):
    count = integral_ref.shape[2]
    left[...] = jnp.zeros_like(left)
    square[...] = jnp.zeros_like(square)
    for d in range(3):
        square[0:20, 0:20] = stiff_ref[d]
        left[d * 32 : d * 32 + 32, :] = square[...].T[0:32, :]
    for f in range(4):
        left[96 + f * 32 : 96 + f * 32 + 20, 0:20] = local_ref[:, f, :]
    packed = pack_left(left[...])
    empty = jnp.zeros((8, count), f32)
    for q in range(9):
        moved[q] = product(
            packed, pack_right(jnp.concatenate([integral_ref[q], empty], axis=0))
        )

    def tile(i, carry):
        lanes = pl.ds(pl.multiple_of(i * 128, 128), 128)
        total = [jnp.zeros((24, 128), f32) for _ in range(9)]
        for q in range(9):
            for d in range(3):
                part = moved[q, d * 32 : d * 32 + 24, lanes]
                for p in range(9):
                    total[p] = total[p] + star_ref[q, p, d : d + 1, lanes] * part
            for f in range(4):
                part = moved[q, 96 + f * 32 : 96 + f * 32 + 24, lanes]
                for p in range(9):
                    total[p] = total[p] - minus_ref[q, p, f : f + 1, lanes] * part
        for p in range(9):
            out_ref[p, :, lanes] = total[p]
        return carry

    lax.fori_loop(0, count // 128, tile, 0)


def neighbour_kernel(
    inner_ref,
    integral_ref,
    lower_ref,
    upper_ref,
    neighbor_ref,
    orientation_ref,
    plus_ref,
    flux_ref,
    out_ref,
    left,
    moved,
):
    count = integral_ref.shape[2]
    extended = jnp.concatenate(
        [integral_ref[...].reshape(216, count), lower_ref[...], upper_ref[...]], axis=1
    )
    extended = jnp.concatenate(halves(extended), axis=0)
    width = extended.shape[1]
    out_ref[...] = inner_ref[...]
    left[...] = jnp.zeros_like(left)
    empty = jnp.zeros((8, count), f32)
    for f in range(4):
        pick = flags(iota((width, count), 0) == neighbor_ref[f : f + 1, :]).astype(bf16)
        found = product(extended, pick)
        found = found[0:216] + found[216:432]
        for a in range(12):
            left[a * 24 : a * 24 + 20, 0:20] = flux_ref[a, :, f, :]
        packed = pack_left(left[...])
        turn = orientation_ref[f : f + 1, :]
        for q in range(9):
            mine = jnp.concatenate([found[q * 24 : q * 24 + 24], empty], axis=0)
            every = product(packed, pack_right(mine))
            chosen = every[0:24]
            for a in range(1, 12):
                chosen = jnp.where(turn == a, every[a * 24 : a * 24 + 24], chosen)
            moved[q] = chosen

        def tile(i, carry):
            lanes = pl.ds(pl.multiple_of(i * 128, 128), 128)
            total = [out_ref[p, :, lanes] for p in range(9)]
            for q in range(9):
                part = moved[q, :, lanes]
                for p in range(9):
                    total[p] = total[p] - plus_ref[q, p, f : f + 1, lanes] * part
            for p in range(9):
                out_ref[p, :, lanes] = total[p]
            return carry

        lax.fori_loop(0, count // 128, tile, 0)


def face_expand(face_ref, pad):
    pad[...] = jnp.zeros_like(pad)
    pad[0:10, 0:25] = face_ref[...]
    row = iota((32, 16), 0)
    pick = flags((row - 10 * thirds(row) == iota((32, 16), 1)) & (row < 30))
    spread = flags((iota((128, 96), 1) & 31) == iota((128, 96), 0))
    wide = product_full(product_full(pick, pad[...]), spread)
    return jnp.where((iota((32, 96), 1) >> 5) == thirds(iota((32, 96), 0)), wide, 0.0)


def friction_kernel(
    arrived_ref,
    position_ref,
    owner_ref,
    impedance_ref,
    eval_ref,
    weight_ref,
    normal_ref,
    shear_ref,
    slip_ref,
    static_ref,
    drop_ref,
    scale_ref,
    reply_ref,
    slip_out_ref,
    traction_ref,
    pad,
    states,
):
    owned = owner_flags(owner_ref).astype(bf16)
    position = position_ref[0:1, :]
    faults = slip_ref.shape[1]
    wave = jnp.zeros((32, 2 * faults), f32)
    for r in range(6):
        high, low = halves(arrived_ref[pl.ds(r, 128, stride=8), :].T)
        found = product(jnp.concatenate([high, low], axis=0), owned)
        found = found[0:128] + found[128:256]
        for j in range(4):
            wave = jnp.where(position == float(4 * r + j), found[j * 32 : j * 32 + 32], wave)
    pwave_minus = impedance_ref[0:1, :]
    pwave_plus = impedance_ref[1:2, :]
    swave_minus = impedance_ref[2:3, :]
    swave_plus = impedance_ref[3:4, :]
    pwave_sum = pwave_minus + pwave_plus
    swave_sum = swave_minus + swave_plus
    viscous = swave_minus * swave_plus / swave_sum
    normal_row = iota((32, faults), 0) < 10
    modal = (
        jnp.where(normal_row, pwave_plus / pwave_sum, swave_plus / swave_sum) * wave[:, 0:faults]
        + jnp.where(normal_row, pwave_minus / pwave_sum, swave_minus / swave_sum)
        * wave[:, faults : 2 * faults]
    ) * (1.0 / time_step)
    evaluate = face_expand(eval_ref, pad)
    states[...] = product_full(evaluate, modal, 0, 0)
    normal = states[0:25, :]
    initial = (shear_ref[:, 0, :], shear_ref[:, 1, :])
    shear = (states[32:57, :] + initial[0], states[64:89, :] + initial[1])
    weakened = jnp.minimum(slip_ref[...] / scale_ref[...], 1.0)
    coefficient = static_ref[...] - drop_ref[...] * weakened
    strength = coefficient * jnp.maximum(-(normal + normal_ref[...]), 0.0)
    magnitude = jnp.sqrt(shear[0] * shear[0] + shear[1] * shear[1])
    ratio = jnp.minimum(1.0, strength / jnp.maximum(magnitude, 1.0))
    final = (shear[0] * ratio, shear[1] * ratio)
    rate_0 = (shear[0] - final[0]) / viscous
    rate_1 = (shear[1] - final[1]) / viscous
    slip_out_ref[...] = slip_ref[...] + time_step * jnp.sqrt(rate_0 * rate_0 + rate_1 * rate_1)
    traction_ref[:, 0, :] = final[0]
    traction_ref[:, 1, :] = final[1]
    states[32:57, :] = final[0] - initial[0]
    states[64:89, :] = final[1] - initial[1]
    weight = face_expand(weight_ref, pad)
    imposed = product_full(weight, states[...])
    high = imposed.astype(bf16).astype(f32)
    low = imposed - high
    high = jnp.concatenate([high, high], axis=1)
    low = jnp.concatenate([low, low], axis=1)
    for r in range(6):
        here = [position == float(4 * r + j) for j in range(4)]
        rows = jnp.concatenate(
            [jnp.where(here[j], high, 0.0).astype(bf16) for j in range(4)]
            + [jnp.where(here[j], low, 0.0).astype(bf16) for j in range(4)],
            axis=0,
        )
        block = product(rows, owned, 1, 1)
        reply_ref[pl.ds(r, 128, stride=8), :] = (block[0:128] + block[128:256]).T
    for r in range(6, 8):
        reply_ref[pl.ds(r, 128, stride=8), :] = jnp.zeros((128, 128), f32)


def final_kernel(
    request_ref,
    returned_ref,
    modal_ref,
    lift_ref,
    dofs_ref,
    partial_ref,
    eval_ref,
    weight_ref,
    out_ref,
    pad,
    totals,
):
    count = dofs_ref.shape[2]
    request = request_ref[...]
    element, _ = slots_of(request)
    turned = request.T
    _, face = slots_of(turned)
    inverse = jnp.where(turned == 0.0, 0.0, 1.0 / jnp.where(turned == 0.0, 1.0, turned))
    row = iota((32, 128), 0)
    normal_row = (row < 10) | (row == 30)
    for r in range(6):
        block = returned_ref[pl.ds(r, 128, stride=8), :].T
        highs = []
        lows = []
        for j in range(4):
            k = 4 * r + j
            plain = jnp.where(row >= 30, 1.0, block[j * 32 : j * 32 + 32])
            scale = jnp.where(normal_row, inverse[24 + k : 25 + k, :], inverse[48 + k : 49 + k, :])
            mine = jnp.concatenate([plain, plain * scale], axis=0)
            side = face[k : k + 1, :]
            mine = jnp.concatenate([jnp.where(side == f, mine, 0.0) for f in range(4)], axis=0)
            high, low = halves(mine)
            highs.append(high)
            lows.append(low)
        values = jnp.concatenate(
            [jnp.concatenate(highs, axis=1), jnp.concatenate(lows, axis=1)], axis=0
        )
        pick = slot_flags(element, 4 * r, 4, count)
        part = product(values, pick)
        part = part[0:256] + part[256:512]
        if r:
            totals[...] += part
        else:
            totals[...] = part
    evaluate = face_expand(eval_ref, pad)
    weight = face_expand(weight_ref, pad)
    gauss = product_full(weight, evaluate, 1, 1) * (1.0 / time_step)
    row = iota((32, count), 0) < 10
    states = []
    for f in range(4):
        base = f * 64
        own = product_full(gauss, modal_ref[base : base + 32, :])
        sides = totals[base + 30 : base + 31, :]
        scaled = jnp.where(row, totals[base + 62 : base + 63, :], totals[base + 63 : base + 64, :])
        states.append(totals[base : base + 32, :] - sides * own)
        states.append(totals[base + 32 : base + 64, :] - scaled * own)
    fault = product_full(lift_ref[...], jnp.concatenate(states, axis=0), 0, 0)
    for p in range(9):
        value = dofs_ref[p] + partial_ref[p, 0:20, :]
        if p in trace_rows:
            k = trace_rows.index(p)
            value = value + fault[k * 32 : k * 32 + 20, :]
        out_ref[p] = value


def call(kernel, name, outs, scratch, operands, flops):
    return pl.pallas_call(
        kernel,
        name=name,
        out_shape=[jax.ShapeDtypeStruct(shape, f32) for shape in outs],
        in_specs=[vmem] * len(operands),
        out_specs=[vmem] * len(outs),
        scratch_shapes=[pltpu.VMEM(shape, f32) for shape in scratch],
        compiler_params=pltpu.CompilerParams(vmem_limit_bytes=48 * 1024 * 1024),
        cost_estimate=pl.CostEstimate(flops=flops, bytes_accessed=4_000_000, transcendentals=0),
    )(*operands)


def exchange(block):
    return lax.all_to_all(block, both, split_axis=0, concat_axis=0, tiled=True)


def per_device(
    dofs,
    star,
    stiff,
    flux_local,
    flux_neighbor,
    solver_minus,
    solver_plus,
    neighbor,
    orientation,
    copy_list,
    face_lift,
    face_eval,
    face_weight,
    side_owner,
    side_face,
    impedance,
    normal_initial,
    shear_initial,
    slip,
    static_friction,
    friction_drop,
    slip_scale,
):
    count = dofs.shape[2]
    faults = side_owner.shape[0]
    owner = jnp.transpose(side_owner)
    wanted = jnp.transpose(side_face)
    star = jnp.transpose(star, (1, 2, 0, 3))
    minus = jnp.transpose(solver_minus, (1, 2, 0, 3))
    plus = jnp.transpose(solver_plus, (1, 2, 0, 3))
    local = jnp.transpose(flux_local, (1, 0, 2))
    flux = jnp.transpose(flux_neighbor, (1, 2, 0, 3))
    lift = jnp.transpose(face_lift, (1, 0, 2))
    evaluate = jnp.transpose(face_eval)
    shear = jnp.transpose(shear_initial, (1, 0, 2))
    request, position = call(
        request_kernel,
        "request",
        [(128, 128), (8, 2 * faults)],
        [],
        [owner, wanted, impedance],
        10**8,
    )
    asked = exchange(request.reshape(128, 1, 128)).reshape(128, 128)
    integral, modal, table, spread, low, up = call(
        predictor_kernel,
        "predictor",
        [(9, 24, count), (256, count), (count, 256), (256, 192), (216, 128), (216, 128)],
        [(9, 32, count), (9, 96, count), (96, 128), (64, 128)],
        [dofs, star, stiff, lift, copy_list],
        10**10,
    )
    (payload,) = call(
        gather_kernel, "gather", [(1024, 128)], [], [asked, table], 10**9
    )
    arrived = exchange(payload.reshape(128, 8, 128)).reshape(1024, 128)
    from_lower = from_behind(up, both, 1)
    from_upper = from_behind(low, both, -1)
    (inner,) = call(
        inner_kernel,
        "inner",
        [(9, 24, count)],
        [(224, 128), (128, 128), (9, 224, count)],
        [integral, star, minus, stiff, local],
        10**10,
    )
    reply, new_slip, traction = call(
        friction_kernel,
        "friction",
        [(1024, 128), (25, faults), (25, 2, faults)],
        [(16, 128), (96, faults)],
        [
            arrived,
            position,
            owner,
            impedance,
            evaluate,
            face_weight,
            normal_initial,
            shear,
            slip,
            static_friction,
            friction_drop,
            slip_scale,
        ],
        10**9,
    )
    returned = exchange(reply.reshape(128, 8, 128)).reshape(1024, 128)
    (partial,) = call(
        neighbour_kernel,
        "neighbour",
        [(9, 24, count)],
        [(288, 128), (9, 24, count)],
        [inner, integral, from_lower, from_upper, neighbor, orientation, plus, flux],
        10**10,
    )
    (new_dofs,) = call(
        final_kernel,
        "final",
        [(9, 20, count)],
        [(16, 128), (256, count)],
        [asked, returned, modal, spread, dofs, partial, evaluate, face_weight],
        10**9,
    )
    return (new_dofs, new_slip, jnp.transpose(traction, (1, 0, 2)))


def solution(mesh):
    in_specs = (
        P(None, None, ("dom", "sub")),
        P(None, None, None, ("dom", "sub")),
        P(),
        P(),
        P(),
        P(None, None, None, ("dom", "sub")),
        P(None, None, None, ("dom", "sub")),
        P(None, ("dom", "sub")),
        P(None, ("dom", "sub")),
        P(None, ("dom", "sub")),
        P(),
        P(),
        P(),
        P(("dom", "sub"), None),
        P(("dom", "sub"), None),
        P(None, ("dom", "sub")),
        P(None, ("dom", "sub")),
        P(None, None, ("dom", "sub")),
        P(None, ("dom", "sub")),
        P(None, ("dom", "sub")),
        P(None, ("dom", "sub")),
        P(None, ("dom", "sub")),
    )
    out_specs = (
        P(None, None, ("dom", "sub")),
        P(None, ("dom", "sub")),
        P(None, None, ("dom", "sub")),
    )
    return jax.shard_map(
        per_device, mesh=mesh, in_specs=in_specs, out_specs=out_specs, check_vma=False
    )
```

time: 644 us -> 95.2 us (0.15)
  local copies, waits for them, and re-layouts: 325 us -> 13.7 us
  matrix products: 199 us -> 0 us
  other arithmetic: 52.7 us -> 0 us
  Pallas kernels: 0 us -> 37.8 us
  starting transfers between devices: 41.6 us -> 30.9 us
  waiting for transfers between devices: 19.6 us -> 11 us
    dot_general x23 -> x0, matrix products: 199 us -> none  [the longest x3 61.5 us: predictor(): current = -jnp.einsum('dqpe,dqbe->pbe', star, moved, precision=highest)]
    gather x14 -> x0, local copies, waits for them, and re-layouts: 113 us -> none  [the longest x3 40.8 us: per_device(): reply = jnp.take(outgoing, source, axis=2) * filled[None, None, :]]
    transpose x5 -> x0, local copies, waits for them, and re-layouts: 50.6 us -> none  [the longest x3 27 us: predictor(): moved = jnp.einsum('dbc,qce->dqbe', stiff, current, precision=highest)]
    pallas_call x0 -> x7, Pallas kernels: none -> 37.8 us  [call(): pl.pallas_call(kernel, name=name, out_shape=[jax.ShapeDtypeStruct(shape,...]
    reshape x6 -> x0, local copies, waits for them, and re-layouts: 36.3 us -> none  [the longest x2 18.1 us: per_device(): payload.reshape(6 * inner, devices, capacity)]
    unnamed x113 -> x72, local copies, waits for them, and re-layouts: 45.6 us -> 13.7 us
    select_n x15 -> x0, other arithmetic: 29.2 us -> none  [the longest x8 16.3 us: per_device(): gathered = jnp.take(extended, neighbor[face], axis=2)]
    dot_general x7 -> x0, local copies, waits for them, and re-layouts: 23.4 us -> none  [the longest x4 14.9 us: per_device(): chosen = jnp.einsum('aqbe,ae->qbe', every_combo, picked, precision=highest)]
  transfers between devices with their start and end apart: 5 -> 5, of which waited for: 1 -> 2; matrix products, arithmetic and copies ran while one was open for 65% -> 0% of each run, Pallas kernels for 0% -> 34%
where the time goes in v1:
time: 95.2 us; the launch traced here: 94.4 us
  Pallas kernels  37.8 us (40%)
  starting transfers between devices  30.9 us (32%)
  local copies, waits for them, and re-layouts  13.7 us (14%)
  waiting for transfers between devices  11 us (12%)
  between operations  0.99 us (1%)
    pallas_call x7, Pallas kernels, call(): pl.pallas_call(kernel, name=name, out_shape=[jax.ShapeDtypeStruct(shape,...  37.8 us
    all_to_all x3, starting transfers between devices, exchange(): return lax.all_to_all(block, both, split_axis=0, concat_axis=0, tiled=True)  24.1 us
    unnamed x72, local copies, waits for them, and re-layouts  13.7 us
    all_to_all x3, waiting for transfers between devices, exchange(): return lax.all_to_all(block, both, split_axis=0, concat_axis=0, tiled=True)  11 us
    ppermute x2, starting transfers between devices, from_behind(): return lax.ppermute(block, axis, route)  6.76 us
  transfers between devices with their start and end apart: 5, of which 2 were waited for; matrix products, arithmetic and copies ran while one was open for 0% of the time, Pallas kernels for 34%

profile of v1, /device:TPU:1, one launch (start us, length us, event | category | flops | bytes accessed | tf_op | source)
XLA Modules:
  0.0 94.4 jit_solution(6036585595503540906)
XLA Ops:
  0.6 0.0 copy-start.15
  0.7 0.7 copy-done.15
  1.4 0.7 copy-done.21
  2.1 0.7 copy-done.22
  2.8 1.3 %request.1 = (f32[128,128]{1,0:T(8,128)}, f32[8,1024]{1,0:T(8,128)S(1)}) custom-call(s32[2,512]{1,0:T(2,128)S(1)} %bitcast.34, s32[2,512]{1,0:T(2,128)S(1)} %bitcast.33, f32[4,512]{1,0:T(4,128)S(1)} %copy-done.15), custom_call_target="tpu_custom_call" | custom-call | flops 100000000 | bytes 4000000 | tf_op jit(solution)/shard_map/request/pallas_call | solution.py:475
  4.0 11.5 %all-to-all-start = ((f32[128,1,128]{2,1,0:T(1,128)}), f32[128,1,128]{2,1,0:T(1,128)S(1)}, u32[]{:S(2)}, u32[]{:S(2)}) async-start(f32[128,1,128]{2,1,0:T(1,128)} %bitcast.3), calls=%async_computation | async-start | bytes 131072 | tf_op jit(solution)/shard_map/all_to_all | solution.py:488
  15.5 0.0 copy-start.24
  15.6 0.0 copy-done.5
  15.6 0.0 copy-done.13
  15.6 0.0 copy-done.14
  15.6 0.6 copy-done.24
  16.2 1.1 %copy-done = f32[3,9,9,512]{3,0,2,1:T(4,128)S(1)} copy-done((f32[3,9,9,512]{3,0,2,1:T(4,128)S(1)}, f32[3,9,9,512]{3,0,2,1:T(4,128)}, u32[]{:S(2)}) %copy-start) | copy-done | bytes 497688
  17.3 6.7 %predictor.1 = (f32[9,24,512]{2,1,0:T(8,128)S(1)}, f32[256,512]{1,0:T(8,128)S(1)}, f32[512,256]{1,0:T(8,128)S(1)}, f32[256,192]{1,0:T(8,128)S(1)}, f32[216,128]{1,0:T(8,128)S(1)}, /*index=5*/f32[216,128]{1,0:T(8,128)S(1)}) custom-call(f32[9,20,512]{2,1,0:T(8,128)S(1)} %copy-done.5, f32[9,9,3,512]{3,2,1,0:T(4,128)S(1)} %bitcast.23, ...), custom_call_target="tpu_custom_call" | custom-call | flops 10000000000 | bytes 4000000 | tf_op jit(solution)/shard_map/predictor/pallas_call | solution.py:475
  24.0 0.8 copy-done.25
  24.8 0.7 copy-done.29
  25.5 0.8 copy-done.31
  26.3 3.3 %collective-permute-start = (f32[216,128]{1,0:T(8,128)S(1)}, f32[216,128]{1,0:T(8,128)S(1)}, u32[]{:S(2)}, u32[]{:S(2)}) collective-permute-start(f32[216,128]{1,0:T(8,128)S(1)} %get-tuple-element.21), channel_id=1, source_target_pairs={{0,1},{1,2},{2,3},{3,4},{4,5},{5,6},{6,7},{7,8},{8,9},{9,10},{10,1... | collective-permute-start | bytes 331784 | tf_op jit(solution)/shard_map/ppermute | solution.py:19
  29.6 3.5 %collective-permute-start.1 = (f32[216,128]{1,0:T(8,128)S(1)}, f32[216,128]{1,0:T(8,128)S(1)}, u32[]{:S(2)}, u32[]{:S(2)}) collective-permute-start(f32[216,128]{1,0:T(8,128)S(1)} %get-tuple-element.22), channel_id=1, source_target_pairs={{1,0},{2,1},{3,2},{4,3},{5,4},{6,5},{7,6},{8,7},{9,8},{10,9},{11,1... | collective-permute-start | bytes 331784 | tf_op jit(solution)/shard_map/ppermute | solution.py:19
  33.1 0.0 all-to-all-done
  33.1 0.0 copy-start.2
  33.1 9.3 %gather.1 = f32[1024,128]{1,0:T(8,128)} custom-call(f32[128,128]{1,0:T(8,128)S(1)} %bitcast.21, f32[512,256]{1,0:T(8,128)S(1)} %get-tuple-element.15.table_ref), custom_call_target="tpu_custom_call" | custom-call | flops 1000000000 | bytes 4000000 | tf_op jit(solution)/shard_map/gather/pallas_call | solution.py:475
  42.4 8.8 %all-to-all-start.1 = ((f32[128,8,128]{2,1,0:T(8,128)}), f32[128,8,128]{2,1,0:T(8,128)S(1)}, u32[]{:S(2)}, u32[]{:S(2)}) async-start(f32[128,8,128]{2,1,0:T(8,128)} %bitcast.7), calls=%async_computation.1 | async-start | bytes 1048576 | tf_op jit(solution)/shard_map/all_to_all | solution.py:488
  51.2 0.0 copy-start.32
  51.2 1.0 %copy-done.32 = f32[9,24,512]{2,1,0:T(8,128)S(1)} copy-done((f32[9,24,512]{2,1,0:T(8,128)S(1)}, f32[9,24,512]{2,1,0:T(8,128)}, u32[]{:S(2)}) %copy-start.32) | copy-done | bytes 442392
  52.2 0.0 copy-start.10
  52.3 0.0 copy-start.11
  52.3 0.0 copy-start.16
  52.3 0.0 copy-start.19
  52.3 0.0 copy-start.20
  52.3 4.7 %inner.1.inner_ref = f32[9,24,512]{2,1,0:T(8,128)S(1)} custom-call(f32[9,24,512]{2,1,0:T(8,128)S(1)} %copy-done.32, f32[9,9,3,512]{3,2,1,0:T(4,128)S(1)} %bitcast.24, f32[9,9,4,512]{3,2,1,0:T(4,128)S(1)} %bitcast.25, f32[3,20,20]{2,1,0:T(8,128)S(1)} %copy-done.13, f32[20,4,20]{2,1,0:T(4,128)S(1)} %bitcast.29), custom_call_target="tpu_custom_call" | custom-call | flops 10000000000 | bytes 4000000 | tf_op jit(solution)/shard_map/inner/pallas_call | solution.py:475
  57.0 0.8 copy-done.34
  57.8 7.5 %all-to-all-done.1 = f32[128,8,128]{2,1,0:T(8,128)S(1)} async-done(((f32[128,8,128]{2,1,0:T(8,128)}), f32[128,8,128]{2,1,0:T(8,128)S(1)}, u32[]{:S(2)}, u32[]{:S(2)}) %all-to-all-start.1) | async-done | bytes 524320 | tf_op jit(solution)/shard_map/all_to_all | solution.py:488
  65.4 0.0 copy-start.4
  65.4 3.9 %friction.1 = (f32[1024,128]{1,0:T(8,128)}, f32[25,512]{1,0:T(8,128)}, f32[25,2,512]{2,1,0:T(2,128)}) custom-call(f32[1024,128]{1,0:T(8,128)S(1)} %bitcast.20, f32[8,1024]{1,0:T(8,128)S(1)} %get-tuple-element.16.position_ref, s32[2,512]{1,0:T(2,128)S(1)} %bitcast.35, f32[4,512]{1,0:T(4,128)S(1)} %copy-done.16, f32[10,25]{1,0:T(8,128)S(1)} %bitcast.31, ...), custom_call_target="tpu_custom_call" | custom-call | flops 1000000000 | bytes 4000000 | tf_op jit(solution)/shard_map/friction/pallas_call | solution.py:475
  69.3 3.8 %all-to-all-start.2 = ((f32[128,8,128]{2,1,0:T(8,128)}), f32[128,8,128]{2,1,0:T(8,128)S(1)}, u32[]{:S(2)}, u32[]{:S(2)}) async-start(f32[128,8,128]{2,1,0:T(8,128)} %bitcast.11), calls=%async_computation.2 | async-start | bytes 1048576 | tf_op jit(solution)/shard_map/all_to_all | solution.py:488
  73.2 0.0 collective-permute-done.lower_ref
  73.2 0.0 collective-permute-done.1.upper_ref
  73.2 0.0 copy-start.33
  73.2 1.0 %copy-done.33 = f32[9,24,512]{2,1,0:T(8,128)S(1)} copy-done((f32[9,24,512]{2,1,0:T(8,128)S(1)}, f32[9,24,512]{2,1,0:T(8,128)}, u32[]{:S(2)}) %copy-start.33) | copy-done | bytes 442392
  74.2 1.0 %copy-done.35 = f32[9,24,512]{2,1,0:T(8,128)S(1)} copy-done((f32[9,24,512]{2,1,0:T(8,128)S(1)}, f32[9,24,512]{2,1,0:T(8,128)}, u32[]{:S(2)}) %copy-start.35) | copy-done | bytes 442392
  75.3 7.9 %neighbour.1.partial_ref = f32[9,24,512]{2,1,0:T(8,128)S(1)} custom-call(f32[9,24,512]{2,1,0:T(8,128)S(1)} %copy-done.35, f32[9,24,512]{2,1,0:T(8,128)S(1)} %copy-done.33, f32[216,128]{1,0:T(8,128)S(1)} %collective-permute-done.lower_ref, f32[216,128]{1,0:T(8,128)S(1)} %collective-permute-done.1.upper_ref, s32[4,512]{1,0:T(4,128)S(1)} %copy-done.17, ...), custom_call_target="tpu_custom_call" | custom-call | flops 10000000000 | bytes 4000000 | tf_op jit(solution)/shard_map/neighbour/pallas_call | solution.py:475
  83.2 0.0 copy-start.27
  83.2 0.8 copy-done.27
  84.0 3.5 %all-to-all-done.2 = f32[128,8,128]{2,1,0:T(8,128)S(1)} async-done(((f32[128,8,128]{2,1,0:T(8,128)}), f32[128,8,128]{2,1,0:T(8,128)S(1)}, u32[]{:S(2)}, u32[]{:S(2)}) %all-to-all-start.2) | async-done | bytes 524320 | tf_op jit(solution)/shard_map/all_to_all | solution.py:488
  87.4 1.0 %copy-done.26 = f32[256,512]{1,0:T(8,128)S(1)} copy-done((f32[256,512]{1,0:T(8,128)S(1)}, f32[256,512]{1,0:T(8,128)}, u32[]{:S(2)}) %copy-start.26) | copy-done | bytes 524312
  88.5 1.0 %copy-done.28 = f32[9,24,512]{2,1,0:T(8,128)S(1)} copy-done((f32[9,24,512]{2,1,0:T(8,128)S(1)}, f32[9,24,512]{2,1,0:T(8,128)}, u32[]{:S(2)}) %copy-start.28) | copy-done | bytes 442392
  89.5 0.9 %copy-done.30 = f32[256,192]{1,0:T(8,128)S(1)} copy-done((f32[256,192]{1,0:T(8,128)S(1)}, f32[256,192]{1,0:T(8,128)}, u32[]{:S(2)}) %copy-start.30) | copy-done | bytes 196632
  90.4 4.0 %final.1 = f32[9,20,512]{2,1,0:T(8,128)} custom-call(f32[128,128]{1,0:T(8,128)S(1)} %bitcast.22, f32[1024,128]{1,0:T(8,128)S(1)} %bitcast.19, f32[256,512]{1,0:T(8,128)S(1)} %copy-done.26, f32[256,192]{1,0:T(8,128)S(1)} %copy-done.30, f32[9,20,512]{2,1,0:T(8,128)S(1)} %copy-done.5, f32[9,24,512]{2,1,0:T(8,128)S(1)} %copy-done.28, f32[10,25]{1,0:T(8,128)S(1)} %bitcast.32, ...), custom_call_target="tpu_custom_call" | custom-call | flops 1000000000 | bytes 4000000 | tf_op jit(solution)/shard_map/final/pallas_call | solution.py:475
  (41 shorter events, 0.1 us)
Async XLA Ops:
  0.6 14.9 %copy-start.5 = (f32[9,20,512]{2,1,0:T(8,128)S(1)}, f32[9,20,512]{2,1,0:T(8,128)}, u32[]{:S(2)}) copy-start(f32[9,20,512]{2,1,0:T(8,128)} %dofs_ref.3) | copy-start | bytes 1105924
  0.6 0.8 copy-start.15
  1.4 0.7 copy-start.21
  2.1 0.7 copy-start.22
  4.0 11.5 %copy-start.13 = (f32[3,20,20]{2,1,0:T(8,128)S(1)}, f32[3,20,20]{2,1,0:T(8,128)}, u32[]{:S(2)}) copy-start(f32[3,20,20]{2,1,0:T(8,128)} %stiff_ref.3) | copy-start | bytes 14404
  4.0 11.5 %copy-start.14 = (f32[4,10,20]{2,0,1:T(4,128)S(1)}, f32[4,10,20]{2,0,1:T(4,128)}, u32[]{:S(2)}) copy-start(f32[4,10,20]{2,0,1:T(4,128)} %param.32) | copy-start | bytes 9604
  4.0 29.0 %all-to-all-start = ((f32[128,1,128]{2,1,0:T(1,128)}), f32[128,1,128]{2,1,0:T(1,128)S(1)}, u32[]{:S(2)}, u32[]{:S(2)}) async-start(f32[128,1,128]{2,1,0:T(1,128)} %bitcast.3), calls=%async_computation | async-start | bytes 131072 | tf_op jit(solution)/shard_map/all_to_all | solution.py:488
  15.5 0.7 copy-start.24
  16.2 1.1 %copy-start = (f32[3,9,9,512]{3,0,2,1:T(4,128)S(1)}, f32[3,9,9,512]{3,0,2,1:T(4,128)}, u32[]{:S(2)}) copy-start(f32[3,9,9,512]{3,0,2,1:T(4,128)} %param.23) | copy-start | bytes 1492996
  24.0 0.8 copy-start.25
  24.8 0.7 copy-start.29
  25.5 0.8 copy-start.31
  26.3 46.9 %collective-permute-start = (f32[216,128]{1,0:T(8,128)S(1)}, f32[216,128]{1,0:T(8,128)S(1)}, u32[]{:S(2)}, u32[]{:S(2)}) collective-permute-start(f32[216,128]{1,0:T(8,128)S(1)} %get-tuple-element.21), channel_id=1, source_target_pairs={{0,1},{1,2},{2,3},{3,4},{4,5},{5,6},{6,7},{7,8},{8,9},{9,10},{10,1... | collective-permute-start | bytes 331784 | tf_op jit(solution)/shard_map/ppermute | solution.py:19
  29.6 43.6 %collective-permute-start.1 = (f32[216,128]{1,0:T(8,128)S(1)}, f32[216,128]{1,0:T(8,128)S(1)}, u32[]{:S(2)}, u32[]{:S(2)}) collective-permute-start(f32[216,128]{1,0:T(8,128)S(1)} %get-tuple-element.22), channel_id=1, source_target_pairs={{1,0},{2,1},{3,2},{4,3},{5,4},{6,5},{7,6},{8,7},{9,8},{10,9},{11,1... | collective-permute-start | bytes 331784 | tf_op jit(solution)/shard_map/ppermute | solution.py:19
  33.1 18.1 %copy-start.2 = (f32[4,9,9,512]{3,0,2,1:T(4,128)S(1)}, f32[4,9,9,512]{3,0,2,1:T(4,128)}, u32[]{:S(2)}) copy-start(f32[4,9,9,512]{3,0,2,1:T(4,128)} %param.27) | copy-start | bytes 1990660
  42.4 8.8 %copy-start.1 = (f32[3,9,9,512]{3,0,2,1:T(4,128)S(1)}, f32[3,9,9,512]{3,0,2,1:T(4,128)}, u32[]{:S(2)}) copy-start(f32[3,9,9,512]{3,0,2,1:T(4,128)} %param.23) | copy-start | bytes 1492996
  42.4 8.8 %copy-start.12 = (f32[4,20,20]{2,0,1:T(4,128)S(1)}, f32[4,20,20]{2,0,1:T(4,128)}, u32[]{:S(2)}) copy-start(f32[4,20,20]{2,0,1:T(4,128)} %param.25) | copy-start | bytes 19204
  42.4 23.0 %all-to-all-start.1 = ((f32[128,8,128]{2,1,0:T(8,128)}), f32[128,8,128]{2,1,0:T(8,128)S(1)}, u32[]{:S(2)}, u32[]{:S(2)}) async-start(f32[128,8,128]{2,1,0:T(8,128)} %bitcast.7), calls=%async_computation.1 | async-start | bytes 1048576 | tf_op jit(solution)/shard_map/all_to_all | solution.py:488
  51.2 1.0 %copy-start.32 = (f32[9,24,512]{2,1,0:T(8,128)S(1)}, f32[9,24,512]{2,1,0:T(8,128)}, u32[]{:S(2)}) copy-start(f32[9,24,512]{2,1,0:T(8,128)} %copy-done.31) | copy-start | bytes 1327108
  52.2 13.1 %copy-start.6 = (f32[2,25,512]{2,0,1:T(2,128)S(1)}, f32[2,25,512]{2,0,1:T(2,128)}, u32[]{:S(2)}) copy-start(f32[2,25,512]{2,0,1:T(2,128)} %param.39) | copy-start | bytes 307204
  52.2 13.1 %copy-start.7 = (f32[25,512]{1,0:T(8,128)S(1)}, f32[25,512]{1,0:T(8,128)}, u32[]{:S(2)}) copy-start(f32[25,512]{1,0:T(8,128)} %normal_ref.1) | copy-start | bytes 153604
  52.2 13.1 %copy-start.8 = (f32[25,512]{1,0:T(8,128)S(1)}, f32[25,512]{1,0:T(8,128)}, u32[]{:S(2)}) copy-start(f32[25,512]{1,0:T(8,128)} %slip_ref.1) | copy-start | bytes 153604
  52.2 13.1 %copy-start.9 = (f32[25,512]{1,0:T(8,128)S(1)}, f32[25,512]{1,0:T(8,128)}, u32[]{:S(2)}) copy-start(f32[25,512]{1,0:T(8,128)} %static_ref.1) | copy-start | bytes 153604
  52.2 13.1 %copy-start.10 = (f32[25,512]{1,0:T(8,128)S(1)}, f32[25,512]{1,0:T(8,128)}, u32[]{:S(2)}) copy-start(f32[25,512]{1,0:T(8,128)} %drop_ref.1) | copy-start | bytes 153604
  52.3 13.1 %copy-start.11 = (f32[25,512]{1,0:T(8,128)S(1)}, f32[25,512]{1,0:T(8,128)}, u32[]{:S(2)}) copy-start(f32[25,512]{1,0:T(8,128)} %scale_ref.1) | copy-start | bytes 153604
  52.3 13.1 %copy-start.16 = (f32[4,512]{1,0:T(4,128)S(1)}, f32[4,512]{1,0:T(4,128)}, u32[]{:S(2)}) copy-start(f32[4,512]{1,0:T(4,128)} %impedance_ref.3) | copy-start | bytes 24580
  52.3 13.1 %copy-start.19 = (f32[25,10]{0,1:T(8,128)S(1)}, f32[25,10]{0,1:T(8,128)}, u32[]{:S(2)}) copy-start(f32[25,10]{0,1:T(8,128)} %param.33) | copy-start | bytes 3004
  52.3 13.1 %copy-start.20 = (f32[10,25]{1,0:T(8,128)S(1)}, f32[10,25]{1,0:T(8,128)}, u32[]{:S(2)}) copy-start(f32[10,25]{1,0:T(8,128)} %weight_ref.3) | copy-start | bytes 3004
  57.0 0.8 copy-start.34
  57.8 7.6 %copy-start.23 = (s32[512,2]{0,1:T(2,128)S(1)}, s32[512,2]{0,1:T(2,128)}, u32[]{:S(2)}) copy-start(s32[512,2]{0,1:T(2,128)} %param.35) | copy-start | bytes 12292
  65.4 7.8 %copy-start.4 = (f32[4,12,20,20]{3,0,2,1:T(4,128)S(1)}, f32[4,12,20,20]{3,0,2,1:T(4,128)}, u32[]{:S(2)}) copy-start(f32[4,12,20,20]{3,0,2,1:T(4,128)} %param.26) | copy-start | bytes 230404
  69.3 3.9 %copy-start.3 = (f32[4,9,9,512]{3,0,2,1:T(4,128)S(1)}, f32[4,9,9,512]{3,0,2,1:T(4,128)}, u32[]{:S(2)}) copy-start(f32[4,9,9,512]{3,0,2,1:T(4,128)} %param.28) | copy-start | bytes 1990660
  69.3 3.9 %copy-start.17 = (s32[4,512]{1,0:T(4,128)S(1)}, s32[4,512]{1,0:T(4,128)}, u32[]{:S(2)}) copy-start(s32[4,512]{1,0:T(4,128)} %neighbor_ref.1) | copy-start | bytes 24580
  69.3 3.9 %copy-start.18 = (s32[4,512]{1,0:T(4,128)S(1)}, s32[4,512]{1,0:T(4,128)}, u32[]{:S(2)}) copy-start(s32[4,512]{1,0:T(4,128)} %orientation_ref.1) | copy-start | bytes 24580
  69.3 18.1 %all-to-all-start.2 = ((f32[128,8,128]{2,1,0:T(8,128)}), f32[128,8,128]{2,1,0:T(8,128)S(1)}, u32[]{:S(2)}, u32[]{:S(2)}) async-start(f32[128,8,128]{2,1,0:T(8,128)} %bitcast.11), calls=%async_computation.2 | async-start | bytes 1048576 | tf_op jit(solution)/shard_map/all_to_all | solution.py:488
  73.2 1.0 %copy-start.33 = (f32[9,24,512]{2,1,0:T(8,128)S(1)}, f32[9,24,512]{2,1,0:T(8,128)}, u32[]{:S(2)}) copy-start(f32[9,24,512]{2,1,0:T(8,128)} %copy-done.31) | copy-start | bytes 1327108
  74.2 1.0 %copy-start.35 = (f32[9,24,512]{2,1,0:T(8,128)S(1)}, f32[9,24,512]{2,1,0:T(8,128)}, u32[]{:S(2)}) copy-start(f32[9,24,512]{2,1,0:T(8,128)} %copy-done.34) | copy-start | bytes 1327108
  83.2 0.8 copy-start.27
  87.4 1.0 %copy-start.26 = (f32[256,512]{1,0:T(8,128)S(1)}, f32[256,512]{1,0:T(8,128)}, u32[]{:S(2)}) copy-start(f32[256,512]{1,0:T(8,128)} %copy-done.25) | copy-start | bytes 1572868
  88.5 1.0 %copy-start.28 = (f32[9,24,512]{2,1,0:T(8,128)S(1)}, f32[9,24,512]{2,1,0:T(8,128)}, u32[]{:S(2)}) copy-start(f32[9,24,512]{2,1,0:T(8,128)} %copy-done.27) | copy-start | bytes 1327108
  89.5 0.9 %copy-start.30 = (f32[256,192]{1,0:T(8,128)S(1)}, f32[256,192]{1,0:T(8,128)}, u32[]{:S(2)}) copy-start(f32[256,192]{1,0:T(8,128)} %copy-done.29) | copy-start | bytes 589828

commit v2 on v1

--- a/solution.py
+++ b/solution.py
@@ -48,8 +48,8 @@
 
 
 def pack_left(a):
-    repeat = flags((iota((128, 128), 1) & 31) == iota((128, 128), 0))
-    wide = product_full(a, repeat)
+    wide = a + pltpu.roll(a, 32, 1)
+    wide = wide + pltpu.roll(wide, 64, 1)
     high = wide.astype(bf16).astype(f32)
     return jnp.where(iota(wide.shape, 1) < 64, high, wide - high).astype(bf16)
 
@@ -68,8 +68,8 @@
     return flags(iota((128, owner.shape[1]), 0) == owner)
 
 
-def request_kernel(owner_ref, face_ref, impedance_ref, request_ref, position_ref):
-    owned = owner_flags(owner_ref)
+def request_kernel(owner_late, face_late, impedance_late, request_ref, position_ref):
+    owned = owner_flags(owner_late.get())
     owned_half = owned.astype(bf16)
     sides = owned.shape[1]
     block = 256
@@ -83,6 +83,8 @@
         carry = carry + jnp.sum(part, axis=1, keepdims=True)
     position = jnp.concatenate(positions, axis=1)
     position_ref[...] = jnp.broadcast_to(position, position_ref.shape)
+    face_ref = face_late.get()
+    impedance_ref = impedance_late.get()
     wanted = jnp.concatenate([face_ref[0:1, :], face_ref[1:2, :]], axis=1).astype(f32) + 1.0
     zp = jnp.concatenate([impedance_ref[0:1, :], -impedance_ref[1:2, :]], axis=1)
     zs = jnp.concatenate([impedance_ref[2:3, :], -impedance_ref[3:4, :]], axis=1)
@@ -101,21 +103,29 @@
     )
 
 
-def lift_expand(lift_ref, lift_pad):
-    lift_pad[...] = jnp.zeros_like(lift_pad)
+def lift_expand(lift_ref, pad, wide):
+    pad[...] = jnp.zeros_like(pad)
+    wide[...] = jnp.zeros_like(wide)
     for face in range(4):
-        lift_pad[face * 16 : face * 16 + 10, 0:20] = lift_ref[:, face, :]
-    row = iota((256, 64), 0)
-    inner = row & 31
-    third = thirds(inner)
-    source = (row >> 6) * 16 + inner - 10 * third
-    pick = flags((source == iota((256, 64), 1)) & (inner < 30))
-    rows = product_full(pick, lift_pad[...])
-    spread = flags((iota((128, 192), 1) & 31) == iota((128, 192), 0))
-    wide = product_full(rows, spread)
-    row = iota((256, 192), 0)
-    want = ((row >> 5) & 1) * 3 + thirds(row & 31)
-    return jnp.where((iota((256, 192), 1) >> 5) == want, wide, 0.0)
+        pad[0:10, 0:20] = lift_ref[:, face, :]
+        block = pad[...]
+        for k in range(6):
+            first = face * 64 + (k // 3) * 32 + (k % 3) * 10
+            lane = k // 4 * 128
+            moved = pltpu.roll(block, 32 * (k % 4), 1) if k % 4 else block
+            wide[first : first + 10, lane : lane + 128] = moved[0:10]
+    return wide[...]
+
+
+def face_expand(face_ref, pad, wide):
+    pad[...] = jnp.zeros_like(pad)
+    wide[...] = jnp.zeros_like(wide)
+    pad[0:10, 0:25] = face_ref[...]
+    block = pad[...]
+    for j in range(3):
+        moved = pltpu.roll(block, 32 * j, 1) if j else block
+        wide[j * 10 : j * 10 + 10, :] = moved[0:10]
+    return wide[:, 0:96]
 
 
 def predictor_kernel(
@@ -123,17 +133,13 @@
     star_ref,
     stiff_ref,
     lift_ref,
-    copy_ref,
     integral_ref,
     modal_ref,
-    table_ref,
-    lift_out_ref,
-    low_ref,
-    up_ref,
     current,
     moved,
     left,
-    lift_pad,
+    pad,
+    wide,
 ):
     count = dofs_ref.shape[2]
     left[...] = jnp.zeros_like(left)
@@ -164,13 +170,7 @@
             return carry
 
         lax.fori_loop(0, count // 128, tile, 0)
-    whole = integral_ref[...].reshape(216, count)
-    high, low = halves(whole)
-    for index, out in ((0, low_ref), (1, up_ref)):
-        pick = flags(iota((count, 128), 0) == copy_ref[index : index + 1, :]).astype(bf16)
-        out[...] = product(high, pick) + product(low, pick)
-    spread = lift_expand(lift_ref, lift_pad)
-    lift_out_ref[...] = spread
+    spread = lift_expand(lift_ref, pad, wide)[:, 0:192]
     for p in range(9):
         current[p, 0:24, :] = integral_ref[p]
     rows = jnp.concatenate([current[r] for r in trace_rows], axis=0)
@@ -182,7 +182,6 @@
         + product(spread_low, rows_high)
     )
     modal_ref[...] = modal
-    table_ref[...] = modal.T
 
 
 def slots_of(request):
@@ -192,45 +191,50 @@
 
 
 def slot_flags(element, first, many, count):
-    lane = iota((128, count), 1)
+    row = iota((count, 128), 0)
     return jnp.concatenate(
-        [
-            flags(element[:, k : k + 1] == lane).astype(bf16)
-            for k in range(first, first + many)
-        ],
-        axis=0,
-    )
-
-
-def gather_kernel(request_ref, table_ref, out_ref):
-    request = request_ref[...]
-    element, face = slots_of(request)
-    table = jnp.concatenate(halves(table_ref[...]), axis=1)
-    lane = iota((128, 128), 1)
+        [flags(element[k : k + 1, :] == row).astype(bf16) for k in range(first, first + many)],
+        axis=1,
+    )
+
+
+def gather_kernel(request_ref, modal_ref, out_ref):
+    turned = request_ref[...].T
+    element, face = slots_of(turned)
+    modal = jnp.concatenate(halves(modal_ref[...]), axis=0)
+    normal_row = iota((32, 128), 0) < 10
     for r in range(6):
-        pick = slot_flags(element, 4 * r, 4, table_ref.shape[0])
-        both_halves = product(pick, table)
-        found = both_halves[:, 0:256] + both_halves[:, 256:512]
-        block = jnp.zeros((128, 128), f32)
+        pick = slot_flags(element, 4 * r, 4, modal_ref.shape[1])
+        found = product(modal, pick)
+        found = found[0:256] + found[256:512]
+        waves = []
         for j in range(4):
             k = 4 * r + j
-            mine = found[j * 128 : j * 128 + 128]
-            side = face[:, k : k + 1]
-            mine = jnp.where(side >= 2, mine[:, 128:256], mine[:, 0:128])
-            mine = jnp.where((side & 1) == 1, pltpu.roll(mine, 64, 1), mine)
-            velocity = pltpu.roll(mine, 96, 1)
-            z = jnp.where(lane < 10, request[:, 24 + k : 25 + k], request[:, 48 + k : 49 + k])
-            wave = jnp.where(lane < 32, mine - z * velocity, 0.0)
-            if j:
-                wave = pltpu.roll(wave, 32 * j, 1)
-            block = block + wave
-        out_ref[pl.ds(r, 128, stride=8), :] = block
-    for r in range(6, 8):
-        out_ref[pl.ds(r, 128, stride=8), :] = jnp.zeros((128, 128), f32)
-
-
-def inner_kernel(integral_ref, star_ref, minus_ref, stiff_ref, local_ref, out_ref, left, square, moved):
-    count = integral_ref.shape[2]
+            mine = found[:, j * 128 : j * 128 + 128]
+            side = face[k : k + 1, :]
+            state = mine[0:64]
+            for f in range(1, 4):
+                state = jnp.where(side == f, mine[f * 64 : f * 64 + 64], state)
+            z = jnp.where(normal_row, turned[24 + k : 25 + k, :], turned[48 + k : 49 + k, :])
+            waves.append(state[0:32] - z * state[32:64])
+        out_ref[pl.ds(r, 128, stride=6), :] = jnp.concatenate(waves, axis=0).T
+
+
+def inner_kernel(
+    integral_ref,
+    dofs_ref,
+    star_ref,
+    minus_ref,
+    stiff_ref,
+    local_ref,
+    copy_ref,
+    out_ref,
+    low_ref,
+    up_ref,
+    left,
+    square,
+    moved,
+):
     left[...] = jnp.zeros_like(left)
     square[...] = jnp.zeros_like(square)
     for d in range(3):
@@ -239,6 +243,13 @@
     for f in range(4):
         left[96 + f * 32 : 96 + f * 32 + 20, 0:20] = local_ref[:, f, :]
     packed = pack_left(left[...])
+    count = integral_ref.shape[2]
+    whole = jnp.concatenate(halves(integral_ref[...].reshape(216, count)), axis=0)
+    wanted = jnp.concatenate([copy_ref[0:1, :], copy_ref[1:2, :]], axis=1)
+    found = product(whole, flags(iota((count, 256), 0) == wanted).astype(bf16))
+    found = found[0:216] + found[216:432]
+    low_ref[...] = found[:, 0:128]
+    up_ref[...] = found[:, 128:256]
     empty = jnp.zeros((8, count), f32)
     for q in range(9):
         moved[q] = product(
@@ -262,6 +273,8 @@
         return carry
 
     lax.fori_loop(0, count // 128, tile, 0)
+    for p in range(9):
+        out_ref[p, 0:20, :] += dofs_ref[p]
 
 
 def neighbour_kernel(
@@ -273,11 +286,30 @@
     orientation_ref,
     plus_ref,
     flux_ref,
+    lift_ref,
+    eval_ref,
+    weight_ref,
     out_ref,
+    own_ref,
+    spread_ref,
     left,
     moved,
+    pad,
+    wide,
+    face_wide,
 ):
     count = integral_ref.shape[2]
+    evaluate = face_expand(eval_ref, pad, face_wide)
+    weight = face_expand(weight_ref, pad, face_wide)
+    gauss = product_full(weight, evaluate, 1, 1) * (1.0 / time_step)
+    spread = lift_expand(lift_ref, pad, wide)
+    spread_ref[...] = spread.T[0:192, :]
+    outer = jnp.concatenate(
+        [product_full(gauss, spread[f * 64 : f * 64 + 32, 0:128]) for f in range(4)], axis=0
+    )
+    empty = jnp.zeros((8, count), f32)
+    rows = [jnp.concatenate([integral_ref[r], empty], axis=0) for r in trace_rows[0:3]]
+    own_ref[...] = product_full(outer[:, 0:96], jnp.concatenate(rows, axis=0))
     extended = jnp.concatenate(
         [integral_ref[...].reshape(216, count), lower_ref[...], upper_ref[...]], axis=1
     )
@@ -285,7 +317,6 @@
     width = extended.shape[1]
     out_ref[...] = inner_ref[...]
     left[...] = jnp.zeros_like(left)
-    empty = jnp.zeros((8, count), f32)
     for f in range(4):
         pick = flags(iota((width, count), 0) == neighbor_ref[f : f + 1, :]).astype(bf16)
         found = product(extended, pick)
@@ -314,16 +345,6 @@
             return carry
 
         lax.fori_loop(0, count // 128, tile, 0)
-
-
-def face_expand(face_ref, pad):
-    pad[...] = jnp.zeros_like(pad)
-    pad[0:10, 0:25] = face_ref[...]
-    row = iota((32, 16), 0)
-    pick = flags((row - 10 * thirds(row) == iota((32, 16), 1)) & (row < 30))
-    spread = flags((iota((128, 96), 1) & 31) == iota((128, 96), 0))
-    wide = product_full(product_full(pick, pad[...]), spread)
-    return jnp.where((iota((32, 96), 1) >> 5) == thirds(iota((32, 96), 0)), wide, 0.0)
 
 
 def friction_kernel(
@@ -342,17 +363,18 @@
     reply_ref,
     slip_out_ref,
     traction_ref,
+    states,
     pad,
-    states,
+    face_wide,
 ):
     owned = owner_flags(owner_ref).astype(bf16)
+    owned_twice = jnp.concatenate([owned, owned], axis=0)
     position = position_ref[0:1, :]
     faults = slip_ref.shape[1]
     wave = jnp.zeros((32, 2 * faults), f32)
     for r in range(6):
-        high, low = halves(arrived_ref[pl.ds(r, 128, stride=8), :].T)
-        found = product(jnp.concatenate([high, low], axis=0), owned)
-        found = found[0:128] + found[128:256]
+        high, low = halves(arrived_ref[pl.ds(r, 128, stride=6), :].T)
+        found = product(jnp.concatenate([high, low], axis=1), owned_twice)
         for j in range(4):
             wave = jnp.where(position == float(4 * r + j), found[j * 32 : j * 32 + 32], wave)
     pwave_minus = impedance_ref[0:1, :]
@@ -368,8 +390,7 @@
         + jnp.where(normal_row, pwave_minus / pwave_sum, swave_minus / swave_sum)
         * wave[:, faults : 2 * faults]
     ) * (1.0 / time_step)
-    evaluate = face_expand(eval_ref, pad)
-    states[...] = product_full(evaluate, modal, 0, 0)
+    states[...] = product_full(face_expand(eval_ref, pad, face_wide), modal, 0, 0)
     normal = states[0:25, :]
     initial = (shear_ref[:, 0, :], shear_ref[:, 1, :])
     shear = (states[32:57, :] + initial[0], states[64:89, :] + initial[1])
@@ -386,48 +407,40 @@
     traction_ref[:, 1, :] = final[1]
     states[32:57, :] = final[0] - initial[0]
     states[64:89, :] = final[1] - initial[1]
-    weight = face_expand(weight_ref, pad)
-    imposed = product_full(weight, states[...])
+    imposed = product_full(face_expand(weight_ref, pad, face_wide), states[...])
     high = imposed.astype(bf16).astype(f32)
     low = imposed - high
     high = jnp.concatenate([high, high], axis=1)
     low = jnp.concatenate([low, low], axis=1)
+    rows = []
+    for k in range(24):
+        here = position == float(k)
+        rows.append(jnp.where(here, high, 0.0).astype(bf16))
+        rows.append(jnp.where(here, low, 0.0).astype(bf16))
+    blocks = product(jnp.concatenate(rows, axis=0), owned, 1, 1)
     for r in range(6):
-        here = [position == float(4 * r + j) for j in range(4)]
-        rows = jnp.concatenate(
-            [jnp.where(here[j], high, 0.0).astype(bf16) for j in range(4)]
-            + [jnp.where(here[j], low, 0.0).astype(bf16) for j in range(4)],
-            axis=0,
-        )
-        block = product(rows, owned, 1, 1)
-        reply_ref[pl.ds(r, 128, stride=8), :] = (block[0:128] + block[128:256]).T
-    for r in range(6, 8):
-        reply_ref[pl.ds(r, 128, stride=8), :] = jnp.zeros((128, 128), f32)
+        parts = [blocks[k * 64 : k * 64 + 32] + blocks[k * 64 + 32 : k * 64 + 64] for k in range(4 * r, 4 * r + 4)]
+        reply_ref[pl.ds(r, 128, stride=6), :] = jnp.concatenate(parts, axis=0).T
 
 
 def final_kernel(
     request_ref,
     returned_ref,
-    modal_ref,
-    lift_ref,
-    dofs_ref,
+    own_ref,
+    spread_ref,
     partial_ref,
-    eval_ref,
-    weight_ref,
     out_ref,
-    pad,
     totals,
 ):
-    count = dofs_ref.shape[2]
+    count = partial_ref.shape[2]
     request = request_ref[...]
-    element, _ = slots_of(request)
     turned = request.T
-    _, face = slots_of(turned)
+    element, face = slots_of(turned)
     inverse = jnp.where(turned == 0.0, 0.0, 1.0 / jnp.where(turned == 0.0, 1.0, turned))
     row = iota((32, 128), 0)
     normal_row = (row < 10) | (row == 30)
     for r in range(6):
-        block = returned_ref[pl.ds(r, 128, stride=8), :].T
+        block = returned_ref[pl.ds(r, 128, stride=6), :].T
         highs = []
         lows = []
         for j in range(4):
@@ -444,42 +457,71 @@
             [jnp.concatenate(highs, axis=1), jnp.concatenate(lows, axis=1)], axis=0
         )
         pick = slot_flags(element, 4 * r, 4, count)
-        part = product(values, pick)
+        part = product(values, pick, 1, 1)
         part = part[0:256] + part[256:512]
         if r:
             totals[...] += part
         else:
             totals[...] = part
-    evaluate = face_expand(eval_ref, pad)
-    weight = face_expand(weight_ref, pad)
-    gauss = product_full(weight, evaluate, 1, 1) * (1.0 / time_step)
     row = iota((32, count), 0) < 10
     states = []
     for f in range(4):
         base = f * 64
-        own = product_full(gauss, modal_ref[base : base + 32, :])
+        own = own_ref[f * 32 : f * 32 + 32, :]
         sides = totals[base + 30 : base + 31, :]
         scaled = jnp.where(row, totals[base + 62 : base + 63, :], totals[base + 63 : base + 64, :])
         states.append(totals[base : base + 32, :] - sides * own)
         states.append(totals[base + 32 : base + 64, :] - scaled * own)
-    fault = product_full(lift_ref[...], jnp.concatenate(states, axis=0), 0, 0)
+    high, low = halves(jnp.concatenate(states, axis=0))
+    spread_high, spread_low = halves(spread_ref[...])
+    fault = product(
+        jnp.concatenate([spread_high, spread_high, spread_low], axis=1),
+        jnp.concatenate([high, low, high], axis=0),
+    )
     for p in range(9):
-        value = dofs_ref[p] + partial_ref[p, 0:20, :]
+        value = partial_ref[p, 0:20, :]
         if p in trace_rows:
             k = trace_rows.index(p)
             value = value + fault[k * 32 : k * 32 + 20, :]
         out_ref[p] = value
 
 
-def call(kernel, name, outs, scratch, operands, flops):
+class Arriving:
+    def __init__(self, copy, ref):
+        self.copy = copy
+        self.ref = ref
+
+    def get(self):
+        self.copy.wait()
+        return self.ref
+
+
+def call(kernel, name, outs, scratch, operands, flops, late=(), room=20):
+    inputs = len(operands)
+    outputs = len(outs)
+    own = len(scratch)
+
+    def body(*refs):
+        sources = list(refs[:inputs])
+        spare = refs[inputs + outputs + own : -1]
+        flags_ref = refs[-1]
+        for index, place in enumerate(late):
+            copy = pltpu.make_async_copy(sources[place], spare[index], flags_ref.at[index])
+            copy.start()
+            sources[place] = Arriving(copy, spare[index])
+        kernel(*sources, *refs[inputs : inputs + outputs + own])
+
+    far = pl.BlockSpec(memory_space=pltpu.HBM)
     return pl.pallas_call(
-        kernel,
+        body,
         name=name,
         out_shape=[jax.ShapeDtypeStruct(shape, f32) for shape in outs],
-        in_specs=[vmem] * len(operands),
-        out_specs=[vmem] * len(outs),
-        scratch_shapes=[pltpu.VMEM(shape, f32) for shape in scratch],
-        compiler_params=pltpu.CompilerParams(vmem_limit_bytes=48 * 1024 * 1024),
+        in_specs=[far if i in late else vmem for i in range(inputs)],
+        out_specs=[vmem] * outputs,
+        scratch_shapes=[pltpu.VMEM(shape, f32) for shape in scratch]
+        + [pltpu.VMEM(operands[i].shape, operands[i].dtype) for i in late]
+        + [pltpu.SemaphoreType.DMA((max(1, len(late)),))],
+        compiler_params=pltpu.CompilerParams(vmem_limit_bytes=room * 1024 * 1024),
         cost_estimate=pl.CostEstimate(flops=flops, bytes_accessed=4_000_000, transcendentals=0),
     )(*operands)
 
@@ -531,35 +573,35 @@
         [],
         [owner, wanted, impedance],
         10**8,
+        late=(0, 1, 2),
+        room=60,
     )
     asked = exchange(request.reshape(128, 1, 128)).reshape(128, 128)
-    integral, modal, table, spread, low, up = call(
+    integral, modal = call(
         predictor_kernel,
         "predictor",
-        [(9, 24, count), (256, count), (count, 256), (256, 192), (216, 128), (216, 128)],
-        [(9, 32, count), (9, 96, count), (96, 128), (64, 128)],
-        [dofs, star, stiff, lift, copy_list],
+        [(9, 24, count), (256, count)],
+        [(9, 32, count), (9, 96, count), (96, 128), (16, 128), (256, 256)],
+        [dofs, star, stiff, lift],
         10**10,
     )
-    (payload,) = call(
-        gather_kernel, "gather", [(1024, 128)], [], [asked, table], 10**9
-    )
-    arrived = exchange(payload.reshape(128, 8, 128)).reshape(1024, 128)
+    (payload,) = call(gather_kernel, "gather", [(768, 128)], [], [asked, modal], 10**9)
+    arrived = exchange(payload.reshape(128, 1, 768)).reshape(768, 128)
+    inner, low, up = call(
+        inner_kernel,
+        "inner",
+        [(9, 24, count), (216, 128), (216, 128)],
+        [(224, 128), (128, 128), (9, 224, count)],
+        [integral, dofs, star, minus, stiff, local, copy_list],
+        10**10,
+    )
     from_lower = from_behind(up, both, 1)
     from_upper = from_behind(low, both, -1)
-    (inner,) = call(
-        inner_kernel,
-        "inner",
-        [(9, 24, count)],
-        [(224, 128), (128, 128), (9, 224, count)],
-        [integral, star, minus, stiff, local],
-        10**10,
-    )
     reply, new_slip, traction = call(
         friction_kernel,
         "friction",
-        [(1024, 128), (25, faults), (25, 2, faults)],
-        [(16, 128), (96, faults)],
+        [(768, 128), (25, faults), (25, 2, faults)],
+        [(96, faults), (16, 128), (32, 128)],
         [
             arrived,
             position,
@@ -576,21 +618,33 @@
         ],
         10**9,
     )
-    returned = exchange(reply.reshape(128, 8, 128)).reshape(1024, 128)
-    (partial,) = call(
+    returned = exchange(reply.reshape(128, 1, 768)).reshape(768, 128)
+    partial, own, spread = call(
         neighbour_kernel,
         "neighbour",
-        [(9, 24, count)],
-        [(288, 128), (9, 24, count)],
-        [inner, integral, from_lower, from_upper, neighbor, orientation, plus, flux],
+        [(9, 24, count), (128, count), (192, 256)],
+        [(288, 128), (9, 24, count), (16, 128), (256, 256), (32, 128)],
+        [
+            inner,
+            integral,
+            from_lower,
+            from_upper,
+            neighbor,
+            orientation,
+            plus,
+            flux,
+            lift,
+            evaluate,
+            face_weight,
+        ],
         10**10,
     )
     (new_dofs,) = call(
         final_kernel,
         "final",
         [(9, 20, count)],
-        [(16, 128), (256, count)],
-        [asked, returned, modal, spread, dofs, partial, evaluate, face_weight],
+        [(256, count)],
+        [asked, returned, own, spread, partial],
         10**9,
     )
     return (new_dofs, new_slip, jnp.transpose(traction, (1, 0, 2)))

time: 95.2 us -> 75.2 us (0.79)
  local copies, waits for them, and re-layouts: 13.7 us -> 3.61 us
  Pallas kernels: 37.8 us -> 28.7 us
  waiting for transfers between devices: 11 us -> 7.35 us
  starting transfers between devices: 30.9 us -> 33.8 us
    unnamed x72 -> x50, local copies, waits for them, and re-layouts: 13.7 us -> 3.61 us
    pallas_call x7, Pallas kernels: 37.8 us -> 28.7 us  [call(): pl.pallas_call(body, name=name, out_shape=[jax.ShapeDtypeStruct(shape, f3...]
    all_to_all x3, waiting for transfers between devices: 11 us -> 7.34 us  [exchange(): return lax.all_to_all(block, both, split_axis=0, concat_axis=0, tiled=True)]
    all_to_all x3, starting transfers between devices: 24.1 us -> 26.9 us  [exchange(): return lax.all_to_all(block, both, split_axis=0, concat_axis=0, tiled=True)]
  transfers between devices with their start and end apart: 5 -> 5, of which waited for: 2 -> 2; matrix products, arithmetic and copies ran while one was open for 0% -> 0% of each run, Pallas kernels for 34% -> 28%
where the time goes in v2:
time: 75.2 us; the launch traced here: 74.8 us
  starting transfers between devices  33.8 us (45%)
  Pallas kernels  28.7 us (38%)
  waiting for transfers between devices  7.35 us (10%)
  local copies, waits for them, and re-layouts  3.61 us (5%)
  between operations  1.23 us (2%)
    pallas_call x7, Pallas kernels, call(): pl.pallas_call(body, name=name, out_shape=[jax.ShapeDtypeStruct(shape, f3...  28.7 us
    all_to_all x3, starting transfers between devices, exchange(): return lax.all_to_all(block, both, split_axis=0, concat_axis=0, tiled=True)  26.9 us
    all_to_all x3, waiting for transfers between devices, exchange(): return lax.all_to_all(block, both, split_axis=0, concat_axis=0, tiled=True)  7.34 us
    ppermute x2, starting transfers between devices, from_behind(): return lax.ppermute(block, axis, route)  6.89 us
    unnamed x50, local copies, waits for them, and re-layouts  3.61 us
  transfers between devices with their start and end apart: 5, of which 2 were waited for; matrix products, arithmetic and copies ran while one was open for 0% of the time, Pallas kernels for 28%

profile of v2, /device:TPU:1, one launch (start us, length us, event | category | flops | bytes accessed | tf_op | source)
XLA Modules:
  0.0 74.8 jit_solution(1106061751810528946)
XLA Ops:
  0.6 0.0 copy-start.5
  0.6 2.1 %request.1 = (f32[128,128]{1,0:T(8,128)}, f32[8,1024]{1,0:T(8,128)}) custom-call(s32[2,512]{1,0:T(2,128)} %bitcast.34, s32[2,512]{1,0:T(2,128)} %bitcast.37, f32[4,512]{1,0:T(4,128)} %refs_3_.1), custom_call_target="tpu_custom_call" | custom-call | flops 100000000 | bytes 4000000 | tf_op jit(solution)/shard_map/request/pallas_call | solution.py:515
  2.8 0.0 copy-start.13
  2.8 0.0 copy-start.14
  2.8 11.5 %all-to-all-start = ((f32[128,1,128]{2,1,0:T(1,128)}), f32[128,1,128]{2,1,0:T(1,128)S(1)}, u32[]{:S(2)}, u32[]{:S(2)}) async-start(f32[128,1,128]{2,1,0:T(1,128)} %bitcast.36), calls=%async_computation | async-start | bytes 131072 | tf_op jit(solution)/shard_map/all_to_all | solution.py:530
  14.3 0.0 copy-done.5
  14.3 0.0 copy-done.13
  14.3 0.0 copy-done.14
  14.3 0.0 copy-start
  14.4 1.1 %copy-done = f32[3,9,9,512]{3,0,2,1:T(4,128)S(1)} copy-done((f32[3,9,9,512]{3,0,2,1:T(4,128)S(1)}, f32[3,9,9,512]{3,0,2,1:T(4,128)}, u32[]{:S(2)}) %copy-start) | copy-done | bytes 497688
  15.4 5.5 %predictor.1 = (f32[9,24,512]{2,1,0:T(8,128)S(1)}, f32[256,512]{1,0:T(8,128)S(1)}) custom-call(f32[9,20,512]{2,1,0:T(8,128)S(1)} %copy-done.5, f32[9,9,3,512]{3,2,1,0:T(4,128)S(1)} %bitcast.23, f32[3,20,20]{2,1,0:T(8,128)S(1)} %copy-done.13, f32[10,4,20]{2,1,0:T(4,128)S(1)} %bitcast.30), custom_call_target="tpu_custom_call" | custom-call | flops 10000000000 | bytes 4000000 | tf_op jit(solution)/shard_map/predictor/pallas_call | solution.py:515
  20.9 3.2 %all-to-all-done = f32[128,1,128]{2,1,0:T(1,128)S(1)} async-done(((f32[128,1,128]{2,1,0:T(1,128)}), f32[128,1,128]{2,1,0:T(1,128)S(1)}, u32[]{:S(2)}, u32[]{:S(2)}) %all-to-all-start) | async-done | bytes 65568 | tf_op jit(solution)/shard_map/all_to_all | solution.py:530
  24.1 2.7 %gather.1 = f32[768,128]{1,0:T(8,128)} custom-call(f32[128,128]{1,0:T(8,128)S(1)} %bitcast.21, f32[256,512]{1,0:T(8,128)S(1)} %get-tuple-element.17.refs_1_), custom_call_target="tpu_custom_call" | custom-call | flops 1000000000 | bytes 4000000 | tf_op jit(solution)/shard_map/gather/pallas_call | solution.py:515
  26.9 0.0 copy-start.1
  26.9 0.0 copy-start.12
  26.9 6.6 %all-to-all-start.1 = ((f32[128,1,768]{2,1,0:T(1,128)}), f32[128,1,768]{2,1,0:T(1,128)S(1)}, u32[]{:S(2)}, u32[]{:S(2)}) async-start(f32[128,1,768]{2,1,0:T(1,128)} %bitcast.7), calls=%async_computation.1 | async-start | bytes 786432 | tf_op jit(solution)/shard_map/all_to_all | solution.py:530
  33.5 0.0 copy-start.21
  33.5 0.0 copy-done.2
  33.5 0.0 copy-done.1
  33.5 0.0 copy-done.12
  33.5 0.6 copy-done.21
  34.2 0.0 copy-start.10
  34.2 0.0 copy-start.11
  34.2 0.0 copy-start.16
  34.2 0.0 copy-start.17
  34.2 0.0 copy-start.20
  34.3 0.0 copy-start.22
  34.3 4.8 %inner.1 = (f32[9,24,512]{2,1,0:T(8,128)S(1)}, f32[216,128]{1,0:T(8,128)S(1)}, f32[216,128]{1,0:T(8,128)S(1)}) custom-call(f32[9,24,512]{2,1,0:T(8,128)S(1)} %get-tuple-element.20.refs_0_.refs_1_, f32[9,20,512]{2,1,0:T(8,128)S(1)} %copy-done.5, f32[9,9,3,512]{3,2,1,0:T(4,128)S(1)} %bitcast.24, f32[9,9,4,512]{3,2,1,0:T(4,128)S(1)} %bitcast.25, ...), custom_call_target="tpu_custom_call" | custom-call | flops 10000000000 | bytes 4000000 | tf_op jit(solution)/shard_map/inner/pallas_call | solution.py:515
  39.0 0.0 copy-start.23
  39.0 0.8 %copy-done.23 = f32[9,24,512]{2,1,0:T(8,128)} copy-done((f32[9,24,512]{2,1,0:T(8,128)}, f32[9,24,512]{2,1,0:T(8,128)S(1)}, u32[]{:S(2)}) %copy-start.23) | copy-done | bytes 442392
  39.8 3.4 %collective-permute-start = (f32[216,128]{1,0:T(8,128)S(1)}, f32[216,128]{1,0:T(8,128)S(1)}, u32[]{:S(2)}, u32[]{:S(2)}) collective-permute-start(f32[216,128]{1,0:T(8,128)S(1)} %get-tuple-element.22), channel_id=1, source_target_pairs={{0,1},{1,2},{2,3},{3,4},{4,5},{5,6},{6,7},{7,8},{8,9},{9,10},{10,1... | collective-permute-start | bytes 331784 | tf_op jit(solution)/shard_map/ppermute | solution.py:19
  43.2 3.5 %collective-permute-start.1 = (f32[216,128]{1,0:T(8,128)S(1)}, f32[216,128]{1,0:T(8,128)S(1)}, u32[]{:S(2)}, u32[]{:S(2)}) collective-permute-start(f32[216,128]{1,0:T(8,128)S(1)} %get-tuple-element.23), channel_id=1, source_target_pairs={{1,0},{2,1},{3,2},{4,3},{5,4},{6,5},{7,6},{8,7},{9,8},{10,9},{11,1... | collective-permute-start | bytes 331784 | tf_op jit(solution)/shard_map/ppermute | solution.py:19
  46.7 0.0 all-to-all-done.1
  46.7 0.0 copy-done.6
  46.7 0.0 copy-done.7
  46.8 0.0 copy-start.4
  46.8 3.1 %friction.1 = (f32[768,128]{1,0:T(8,128)}, f32[25,512]{1,0:T(8,128)}, f32[25,2,512]{2,1,0:T(2,128)}) custom-call(f32[768,128]{1,0:T(8,128)S(1)} %bitcast.20, f32[8,1024]{1,0:T(8,128)S(1)} %copy-done.22, s32[2,512]{1,0:T(2,128)S(1)} %bitcast.35, f32[4,512]{1,0:T(4,128)S(1)} %copy-done.15, f32[10,25]{1,0:T(8,128)S(1)} %bitcast.32, f32[10,25]{1,0:T(8,128)S(1)} %copy-done.17, ...), custom_call_target="tpu_custom_call" | custom-call | flops 1000000000 | bytes 4000000 | tf_op jit(solution)/shard_map/friction/pallas_call | solution.py:515
  50.0 0.0 copy-start.3
  50.0 0.0 copy-start.18
  50.0 0.0 copy-start.19
  50.0 8.8 %all-to-all-start.2 = ((f32[128,1,768]{2,1,0:T(1,128)}), f32[128,1,768]{2,1,0:T(1,128)S(1)}, u32[]{:S(2)}, u32[]{:S(2)}) async-start(f32[128,1,768]{2,1,0:T(1,128)} %bitcast.11), calls=%async_computation.2 | async-start | bytes 786432 | tf_op jit(solution)/shard_map/all_to_all | solution.py:530
  58.9 0.0 collective-permute-done.refs_2_
  58.9 0.0 collective-permute-done.1.refs_3_
  58.9 0.0 copy-start.24
  58.9 1.0 %copy-done.24 = f32[9,24,512]{2,1,0:T(8,128)S(1)} copy-done((f32[9,24,512]{2,1,0:T(8,128)S(1)}, f32[9,24,512]{2,1,0:T(8,128)}, u32[]{:S(2)}) %copy-start.24) | copy-done | bytes 442392
  59.9 7.5 %neighbour.1 = (f32[9,24,512]{2,1,0:T(8,128)S(1)}, f32[128,512]{1,0:T(8,128)S(1)}, f32[192,256]{1,0:T(8,128)S(1)}) custom-call(f32[9,24,512]{2,1,0:T(8,128)S(1)} %copy-done.24, f32[9,24,512]{2,1,0:T(8,128)S(1)} %get-tuple-element.20.refs_0_.refs_1_, f32[216,128]{1,0:T(8,128)S(1)} %collective-permute-done.refs_2_, ...), custom_call_target="tpu_custom_call" | custom-call | flops 10000000000 | bytes 4000000 | tf_op jit(solution)/shard_map/neighbour/pallas_call | solution.py:515
  67.4 4.2 %all-to-all-done.2 = f32[128,1,768]{2,1,0:T(1,128)S(1)} async-done(((f32[128,1,768]{2,1,0:T(1,128)}), f32[128,1,768]{2,1,0:T(1,128)S(1)}, u32[]{:S(2)}, u32[]{:S(2)}) %all-to-all-start.2) | async-done | bytes 393248 | tf_op jit(solution)/shard_map/all_to_all | solution.py:530
  71.6 3.0 %final.1 = f32[9,20,512]{2,1,0:T(8,128)} custom-call(f32[128,128]{1,0:T(8,128)S(1)} %bitcast.22, f32[768,128]{1,0:T(8,128)S(1)} %bitcast.19, f32[128,512]{1,0:T(8,128)S(1)} %get-tuple-element.24.refs_2_, f32[192,256]{1,0:T(8,128)S(1)} %get-tuple-element.25.refs_3_, f32[9,24,512]{2,1,0:T(8,128)S(1)} %get-tuple-element.26.refs_4_), custom_call_target="tpu_custom_call" | custom-call | flops 1000000000 | bytes 4000000 | tf_op jit(solution)/shard_map/final/pallas_call | solution.py:515
  (19 shorter events, 0.0 us)
Async XLA Ops:
  0.6 13.7 %copy-start.5 = (f32[9,20,512]{2,1,0:T(8,128)S(1)}, f32[9,20,512]{2,1,0:T(8,128)}, u32[]{:S(2)}) copy-start(f32[9,20,512]{2,1,0:T(8,128)} %refs_1_.1) | copy-start | bytes 1105924
  2.8 11.5 %copy-start.13 = (f32[3,20,20]{2,1,0:T(8,128)S(1)}, f32[3,20,20]{2,1,0:T(8,128)}, u32[]{:S(2)}) copy-start(f32[3,20,20]{2,1,0:T(8,128)} %refs_4_.2) | copy-start | bytes 14404
  2.8 11.5 %copy-start.14 = (f32[4,10,20]{2,0,1:T(4,128)S(1)}, f32[4,10,20]{2,0,1:T(4,128)}, u32[]{:S(2)}) copy-start(f32[4,10,20]{2,0,1:T(4,128)} %param.32) | copy-start | bytes 9604
  2.8 21.3 %all-to-all-start = ((f32[128,1,128]{2,1,0:T(1,128)}), f32[128,1,128]{2,1,0:T(1,128)S(1)}, u32[]{:S(2)}, u32[]{:S(2)}) async-start(f32[128,1,128]{2,1,0:T(1,128)} %bitcast.36), calls=%async_computation | async-start | bytes 131072 | tf_op jit(solution)/shard_map/all_to_all | solution.py:530
  14.3 1.1 %copy-start = (f32[3,9,9,512]{3,0,2,1:T(4,128)S(1)}, f32[3,9,9,512]{3,0,2,1:T(4,128)}, u32[]{:S(2)}) copy-start(f32[3,9,9,512]{3,0,2,1:T(4,128)} %param.23) | copy-start | bytes 1492996
  24.1 9.4 %copy-start.2 = (f32[4,9,9,512]{3,0,2,1:T(4,128)S(1)}, f32[4,9,9,512]{3,0,2,1:T(4,128)}, u32[]{:S(2)}) copy-start(f32[4,9,9,512]{3,0,2,1:T(4,128)} %param.27) | copy-start | bytes 1990660
  26.9 6.7 %copy-start.1 = (f32[3,9,9,512]{3,0,2,1:T(4,128)S(1)}, f32[3,9,9,512]{3,0,2,1:T(4,128)}, u32[]{:S(2)}) copy-start(f32[3,9,9,512]{3,0,2,1:T(4,128)} %param.23) | copy-start | bytes 1492996
  26.9 6.7 %copy-start.12 = (f32[4,20,20]{2,0,1:T(4,128)S(1)}, f32[4,20,20]{2,0,1:T(4,128)}, u32[]{:S(2)}) copy-start(f32[4,20,20]{2,0,1:T(4,128)} %param.25) | copy-start | bytes 19204
  26.9 19.8 %all-to-all-start.1 = ((f32[128,1,768]{2,1,0:T(1,128)}), f32[128,1,768]{2,1,0:T(1,128)S(1)}, u32[]{:S(2)}, u32[]{:S(2)}) async-start(f32[128,1,768]{2,1,0:T(1,128)} %bitcast.7), calls=%async_computation.1 | async-start | bytes 786432 | tf_op jit(solution)/shard_map/all_to_all | solution.py:530
  33.5 0.7 copy-start.21
  34.2 12.5 %copy-start.6 = (f32[2,25,512]{2,0,1:T(2,128)S(1)}, f32[2,25,512]{2,0,1:T(2,128)}, u32[]{:S(2)}) copy-start(f32[2,25,512]{2,0,1:T(2,128)} %param.39) | copy-start | bytes 307204
  34.2 12.5 %copy-start.7 = (f32[25,512]{1,0:T(8,128)S(1)}, f32[25,512]{1,0:T(8,128)}, u32[]{:S(2)}) copy-start(f32[25,512]{1,0:T(8,128)} %refs_6_.2) | copy-start | bytes 153604
  34.2 12.5 %copy-start.8 = (f32[25,512]{1,0:T(8,128)S(1)}, f32[25,512]{1,0:T(8,128)}, u32[]{:S(2)}) copy-start(f32[25,512]{1,0:T(8,128)} %refs_8_.1) | copy-start | bytes 153604
  34.2 12.6 %copy-start.9 = (f32[25,512]{1,0:T(8,128)S(1)}, f32[25,512]{1,0:T(8,128)}, u32[]{:S(2)}) copy-start(f32[25,512]{1,0:T(8,128)} %refs_9_.1) | copy-start | bytes 153604
  34.2 12.6 %copy-start.10 = (f32[25,512]{1,0:T(8,128)S(1)}, f32[25,512]{1,0:T(8,128)}, u32[]{:S(2)}) copy-start(f32[25,512]{1,0:T(8,128)} %refs_10_.2) | copy-start | bytes 153604
  34.2 12.6 %copy-start.11 = (f32[25,512]{1,0:T(8,128)S(1)}, f32[25,512]{1,0:T(8,128)}, u32[]{:S(2)}) copy-start(f32[25,512]{1,0:T(8,128)} %refs_11_.1) | copy-start | bytes 153604
  34.2 12.6 %copy-start.16 = (f32[25,10]{0,1:T(8,128)S(1)}, f32[25,10]{0,1:T(8,128)}, u32[]{:S(2)}) copy-start(f32[25,10]{0,1:T(8,128)} %param.33) | copy-start | bytes 3004
  34.2 12.6 %copy-start.17 = (f32[10,25]{1,0:T(8,128)S(1)}, f32[10,25]{1,0:T(8,128)}, u32[]{:S(2)}) copy-start(f32[10,25]{1,0:T(8,128)} %refs_10_.3) | copy-start | bytes 3004
  34.2 12.6 %copy-start.20 = (s32[512,2]{0,1:T(2,128)S(1)}, s32[512,2]{0,1:T(2,128)}, u32[]{:S(2)}) copy-start(s32[512,2]{0,1:T(2,128)} %param.35) | copy-start | bytes 12292
  34.3 12.6 %copy-start.22 = (f32[8,1024]{1,0:T(8,128)S(1)}, f32[8,1024]{1,0:T(8,128)}, u32[]{:S(2)}) copy-start(f32[8,1024]{1,0:T(8,128)} %get-tuple-element.18.refs_1_) | copy-start | bytes 98308
  39.0 0.8 %copy-start.23 = (f32[9,24,512]{2,1,0:T(8,128)}, f32[9,24,512]{2,1,0:T(8,128)S(1)}, u32[]{:S(2)}) copy-start(f32[9,24,512]{2,1,0:T(8,128)S(1)} %get-tuple-element.21.refs_0_) | copy-start | bytes 1327108
  39.8 7.0 %copy-start.15 = (f32[4,512]{1,0:T(4,128)S(1)}, f32[4,512]{1,0:T(4,128)}, u32[]{:S(2)}) copy-start(f32[4,512]{1,0:T(4,128)} %refs_3_.1) | copy-start | bytes 24580
  39.8 19.1 %collective-permute-start = (f32[216,128]{1,0:T(8,128)S(1)}, f32[216,128]{1,0:T(8,128)S(1)}, u32[]{:S(2)}, u32[]{:S(2)}) collective-permute-start(f32[216,128]{1,0:T(8,128)S(1)} %get-tuple-element.22), channel_id=1, source_target_pairs={{0,1},{1,2},{2,3},{3,4},{4,5},{5,6},{6,7},{7,8},{8,9},{9,10},{10,1... | collective-permute-start | bytes 331784 | tf_op jit(solution)/shard_map/ppermute | solution.py:19
  43.2 15.7 %collective-permute-start.1 = (f32[216,128]{1,0:T(8,128)S(1)}, f32[216,128]{1,0:T(8,128)S(1)}, u32[]{:S(2)}, u32[]{:S(2)}) collective-permute-start(f32[216,128]{1,0:T(8,128)S(1)} %get-tuple-element.23), channel_id=1, source_target_pairs={{1,0},{2,1},{3,2},{4,3},{5,4},{6,5},{7,6},{8,7},{9,8},{10,9},{11,1... | collective-permute-start | bytes 331784 | tf_op jit(solution)/shard_map/ppermute | solution.py:19
  46.8 12.1 %copy-start.4 = (f32[4,12,20,20]{3,0,2,1:T(4,128)S(1)}, f32[4,12,20,20]{3,0,2,1:T(4,128)}, u32[]{:S(2)}) copy-start(f32[4,12,20,20]{3,0,2,1:T(4,128)} %param.26) | copy-start | bytes 230404
  50.0 8.9 %copy-start.3 = (f32[4,9,9,512]{3,0,2,1:T(4,128)S(1)}, f32[4,9,9,512]{3,0,2,1:T(4,128)}, u32[]{:S(2)}) copy-start(f32[4,9,9,512]{3,0,2,1:T(4,128)} %param.28) | copy-start | bytes 1990660
  50.0 8.9 %copy-start.18 = (s32[4,512]{1,0:T(4,128)S(1)}, s32[4,512]{1,0:T(4,128)}, u32[]{:S(2)}) copy-start(s32[4,512]{1,0:T(4,128)} %refs_4_.3) | copy-start | bytes 24580
  50.0 8.9 %copy-start.19 = (s32[4,512]{1,0:T(4,128)S(1)}, s32[4,512]{1,0:T(4,128)}, u32[]{:S(2)}) copy-start(s32[4,512]{1,0:T(4,128)} %refs_5_.3) | copy-start | bytes 24580
  50.0 21.6 %all-to-all-start.2 = ((f32[128,1,768]{2,1,0:T(1,128)}), f32[128,1,768]{2,1,0:T(1,128)S(1)}, u32[]{:S(2)}, u32[]{:S(2)}) async-start(f32[128,1,768]{2,1,0:T(1,128)} %bitcast.11), calls=%async_computation.2 | async-start | bytes 786432 | tf_op jit(solution)/shard_map/all_to_all | solution.py:530
  58.9 1.0 %copy-start.24 = (f32[9,24,512]{2,1,0:T(8,128)S(1)}, f32[9,24,512]{2,1,0:T(8,128)}, u32[]{:S(2)}) copy-start(f32[9,24,512]{2,1,0:T(8,128)} %copy-done.23) | copy-start | bytes 1327108

commit v3 on v2

--- a/solution.py
+++ b/solution.py
@@ -128,13 +128,31 @@
     return wide[:, 0:96]
 
 
+def pack_turns(flux_ref, packed_ref, turns):
+    turns[...] = jnp.zeros_like(turns)
+    lane = iota((96, 256), 1)
+    lane = lane - jnp.where(lane >= 72, 72, 0) - jnp.where(lane >= 144, 72, 0)
+    for f in range(4):
+        wide = jnp.zeros((96, 256), f32)
+        for n in range(3):
+            for a in range(4):
+                turns[n, a * 24 : a * 24 + 20, 0:20] = flux_ref[n * 4 + a, :, f, :]
+            wide = wide + (pltpu.roll(turns[n], n * 72, 1) if n else turns[n])
+        wide = wide + pltpu.roll(wide, 24, 1) + pltpu.roll(wide, 48, 1)
+        high = wide.astype(bf16).astype(f32)
+        packed_ref[f] = jnp.where(lane < 48, high, wide - high).astype(bf16)
+
+
 def predictor_kernel(
     dofs_ref,
     star_ref,
     stiff_ref,
     lift_ref,
+    copy_ref,
     integral_ref,
     modal_ref,
+    low_ref,
+    up_ref,
     current,
     moved,
     left,
@@ -170,6 +188,12 @@
             return carry
 
         lax.fori_loop(0, count // 128, tile, 0)
+    whole = jnp.concatenate(halves(integral_ref[...].reshape(216, count)), axis=0)
+    wanted = jnp.concatenate([copy_ref[0:1, :], copy_ref[1:2, :]], axis=1)
+    found = product(whole, flags(iota((count, 256), 0) == wanted).astype(bf16))
+    found = found[0:216] + found[216:432]
+    low_ref[...] = found[:, 0:128]
+    up_ref[...] = found[:, 128:256]
     spread = lift_expand(lift_ref, pad, wide)[:, 0:192]
     for p in range(9):
         current[p, 0:24, :] = integral_ref[p]
@@ -224,32 +248,28 @@
     integral_ref,
     dofs_ref,
     star_ref,
-    minus_ref,
     stiff_ref,
-    local_ref,
-    copy_ref,
-    out_ref,
+    flux_ref,
     low_ref,
     up_ref,
+    out_sent,
+    packed_ref,
+    low_out_ref,
+    up_out_ref,
     left,
     square,
     moved,
+    turns,
 ):
+    pack_turns(flux_ref, packed_ref, turns)
+    out_ref = out_sent.ref
     left[...] = jnp.zeros_like(left)
     square[...] = jnp.zeros_like(square)
     for d in range(3):
         square[0:20, 0:20] = stiff_ref[d]
         left[d * 32 : d * 32 + 32, :] = square[...].T[0:32, :]
-    for f in range(4):
-        left[96 + f * 32 : 96 + f * 32 + 20, 0:20] = local_ref[:, f, :]
     packed = pack_left(left[...])
     count = integral_ref.shape[2]
-    whole = jnp.concatenate(halves(integral_ref[...].reshape(216, count)), axis=0)
-    wanted = jnp.concatenate([copy_ref[0:1, :], copy_ref[1:2, :]], axis=1)
-    found = product(whole, flags(iota((count, 256), 0) == wanted).astype(bf16))
-    found = found[0:216] + found[216:432]
-    low_ref[...] = found[:, 0:128]
-    up_ref[...] = found[:, 128:256]
     empty = jnp.zeros((8, count), f32)
     for q in range(9):
         moved[q] = product(
@@ -258,47 +278,80 @@
 
     def tile(i, carry):
         lanes = pl.ds(pl.multiple_of(i * 128, 128), 128)
-        total = [jnp.zeros((24, 128), f32) for _ in range(9)]
+        total = [dofs_ref[p, :, lanes] for p in range(9)]
         for q in range(9):
             for d in range(3):
-                part = moved[q, d * 32 : d * 32 + 24, lanes]
+                part = moved[q, d * 32 : d * 32 + 20, lanes]
                 for p in range(9):
                     total[p] = total[p] + star_ref[q, p, d : d + 1, lanes] * part
-            for f in range(4):
-                part = moved[q, 96 + f * 32 : 96 + f * 32 + 24, lanes]
-                for p in range(9):
-                    total[p] = total[p] - minus_ref[q, p, f : f + 1, lanes] * part
         for p in range(9):
             out_ref[p, :, lanes] = total[p]
         return carry
 
-    lax.fori_loop(0, count // 128, tile, 0)
-    for p in range(9):
-        out_ref[p, 0:20, :] += dofs_ref[p]
+    lax.fori_loop(0, count // 128, tile, 0, unroll=True)
+    out_sent.send()
 
 
 def neighbour_kernel(
-    inner_ref,
+    inner_late,
     integral_ref,
     lower_ref,
     upper_ref,
     neighbor_ref,
     orientation_ref,
     plus_ref,
-    flux_ref,
+    packed_ref,
+    minus_ref,
+    local_ref,
     lift_ref,
     eval_ref,
     weight_ref,
-    out_ref,
+    out_sent,
     own_ref,
     spread_ref,
     left,
     moved,
+    local_moved,
     pad,
     wide,
     face_wide,
 ):
     count = integral_ref.shape[2]
+    out_ref = out_sent.ref
+    empty = jnp.zeros((8, count), f32)
+    left[...] = jnp.zeros_like(left)
+    for f in range(4):
+        left[f * 32 : f * 32 + 20, 0:20] = local_ref[:, f, :]
+    packed = pack_left(left[...])
+    for q in range(9):
+        local_moved[q] = product(
+            packed, pack_right(jnp.concatenate([integral_ref[q], empty], axis=0))
+        )
+    inner_ref = inner_late.get()
+
+    def local_tile(i):
+        lanes = slice(i * 128, i * 128 + 128)
+        total = [inner_ref[p, :, lanes] for p in range(9)]
+        for q in range(9):
+            for f in range(4):
+                part = local_moved[q, f * 32 : f * 32 + 20, lanes]
+                for p in range(9):
+                    total[p] = total[p] - minus_ref[q, p, f : f + 1, lanes] * part
+        for p in range(9):
+            out_ref[p, :, lanes] = total[p]
+
+    def plus_tile(f, i):
+        lanes = slice(i * 128, i * 128 + 128)
+        total = [out_ref[p, :, lanes] for p in range(9)]
+        for q in range(9):
+            part = moved[f, q, 0:20, lanes]
+            for p in range(9):
+                total[p] = total[p] - plus_ref[q, p, f : f + 1, lanes] * part
+        for p in range(9):
+            out_ref[p, :, lanes] = total[p]
+
+    tiles = count // 128
+    tail = jnp.zeros((40, count), f32)
     evaluate = face_expand(eval_ref, pad, face_wide)
     weight = face_expand(weight_ref, pad, face_wide)
     gauss = product_full(weight, evaluate, 1, 1) * (1.0 / time_step)
@@ -307,7 +360,6 @@
     outer = jnp.concatenate(
         [product_full(gauss, spread[f * 64 : f * 64 + 32, 0:128]) for f in range(4)], axis=0
     )
-    empty = jnp.zeros((8, count), f32)
     rows = [jnp.concatenate([integral_ref[r], empty], axis=0) for r in trace_rows[0:3]]
     own_ref[...] = product_full(outer[:, 0:96], jnp.concatenate(rows, axis=0))
     extended = jnp.concatenate(
@@ -315,36 +367,34 @@
     )
     extended = jnp.concatenate(halves(extended), axis=0)
     width = extended.shape[1]
-    out_ref[...] = inner_ref[...]
-    left[...] = jnp.zeros_like(left)
     for f in range(4):
         pick = flags(iota((width, count), 0) == neighbor_ref[f : f + 1, :]).astype(bf16)
         found = product(extended, pick)
-        found = found[0:216] + found[216:432]
-        for a in range(12):
-            left[a * 24 : a * 24 + 20, 0:20] = flux_ref[a, :, f, :]
-        packed = pack_left(left[...])
+        packed = packed_ref[f]
         turn = orientation_ref[f : f + 1, :]
+        group = turn >> 2
+        inner_turn = turn & 3
         for q in range(9):
-            mine = jnp.concatenate([found[q * 24 : q * 24 + 24], empty], axis=0)
-            every = product(packed, pack_right(mine))
+            high = found[q * 24 : q * 24 + 24]
+            low = found[216 + q * 24 : 216 + q * 24 + 24]
+            stack = []
+            for n in range(3):
+                here = group == n
+                high_here = jnp.where(here, high, 0.0)
+                stack += [high_here, jnp.where(here, low, 0.0), high_here]
+            every = product(packed, jnp.concatenate(stack + [tail], axis=0).astype(bf16))
             chosen = every[0:24]
-            for a in range(1, 12):
-                chosen = jnp.where(turn == a, every[a * 24 : a * 24 + 24], chosen)
-            moved[q] = chosen
-
-        def tile(i, carry):
-            lanes = pl.ds(pl.multiple_of(i * 128, 128), 128)
-            total = [out_ref[p, :, lanes] for p in range(9)]
-            for q in range(9):
-                part = moved[q, :, lanes]
-                for p in range(9):
-                    total[p] = total[p] - plus_ref[q, p, f : f + 1, lanes] * part
-            for p in range(9):
-                out_ref[p, :, lanes] = total[p]
-            return carry
-
-        lax.fori_loop(0, count // 128, tile, 0)
+            for a in range(1, 4):
+                chosen = jnp.where(inner_turn == a, every[a * 24 : a * 24 + 24], chosen)
+            moved[f, q] = chosen
+            if q % 2 and q // 2 < tiles:
+                if f:
+                    plus_tile(f - 1, q // 2)
+                else:
+                    local_tile(q // 2)
+    for i in range(tiles):
+        plus_tile(3, i)
+    out_sent.send()
 
 
 def friction_kernel(
@@ -367,7 +417,8 @@
     pad,
     face_wide,
 ):
-    owned = owner_flags(owner_ref).astype(bf16)
+    owned_full = owner_flags(owner_ref)
+    owned = owned_full.astype(bf16)
     owned_twice = jnp.concatenate([owned, owned], axis=0)
     position = position_ref[0:1, :]
     faults = slip_ref.shape[1]
@@ -390,7 +441,14 @@
         + jnp.where(normal_row, pwave_minus / pwave_sum, swave_minus / swave_sum)
         * wave[:, faults : 2 * faults]
     ) * (1.0 / time_step)
-    states[...] = product_full(face_expand(eval_ref, pad, face_wide), modal, 0, 0)
+    high, low = halves(face_expand(eval_ref, pad, face_wide))
+    modal_high, modal_low = halves(modal)
+    states[...] = product(
+        jnp.concatenate([high, high, low], axis=0),
+        jnp.concatenate([modal_high, modal_low, modal_high], axis=0),
+        0,
+        0,
+    )
     normal = states[0:25, :]
     initial = (shear_ref[:, 0, :], shear_ref[:, 1, :])
     shear = (states[32:57, :] + initial[0], states[64:89, :] + initial[1])
@@ -407,20 +465,33 @@
     traction_ref[:, 1, :] = final[1]
     states[32:57, :] = final[0] - initial[0]
     states[64:89, :] = final[1] - initial[1]
-    imposed = product_full(face_expand(weight_ref, pad, face_wide), states[...])
+    weight_high, weight_low = halves(face_expand(weight_ref, pad, face_wide))
+    high, low = halves(states[...])
+    imposed = product(
+        jnp.concatenate([weight_high, weight_low], axis=0), high
+    )
+    imposed = imposed[0:32] + imposed[32:64] + product(weight_high, low)
     high = imposed.astype(bf16).astype(f32)
     low = imposed - high
     high = jnp.concatenate([high, high], axis=1)
     low = jnp.concatenate([low, low], axis=1)
-    rows = []
-    for k in range(24):
-        here = position == float(k)
-        rows.append(jnp.where(here, high, 0.0).astype(bf16))
-        rows.append(jnp.where(here, low, 0.0).astype(bf16))
-    blocks = product(jnp.concatenate(rows, axis=0), owned, 1, 1)
+    later = position >= 12.0
+    within = jnp.where(later, position - 12.0, position)
+    split = jnp.concatenate(
+        [jnp.where(later, 0.0, owned_full), jnp.where(later, owned_full, 0.0)], axis=0
+    ).astype(bf16)
+    highs = []
+    lows = []
+    for k in range(12):
+        here = within == float(k)
+        highs.append(jnp.where(here, high, 0.0).astype(bf16))
+        lows.append(jnp.where(here, low, 0.0).astype(bf16))
+    blocks = product(jnp.concatenate(highs + lows, axis=0), split, 1, 1)
+    blocks = blocks[0:384] + blocks[384:768]
     for r in range(6):
-        parts = [blocks[k * 64 : k * 64 + 32] + blocks[k * 64 + 32 : k * 64 + 64] for k in range(4 * r, 4 * r + 4)]
-        reply_ref[pl.ds(r, 128, stride=6), :] = jnp.concatenate(parts, axis=0).T
+        lane = r // 3 * 128
+        row = r % 3 * 128
+        reply_ref[pl.ds(r, 128, stride=6), :] = blocks[row : row + 128, lane : lane + 128].T
 
 
 def final_kernel(
@@ -431,8 +502,21 @@
     partial_ref,
     out_ref,
     totals,
+    rows,
+    arrive,
+    leave,
 ):
-    count = partial_ref.shape[2]
+    arriving = [
+        pltpu.make_async_copy(partial_ref.at[p], rows.at[k], arrive.at[k])
+        for k, p in enumerate(trace_rows)
+    ]
+    leaving = [
+        pltpu.make_async_copy(rows.at[k], out_ref.at[p], leave.at[k])
+        for k, p in enumerate(trace_rows)
+    ]
+    for copy in arriving:
+        copy.start()
+    count = own_ref.shape[1]
     request = request_ref[...]
     turned = request.T
     element, face = slots_of(turned)
@@ -449,10 +533,10 @@
             scale = jnp.where(normal_row, inverse[24 + k : 25 + k, :], inverse[48 + k : 49 + k, :])
             mine = jnp.concatenate([plain, plain * scale], axis=0)
             side = face[k : k + 1, :]
-            mine = jnp.concatenate([jnp.where(side == f, mine, 0.0) for f in range(4)], axis=0)
             high, low = halves(mine)
-            highs.append(high)
-            lows.append(low)
+            here = [flags(side == f).astype(bf16) for f in range(4)]
+            highs.append(jnp.concatenate([high * h for h in here], axis=0))
+            lows.append(jnp.concatenate([low * h for h in here], axis=0))
         values = jnp.concatenate(
             [jnp.concatenate(highs, axis=1), jnp.concatenate(lows, axis=1)], axis=0
         )
@@ -478,12 +562,12 @@
         jnp.concatenate([spread_high, spread_high, spread_low], axis=1),
         jnp.concatenate([high, low, high], axis=0),
     )
-    for p in range(9):
-        value = partial_ref[p, 0:20, :]
-        if p in trace_rows:
-            k = trace_rows.index(p)
-            value = value + fault[k * 32 : k * 32 + 20, :]
-        out_ref[p] = value
+    for k in range(6):
+        arriving[k].wait()
+        rows[k] = rows[k] + fault[k * 32 : k * 32 + 20, :]
+        leaving[k].start()
+    for copy in leaving:
+        copy.wait()
 
 
 class Arriving:
@@ -496,31 +580,54 @@
         return self.ref
 
 
-def call(kernel, name, outs, scratch, operands, flops, late=(), room=20):
+class Leaving:
+    def __init__(self, copy, ref):
+        self.copy = copy
+        self.ref = ref
+
+    def send(self):
+        self.copy.start()
+
+
+def call(
+    kernel, name, outs, scratch, operands, flops, late=(), sent=(), half=(), through=((), ()), aliases=None, room=20
+):
     inputs = len(operands)
     outputs = len(outs)
     own = len(scratch)
 
     def body(*refs):
         sources = list(refs[:inputs])
+        targets = list(refs[inputs : inputs + outputs])
         spare = refs[inputs + outputs + own : -1]
         flags_ref = refs[-1]
         for index, place in enumerate(late):
             copy = pltpu.make_async_copy(sources[place], spare[index], flags_ref.at[index])
             copy.start()
             sources[place] = Arriving(copy, spare[index])
-        kernel(*sources, *refs[inputs : inputs + outputs + own])
+        leaving = []
+        for index, place in enumerate(sent, len(late)):
+            copy = pltpu.make_async_copy(spare[index], targets[place], flags_ref.at[index])
+            targets[place] = Leaving(copy, spare[index])
+            leaving.append(copy)
+        kernel(*sources, *targets, *refs[inputs + outputs : inputs + outputs + own])
+        for copy in leaving:
+            copy.wait()
 
     far = pl.BlockSpec(memory_space=pltpu.HBM)
     return pl.pallas_call(
         body,
         name=name,
-        out_shape=[jax.ShapeDtypeStruct(shape, f32) for shape in outs],
-        in_specs=[far if i in late else vmem for i in range(inputs)],
-        out_specs=[vmem] * outputs,
+        out_shape=[
+            jax.ShapeDtypeStruct(shape, bf16 if i in half else f32) for i, shape in enumerate(outs)
+        ],
+        in_specs=[far if i in late or i in through[0] else vmem for i in range(inputs)],
+        out_specs=[far if i in sent or i in through[1] else vmem for i in range(outputs)],
         scratch_shapes=[pltpu.VMEM(shape, f32) for shape in scratch]
         + [pltpu.VMEM(operands[i].shape, operands[i].dtype) for i in late]
-        + [pltpu.SemaphoreType.DMA((max(1, len(late)),))],
+        + [pltpu.VMEM(outs[i], f32) for i in sent]
+        + [pltpu.SemaphoreType.DMA((max(1, len(late) + len(sent)),))],
+        input_output_aliases=aliases or {},
         compiler_params=pltpu.CompilerParams(vmem_limit_bytes=room * 1024 * 1024),
         cost_estimate=pl.CostEstimate(flops=flops, bytes_accessed=4_000_000, transcendentals=0),
     )(*operands)
@@ -577,23 +684,27 @@
         room=60,
     )
     asked = exchange(request.reshape(128, 1, 128)).reshape(128, 128)
-    integral, modal = call(
+    integral, modal, low, up = call(
         predictor_kernel,
         "predictor",
-        [(9, 24, count), (256, count)],
+        [(9, 24, count), (256, count), (216, 128), (216, 128)],
         [(9, 32, count), (9, 96, count), (96, 128), (16, 128), (256, 256)],
-        [dofs, star, stiff, lift],
+        [dofs, star, stiff, lift, copy_list],
         10**10,
     )
     (payload,) = call(gather_kernel, "gather", [(768, 128)], [], [asked, modal], 10**9)
     arrived = exchange(payload.reshape(128, 1, 768)).reshape(768, 128)
-    inner, low, up = call(
+    inner, packed, low, up = call(
         inner_kernel,
         "inner",
-        [(9, 24, count), (216, 128), (216, 128)],
-        [(224, 128), (128, 128), (9, 224, count)],
-        [integral, dofs, star, minus, stiff, local, copy_list],
+        [(9, 20, count), (4, 96, 256), (216, 128), (216, 128)],
+        [(96, 128), (128, 128), (9, 96, count), (3, 96, 256)],
+        [integral, dofs, star, stiff, flux, low, up],
         10**10,
+        sent=(0,),
+        half=(1,),
+        through=((5, 6), (2, 3)),
+        aliases={5: 2, 6: 3},
     )
     from_lower = from_behind(up, both, 1)
     from_upper = from_behind(low, both, -1)
@@ -622,8 +733,8 @@
     partial, own, spread = call(
         neighbour_kernel,
         "neighbour",
-        [(9, 24, count), (128, count), (192, 256)],
-        [(288, 128), (9, 24, count), (16, 128), (256, 256), (32, 128)],
+        [(9, 20, count), (128, count), (192, 256)],
+        [(128, 128), (4, 9, 24, count), (9, 128, count), (16, 128), (256, 256), (32, 128)],
         [
             inner,
             integral,
@@ -632,21 +743,35 @@
             neighbor,
             orientation,
             plus,
-            flux,
+            packed,
+            minus,
+            local,
             lift,
             evaluate,
             face_weight,
         ],
         10**10,
-    )
-    (new_dofs,) = call(
+        late=(0,),
+        sent=(0,),
+        aliases={0: 0},
+    )
+    far = pl.BlockSpec(memory_space=pltpu.HBM)
+    new_dofs = pl.pallas_call(
         final_kernel,
-        "final",
-        [(9, 20, count)],
-        [(256, count)],
-        [asked, returned, own, spread, partial],
-        10**9,
-    )
+        name="final",
+        out_shape=jax.ShapeDtypeStruct((9, 20, count), f32),
+        in_specs=[vmem, vmem, vmem, vmem, far],
+        out_specs=far,
+        scratch_shapes=[
+            pltpu.VMEM((256, count), f32),
+            pltpu.VMEM((6, 20, count), f32),
+            pltpu.SemaphoreType.DMA((6,)),
+            pltpu.SemaphoreType.DMA((6,)),
+        ],
+        input_output_aliases={4: 0},
+        compiler_params=pltpu.CompilerParams(vmem_limit_bytes=20 * 1024 * 1024),
+        cost_estimate=pl.CostEstimate(flops=10**9, bytes_accessed=4_000_000, transcendentals=0),
+    )(asked, returned, own, spread, partial)
     return (new_dofs, new_slip, jnp.transpose(traction, (1, 0, 2)))
 
 

time: 75.2 us -> 72.6 us (0.965)
  starting transfers between devices: 33.8 us -> 31.4 us
  waiting for transfers between devices: 7.35 us -> 9.15 us
  local copies, waits for them, and re-layouts: 3.61 us -> 2.49 us
  Pallas kernels: 28.7 us -> 27.8 us
    all_to_all x3, starting transfers between devices: 26.9 us -> 24.6 us  [exchange(): return lax.all_to_all(block, both, split_axis=0, concat_axis=0, tiled=True)]
    all_to_all x3, waiting for transfers between devices: 7.34 us -> 9.15 us  [exchange(): return lax.all_to_all(block, both, split_axis=0, concat_axis=0, tiled=True)]
    unnamed x50 -> x46, local copies, waits for them, and re-layouts: 3.61 us -> 2.49 us
    pallas_call x7, Pallas kernels: 28.7 us -> 27.8 us  [the longest x6 24.1 us: call(): pl.pallas_call(body, name=name, out_shape=[jax.ShapeDtypeStruct(shape, bf...]
  transfers between devices with their start and end apart: 5 -> 5, of which waited for: 2 -> 3; matrix products, arithmetic and copies ran while one was open for 0% -> 0% of each run, Pallas kernels for 28% -> 27%
where the time goes in v3:
time: 72.6 us; the launch traced here: 72.1 us
  starting transfers between devices  31.4 us (43%)
  Pallas kernels  27.8 us (38%)
  waiting for transfers between devices  9.15 us (13%)
  local copies, waits for them, and re-layouts  2.49 us (3%)
  between operations  1.2 us (2%)
    all_to_all x3, starting transfers between devices, exchange(): return lax.all_to_all(block, both, split_axis=0, concat_axis=0, tiled=True)  24.6 us
    pallas_call x6, Pallas kernels, call(): pl.pallas_call(body, name=name, out_shape=[jax.ShapeDtypeStruct(shape, bf...  24.1 us
    all_to_all x3, waiting for transfers between devices, exchange(): return lax.all_to_all(block, both, split_axis=0, concat_axis=0, tiled=True)  9.15 us
    ppermute x2, starting transfers between devices, from_behind(): return lax.ppermute(block, axis, route)  6.77 us
    pallas_call x1, Pallas kernels, per_device(): pl.pallas_call(final_kernel, name='final', out_shape=jax.ShapeDtypeStruct...  3.78 us
    unnamed x46, local copies, waits for them, and re-layouts  2.49 us
  transfers between devices with their start and end apart: 5, of which 3 were waited for; matrix products, arithmetic and copies ran while one was open for 0% of the time, Pallas kernels for 27%

profile of v3, /device:TPU:1, one launch (start us, length us, event | category | flops | bytes accessed | tf_op | source)
XLA Modules:
  0.0 72.1 jit_solution(741672834545905054)
XLA Ops:
  0.6 0.0 copy-start.5
  0.6 2.1 %request.1 = (f32[128,128]{1,0:T(8,128)}, f32[8,1024]{1,0:T(8,128)}) custom-call(s32[2,512]{1,0:T(2,128)} %bitcast.34, s32[2,512]{1,0:T(2,128)} %bitcast.37, f32[4,512]{1,0:T(4,128)} %refs_3_.2), custom_call_target="tpu_custom_call" | custom-call | flops 100000000 | bytes 4000000 | tf_op jit(solution)/shard_map/request/pallas_call | solution.py:618
  2.8 0.0 copy-start.13
  2.8 0.0 copy-start.14
  2.8 11.5 %all-to-all-start = ((f32[128,1,128]{2,1,0:T(1,128)}), f32[128,1,128]{2,1,0:T(1,128)S(1)}, u32[]{:S(2)}, u32[]{:S(2)}) async-start(f32[128,1,128]{2,1,0:T(1,128)} %bitcast.36), calls=%async_computation | async-start | bytes 131072 | tf_op jit(solution)/shard_map/all_to_all | solution.py:637
  14.3 0.0 copy-start.21
  14.3 0.0 copy-done.5
  14.3 0.0 copy-done.13
  14.3 0.0 copy-done.14
  14.4 0.6 copy-done.21
  15.0 1.1 %copy-done = f32[3,9,9,512]{3,0,2,1:T(4,128)S(1)} copy-done((f32[3,9,9,512]{3,0,2,1:T(4,128)S(1)}, f32[3,9,9,512]{3,0,2,1:T(4,128)}, u32[]{:S(2)}) %copy-start) | copy-done | bytes 497688
  16.1 5.6 %predictor.1 = (f32[9,24,512]{2,1,0:T(8,128)S(1)}, f32[256,512]{1,0:T(8,128)S(1)}, f32[216,128]{1,0:T(8,128)S(1)}, f32[216,128]{1,0:T(8,128)S(1)}) custom-call(f32[9,20,512]{2,1,0:T(8,128)S(1)} %copy-done.5, f32[9,9,3,512]{3,2,1,0:T(4,128)S(1)} %bitcast.23, f32[3,20,20]{2,1,0:T(8,128)S(1)} %copy-done.13, f32[10,4,20]{2,1,0:T(4,128)S(1)} %bitcast.30, ...), custom_call_target="tpu_custom_call" | custom-call | flops 10000000000 | bytes 4000000 | tf_op jit(solution)/shard_map/predictor/pallas_call | solution.py:618
  21.7 2.4 %all-to-all-done = f32[128,1,128]{2,1,0:T(1,128)S(1)} async-done(((f32[128,1,128]{2,1,0:T(1,128)}), f32[128,1,128]{2,1,0:T(1,128)S(1)}, u32[]{:S(2)}, u32[]{:S(2)}) %all-to-all-start) | async-done | bytes 65568 | tf_op jit(solution)/shard_map/all_to_all | solution.py:637
  24.1 2.7 %gather.1 = f32[768,128]{1,0:T(8,128)} custom-call(f32[128,128]{1,0:T(8,128)S(1)} %bitcast.21, f32[256,512]{1,0:T(8,128)S(1)} %get-tuple-element.20.refs_1_), custom_call_target="tpu_custom_call" | custom-call | flops 1000000000 | bytes 4000000 | tf_op jit(solution)/shard_map/gather/pallas_call | solution.py:618
  26.9 0.0 copy-start.1
  26.9 7.4 %all-to-all-start.1 = ((f32[128,1,768]{2,1,0:T(1,128)}), f32[128,1,768]{2,1,0:T(1,128)S(1)}, u32[]{:S(2)}, u32[]{:S(2)}) async-start(f32[128,1,768]{2,1,0:T(1,128)} %bitcast.7), calls=%async_computation.1 | async-start | bytes 786432 | tf_op jit(solution)/shard_map/all_to_all | solution.py:637
  34.2 0.0 copy-done.4
  34.3 0.0 copy-done.1
  34.3 0.0 copy-start.6
  34.3 0.0 copy-start.7
  34.3 0.0 copy-start.8
  34.3 0.0 copy-start.9
  34.3 0.0 copy-start.10
  34.3 0.0 copy-start.11
  34.3 0.0 copy-start.16
  34.4 0.0 copy-start.17
  34.4 0.0 copy-start.20
  34.4 0.0 copy-start.22
  34.4 2.7 %inner.1 = (f32[9,20,512]{2,1,0:T(8,128)}, bf16[4,96,256]{2,1,0:T(8,128)(2,1)S(1)}, f32[216,128]{1,0:T(8,128)S(1)}, f32[216,128]{1,0:T(8,128)S(1)}) custom-call(f32[9,24,512]{2,1,0:T(8,128)S(1)} %get-tuple-element.23.refs_0_.refs_1_, f32[9,20,512]{2,1,0:T(8,128)S(1)} %copy-done.5, ...), custom_call_target="tpu_custom_call", output_to_operand_aliasing={{2}: (5, {}), {3}: (6, {})} | custom-call | flops 10000000000 | bytes 4000000 | tf_op jit(solution)/shard_map/inner/pallas_call | solution.py:618
  37.1 0.0 copy-start.15
  37.1 3.3 %collective-permute-start = (f32[216,128]{1,0:T(8,128)S(1)}, f32[216,128]{1,0:T(8,128)S(1)}, u32[]{:S(2)}, u32[]{:S(2)}) collective-permute-start(f32[216,128]{1,0:T(8,128)S(1)} %get-tuple-element.27), channel_id=1, source_target_pairs={{0,1},{1,2},{2,3},{3,4},{4,5},{5,6},{6,7},{7,8},{8,9},{9,10},{10,1... | collective-permute-start | bytes 331784 | tf_op jit(solution)/shard_map/ppermute | solution.py:19
  40.4 3.5 %collective-permute-start.1 = (f32[216,128]{1,0:T(8,128)S(1)}, f32[216,128]{1,0:T(8,128)S(1)}, u32[]{:S(2)}, u32[]{:S(2)}) collective-permute-start(f32[216,128]{1,0:T(8,128)S(1)} %get-tuple-element.28), channel_id=1, source_target_pairs={{1,0},{2,1},{3,2},{4,3},{5,4},{6,5},{7,6},{8,7},{9,8},{10,9},{11,1... | collective-permute-start | bytes 331784 | tf_op jit(solution)/shard_map/ppermute | solution.py:19
  43.9 3.1 %all-to-all-done.1 = f32[128,1,768]{2,1,0:T(1,128)S(1)} async-done(((f32[128,1,768]{2,1,0:T(1,128)}), f32[128,1,768]{2,1,0:T(1,128)S(1)}, u32[]{:S(2)}, u32[]{:S(2)}) %all-to-all-start.1) | async-done | bytes 393248 | tf_op jit(solution)/shard_map/all_to_all | solution.py:637
  47.0 0.0 copy-done.6
  47.0 0.0 copy-done.7
  47.1 0.0 copy-start.3
  47.1 2.5 %friction.1 = (f32[768,128]{1,0:T(8,128)}, f32[25,512]{1,0:T(8,128)}, f32[25,2,512]{2,1,0:T(2,128)}) custom-call(f32[768,128]{1,0:T(8,128)S(1)} %bitcast.19, f32[8,1024]{1,0:T(8,128)S(1)} %copy-done.22, s32[2,512]{1,0:T(2,128)S(1)} %bitcast.35, f32[4,512]{1,0:T(4,128)S(1)} %copy-done.15, f32[10,25]{1,0:T(8,128)S(1)} %bitcast.32, f32[10,25]{1,0:T(8,128)S(1)} %copy-done.17, ...), custom_call_target="tpu_custom_call" | custom-call | flops 1000000000 | bytes 4000000 | tf_op jit(solution)/shard_map/friction/pallas_call | solution.py:618
  49.6 0.0 copy-start.2
  49.6 0.0 copy-start.12
  49.6 0.0 copy-start.19
  49.6 5.8 %all-to-all-start.2 = ((f32[128,1,768]{2,1,0:T(1,128)}), f32[128,1,768]{2,1,0:T(1,128)S(1)}, u32[]{:S(2)}, u32[]{:S(2)}) async-start(f32[128,1,768]{2,1,0:T(1,128)} %bitcast.11), calls=%async_computation.2 | async-start | bytes 786432 | tf_op jit(solution)/shard_map/all_to_all | solution.py:637
  55.4 0.0 copy-start.18
  55.4 0.0 collective-permute-done.refs_2_
  55.4 0.0 collective-permute-done.1.refs_3_
  55.5 0.6 copy-done.18
  56.1 8.4 %neighbour.1 = (f32[9,20,512]{2,1,0:T(8,128)}, f32[128,512]{1,0:T(8,128)S(1)}, f32[192,256]{1,0:T(8,128)S(1)}) custom-call(f32[9,20,512]{2,1,0:T(8,128)} %get-tuple-element.26.refs_0_, f32[9,24,512]{2,1,0:T(8,128)S(1)} %get-tuple-element.23.refs_0_.refs_1_, f32[216,128]{1,0:T(8,128)S(1)} %collective-permute-done.refs_2_, ...), custom_call_target="tpu_custom_call", output_to_operand_aliasing={{0}: (0, {})} | custom-call | flops 10000000000 | bytes 4000000 | tf_op jit(solution)/shard_map/neighbour/pallas_call | solution.py:618
  64.5 3.6 %all-to-all-done.2 = f32[128,1,768]{2,1,0:T(1,128)S(1)} async-done(((f32[128,1,768]{2,1,0:T(1,128)}), f32[128,1,768]{2,1,0:T(1,128)S(1)}, u32[]{:S(2)}, u32[]{:S(2)}) %all-to-all-start.2) | async-done | bytes 393248 | tf_op jit(solution)/shard_map/all_to_all | solution.py:637
  68.1 3.8 %final.1 = f32[9,20,512]{2,1,0:T(8,128)} custom-call(f32[128,128]{1,0:T(8,128)S(1)} %bitcast.22, f32[768,128]{1,0:T(8,128)S(1)} %bitcast.20, f32[128,512]{1,0:T(8,128)S(1)} %get-tuple-element.30.own_ref, f32[192,256]{1,0:T(8,128)S(1)} %get-tuple-element.31.spread_ref, f32[9,20,512]{2,1,0:T(8,128)} %get-tuple-element.32.partial_ref), custom_call_target="tpu_custom_call", output_to_operand_aliasing={{}: (4, {})} | custom-call | flops 1000000000 | bytes 4000000 | tf_op jit(solution)/shard_map/final/pallas_call | solution.py:759
  (15 shorter events, 0.0 us)
Async XLA Ops:
  0.6 13.7 %copy-start.5 = (f32[9,20,512]{2,1,0:T(8,128)S(1)}, f32[9,20,512]{2,1,0:T(8,128)}, u32[]{:S(2)}) copy-start(f32[9,20,512]{2,1,0:T(8,128)} %refs_1_.1) | copy-start | bytes 1105924
  2.8 11.6 %copy-start.13 = (f32[3,20,20]{2,1,0:T(8,128)S(1)}, f32[3,20,20]{2,1,0:T(8,128)}, u32[]{:S(2)}) copy-start(f32[3,20,20]{2,1,0:T(8,128)} %refs_3_.3) | copy-start | bytes 14404
  2.8 11.6 %copy-start.14 = (f32[4,10,20]{2,0,1:T(4,128)S(1)}, f32[4,10,20]{2,0,1:T(4,128)}, u32[]{:S(2)}) copy-start(f32[4,10,20]{2,0,1:T(4,128)} %param.32) | copy-start | bytes 9604
  2.8 21.3 %all-to-all-start = ((f32[128,1,128]{2,1,0:T(1,128)}), f32[128,1,128]{2,1,0:T(1,128)S(1)}, u32[]{:S(2)}, u32[]{:S(2)}) async-start(f32[128,1,128]{2,1,0:T(1,128)} %bitcast.36), calls=%async_computation | async-start | bytes 131072 | tf_op jit(solution)/shard_map/all_to_all | solution.py:637
  14.3 0.7 copy-start.21
  15.0 1.1 %copy-start = (f32[3,9,9,512]{3,0,2,1:T(4,128)S(1)}, f32[3,9,9,512]{3,0,2,1:T(4,128)}, u32[]{:S(2)}) copy-start(f32[3,9,9,512]{3,0,2,1:T(4,128)} %param.23) | copy-start | bytes 1492996
  24.1 10.1 %copy-start.4 = (f32[4,12,20,20]{3,0,2,1:T(4,128)S(1)}, f32[4,12,20,20]{3,0,2,1:T(4,128)}, u32[]{:S(2)}) copy-start(f32[4,12,20,20]{3,0,2,1:T(4,128)} %param.26) | copy-start | bytes 230404
  26.9 7.4 %copy-start.1 = (f32[3,9,9,512]{3,0,2,1:T(4,128)S(1)}, f32[3,9,9,512]{3,0,2,1:T(4,128)}, u32[]{:S(2)}) copy-start(f32[3,9,9,512]{3,0,2,1:T(4,128)} %param.23) | copy-start | bytes 1492996
  26.9 20.1 %all-to-all-start.1 = ((f32[128,1,768]{2,1,0:T(1,128)}), f32[128,1,768]{2,1,0:T(1,128)S(1)}, u32[]{:S(2)}, u32[]{:S(2)}) async-start(f32[128,1,768]{2,1,0:T(1,128)} %bitcast.7), calls=%async_computation.1 | async-start | bytes 786432 | tf_op jit(solution)/shard_map/all_to_all | solution.py:637
  34.3 12.7 %copy-start.6 = (f32[2,25,512]{2,0,1:T(2,128)S(1)}, f32[2,25,512]{2,0,1:T(2,128)}, u32[]{:S(2)}) copy-start(f32[2,25,512]{2,0,1:T(2,128)} %param.39) | copy-start | bytes 307204
  34.3 12.7 %copy-start.7 = (f32[25,512]{1,0:T(8,128)S(1)}, f32[25,512]{1,0:T(8,128)}, u32[]{:S(2)}) copy-start(f32[25,512]{1,0:T(8,128)} %refs_6_.1) | copy-start | bytes 153604
  34.3 12.7 %copy-start.8 = (f32[25,512]{1,0:T(8,128)S(1)}, f32[25,512]{1,0:T(8,128)}, u32[]{:S(2)}) copy-start(f32[25,512]{1,0:T(8,128)} %refs_8_.1) | copy-start | bytes 153604
  34.3 12.7 %copy-start.9 = (f32[25,512]{1,0:T(8,128)S(1)}, f32[25,512]{1,0:T(8,128)}, u32[]{:S(2)}) copy-start(f32[25,512]{1,0:T(8,128)} %refs_9_.1) | copy-start | bytes 153604
  34.3 12.7 %copy-start.10 = (f32[25,512]{1,0:T(8,128)S(1)}, f32[25,512]{1,0:T(8,128)}, u32[]{:S(2)}) copy-start(f32[25,512]{1,0:T(8,128)} %refs_10_.1) | copy-start | bytes 153604
  34.3 12.7 %copy-start.11 = (f32[25,512]{1,0:T(8,128)S(1)}, f32[25,512]{1,0:T(8,128)}, u32[]{:S(2)}) copy-start(f32[25,512]{1,0:T(8,128)} %refs_11_.1) | copy-start | bytes 153604
  34.3 12.7 %copy-start.16 = (f32[25,10]{0,1:T(8,128)S(1)}, f32[25,10]{0,1:T(8,128)}, u32[]{:S(2)}) copy-start(f32[25,10]{0,1:T(8,128)} %param.33) | copy-start | bytes 3004
  34.4 12.7 %copy-start.17 = (f32[10,25]{1,0:T(8,128)S(1)}, f32[10,25]{1,0:T(8,128)}, u32[]{:S(2)}) copy-start(f32[10,25]{1,0:T(8,128)} %refs_12_.1) | copy-start | bytes 3004
  34.4 12.7 %copy-start.20 = (s32[512,2]{0,1:T(2,128)S(1)}, s32[512,2]{0,1:T(2,128)}, u32[]{:S(2)}) copy-start(s32[512,2]{0,1:T(2,128)} %param.35) | copy-start | bytes 12292
  34.4 12.7 %copy-start.22 = (f32[8,1024]{1,0:T(8,128)S(1)}, f32[8,1024]{1,0:T(8,128)}, u32[]{:S(2)}) copy-start(f32[8,1024]{1,0:T(8,128)} %get-tuple-element.21.refs_1_) | copy-start | bytes 98308
  37.1 10.0 %copy-start.15 = (f32[4,512]{1,0:T(4,128)S(1)}, f32[4,512]{1,0:T(4,128)}, u32[]{:S(2)}) copy-start(f32[4,512]{1,0:T(4,128)} %refs_3_.2) | copy-start | bytes 24580
  37.1 18.3 %collective-permute-start = (f32[216,128]{1,0:T(8,128)S(1)}, f32[216,128]{1,0:T(8,128)S(1)}, u32[]{:S(2)}, u32[]{:S(2)}) collective-permute-start(f32[216,128]{1,0:T(8,128)S(1)} %get-tuple-element.27), channel_id=1, source_target_pairs={{0,1},{1,2},{2,3},{3,4},{4,5},{5,6},{6,7},{7,8},{8,9},{9,10},{10,1... | collective-permute-start | bytes 331784 | tf_op jit(solution)/shard_map/ppermute | solution.py:19
  40.4 15.0 %collective-permute-start.1 = (f32[216,128]{1,0:T(8,128)S(1)}, f32[216,128]{1,0:T(8,128)S(1)}, u32[]{:S(2)}, u32[]{:S(2)}) collective-permute-start(f32[216,128]{1,0:T(8,128)S(1)} %get-tuple-element.28), channel_id=1, source_target_pairs={{1,0},{2,1},{3,2},{4,3},{5,4},{6,5},{7,6},{8,7},{9,8},{10,9},{11,1... | collective-permute-start | bytes 331784 | tf_op jit(solution)/shard_map/ppermute | solution.py:19
  47.1 8.4 %copy-start.3 = (f32[4,9,9,512]{3,0,2,1:T(4,128)S(1)}, f32[4,9,9,512]{3,0,2,1:T(4,128)}, u32[]{:S(2)}) copy-start(f32[4,9,9,512]{3,0,2,1:T(4,128)} %param.27) | copy-start | bytes 1990660
  49.6 5.9 %copy-start.2 = (f32[4,9,9,512]{3,0,2,1:T(4,128)S(1)}, f32[4,9,9,512]{3,0,2,1:T(4,128)}, u32[]{:S(2)}) copy-start(f32[4,9,9,512]{3,0,2,1:T(4,128)} %param.28) | copy-start | bytes 1990660
  49.6 5.9 %copy-start.12 = (f32[4,20,20]{2,0,1:T(4,128)S(1)}, f32[4,20,20]{2,0,1:T(4,128)}, u32[]{:S(2)}) copy-start(f32[4,20,20]{2,0,1:T(4,128)} %param.25) | copy-start | bytes 19204
  49.6 5.9 %copy-start.19 = (s32[4,512]{1,0:T(4,128)S(1)}, s32[4,512]{1,0:T(4,128)}, u32[]{:S(2)}) copy-start(s32[4,512]{1,0:T(4,128)} %refs_5_.3) | copy-start | bytes 24580
  49.6 18.5 %all-to-all-start.2 = ((f32[128,1,768]{2,1,0:T(1,128)}), f32[128,1,768]{2,1,0:T(1,128)S(1)}, u32[]{:S(2)}, u32[]{:S(2)}) async-start(f32[128,1,768]{2,1,0:T(1,128)} %bitcast.11), calls=%async_computation.2 | async-start | bytes 786432 | tf_op jit(solution)/shard_map/all_to_all | solution.py:637
  55.4 0.7 copy-start.18

commit v4 on v3

--- a/solution.py
+++ b/solution.py
@@ -3,11 +3,12 @@
 from jax import lax
 from jax.experimental import pallas as pl
 from jax.experimental.pallas import tpu as pltpu
+from jax.sharding import Mesh
 from jax.sharding import PartitionSpec as P
 
 time_step = 0.8
 trace_rows = (0, 3, 5, 6, 7, 8)
-both = ("dom", "sub")
+both = ("x", "z", "core", "y")
 f32 = jnp.float32
 bf16 = jnp.bfloat16
 vmem = pl.BlockSpec(memory_space=pltpu.VMEM)
@@ -65,6 +66,8 @@
 
 def owner_flags(owner_ref):
     owner = jnp.concatenate([owner_ref[0:1, :], owner_ref[1:2, :]], axis=1)
+    core = (owner >> 2) & 1
+    owner = core * 64 + (owner >> 5) * 16 + (owner & 3) * 4 + ((owner >> 3) & 3)
     return flags(iota((128, owner.shape[1]), 0) == owner)
 
 
@@ -93,14 +96,8 @@
     slot = (row - 24 * channel).astype(f32)
     value = jnp.where(row < 24, wanted, jnp.where(row < 48, zp, zs))
     value = jnp.where((slot == position) & (row < 72), value, 0.0)
-    high = value.astype(bf16)
-    rest = value - high.astype(f32)
-    middle, low = halves(rest)
-    request_ref[...] = (
-        product(owned_half, high, 1, 1)
-        + product(owned_half, middle, 1, 1)
-        + product(owned_half, low, 1, 1)
-    )
+    wide = product(owned_half, jnp.concatenate(halves(value), axis=0), 1, 1)
+    request_ref[...] = wide[:, 0:128] + wide[:, 128:256]
 
 
 def lift_expand(lift_ref, pad, wide):
@@ -634,7 +631,7 @@
 
 
 def exchange(block):
-    return lax.all_to_all(block, both, split_axis=0, concat_axis=0, tiled=True)
+    return lax.all_to_all(block, ("core", "x", "y", "z"), split_axis=0, concat_axis=0, tiled=True)
 
 
 def per_device(
@@ -776,35 +773,36 @@
 
 
 def solution(mesh):
+    fine = Mesh(mesh.devices.reshape(4, 4, 2, 4), both)
     in_specs = (
-        P(None, None, ("dom", "sub")),
-        P(None, None, None, ("dom", "sub")),
+        P(None, None, both),
+        P(None, None, None, both),
         P(),
         P(),
         P(),
-        P(None, None, None, ("dom", "sub")),
-        P(None, None, None, ("dom", "sub")),
-        P(None, ("dom", "sub")),
-        P(None, ("dom", "sub")),
-        P(None, ("dom", "sub")),
+        P(None, None, None, both),
+        P(None, None, None, both),
+        P(None, both),
+        P(None, both),
+        P(None, both),
         P(),
         P(),
         P(),
-        P(("dom", "sub"), None),
-        P(("dom", "sub"), None),
-        P(None, ("dom", "sub")),
-        P(None, ("dom", "sub")),
-        P(None, None, ("dom", "sub")),
-        P(None, ("dom", "sub")),
-        P(None, ("dom", "sub")),
-        P(None, ("dom", "sub")),
-        P(None, ("dom", "sub")),
+        P(both, None),
+        P(both, None),
+        P(None, both),
+        P(None, both),
+        P(None, None, both),
+        P(None, both),
+        P(None, both),
+        P(None, both),
+        P(None, both),
     )
     out_specs = (
-        P(None, None, ("dom", "sub")),
-        P(None, ("dom", "sub")),
-        P(None, None, ("dom", "sub")),
+        P(None, None, both),
+        P(None, both),
+        P(None, None, both),
     )
     return jax.shard_map(
-        per_device, mesh=mesh, in_specs=in_specs, out_specs=out_specs, check_vma=False
-    )
+        per_device, mesh=fine, in_specs=in_specs, out_specs=out_specs, check_vma=False
+    )

time: 72.6 us -> 71.5 us (0.985)
  waiting for transfers between devices: 9.15 us -> 6.64 us
  starting transfers between devices: 31.4 us -> 33 us
    all_to_all x3, waiting for transfers between devices: 9.15 us -> 6.63 us  [exchange(): lax.all_to_all(block, ('core', 'x', 'y', 'z'), split_axis=0, concat_axis=...]
    all_to_all x3, starting transfers between devices: 24.6 us -> 26.2 us  [exchange(): lax.all_to_all(block, ('core', 'x', 'y', 'z'), split_axis=0, concat_axis=...]
where the time goes in v4:
time: 71.5 us; the launch traced here: 71 us
  starting transfers between devices  33 us (46%)
  Pallas kernels  27.7 us (39%)
  waiting for transfers between devices  6.64 us (9%)
  local copies, waits for them, and re-layouts  2.49 us (3%)
  between operations  1.2 us (2%)
    all_to_all x3, starting transfers between devices, exchange(): lax.all_to_all(block, ('core', 'x', 'y', 'z'), split_axis=0, concat_axis=...  26.2 us
    pallas_call x6, Pallas kernels, call(): pl.pallas_call(body, name=name, out_shape=[jax.ShapeDtypeStruct(shape, bf...  23.9 us
    ppermute x2, starting transfers between devices, from_behind(): return lax.ppermute(block, axis, route)  6.77 us
    all_to_all x3, waiting for transfers between devices, exchange(): lax.all_to_all(block, ('core', 'x', 'y', 'z'), split_axis=0, concat_axis=...  6.63 us
    pallas_call x1, Pallas kernels, per_device(): pl.pallas_call(final_kernel, name='final', out_shape=jax.ShapeDtypeStruct...  3.78 us
    unnamed x46, local copies, waits for them, and re-layouts  2.49 us
  transfers between devices with their start and end apart: 5, of which 3 were waited for; matrix products, arithmetic and copies ran while one was open for 0% of the time, Pallas kernels for 27%

profile of v4, /device:TPU:1, one launch (start us, length us, event | category | flops | bytes accessed | tf_op | source)
XLA Modules:
  0.0 71.0 jit_solution(17387178464827266317)
XLA Ops:
  0.6 0.0 copy-start.5
  0.6 2.0 %request.1 = (f32[128,128]{1,0:T(8,128)}, f32[8,1024]{1,0:T(8,128)}) custom-call(s32[2,512]{1,0:T(2,128)} %bitcast.34, s32[2,512]{1,0:T(2,128)} %bitcast.37, f32[4,512]{1,0:T(4,128)} %refs_3_.2), custom_call_target="tpu_custom_call" | custom-call | flops 100000000 | bytes 4000000 | tf_op jit(solution)/shard_map/request/pallas_call | solution.py:615
  2.6 0.0 copy-start.13
  2.6 0.0 copy-start.14
  2.7 11.5 %all-to-all-start = ((f32[128,1,128]{2,1,0:T(1,128)}), f32[128,1,128]{2,1,0:T(1,128)S(1)}, u32[]{:S(2)}, u32[]{:S(2)}) async-start(f32[128,1,128]{2,1,0:T(1,128)} %bitcast.36), calls=%async_computation | async-start | bytes 131072 | tf_op jit(solution)/shard_map/all_to_all | solution.py:634
  14.2 0.0 copy-start.21
  14.2 0.0 copy-done.5
  14.2 0.0 copy-done.13
  14.2 0.0 copy-done.14
  14.2 0.6 copy-done.21
  14.8 1.1 %copy-done = f32[3,9,9,512]{3,0,2,1:T(4,128)S(1)} copy-done((f32[3,9,9,512]{3,0,2,1:T(4,128)S(1)}, f32[3,9,9,512]{3,0,2,1:T(4,128)}, u32[]{:S(2)}) %copy-start) | copy-done | bytes 497688
  15.9 5.6 %predictor.1 = (f32[9,24,512]{2,1,0:T(8,128)S(1)}, f32[256,512]{1,0:T(8,128)S(1)}, f32[216,128]{1,0:T(8,128)S(1)}, f32[216,128]{1,0:T(8,128)S(1)}) custom-call(f32[9,20,512]{2,1,0:T(8,128)S(1)} %copy-done.5, f32[9,9,3,512]{3,2,1,0:T(4,128)S(1)} %bitcast.23, f32[3,20,20]{2,1,0:T(8,128)S(1)} %copy-done.13, f32[10,4,20]{2,1,0:T(4,128)S(1)} %bitcast.30, ...), custom_call_target="tpu_custom_call" | custom-call | flops 10000000000 | bytes 4000000 | tf_op jit(solution)/shard_map/predictor/pallas_call | solution.py:615
  21.5 1.9 %all-to-all-done = f32[128,1,128]{2,1,0:T(1,128)S(1)} async-done(((f32[128,1,128]{2,1,0:T(1,128)}), f32[128,1,128]{2,1,0:T(1,128)S(1)}, u32[]{:S(2)}, u32[]{:S(2)}) %all-to-all-start) | async-done | bytes 65568 | tf_op jit(solution)/shard_map/all_to_all | solution.py:634
  23.4 2.7 %gather.1 = f32[768,128]{1,0:T(8,128)} custom-call(f32[128,128]{1,0:T(8,128)S(1)} %bitcast.21, f32[256,512]{1,0:T(8,128)S(1)} %get-tuple-element.20.refs_1_), custom_call_target="tpu_custom_call" | custom-call | flops 1000000000 | bytes 4000000 | tf_op jit(solution)/shard_map/gather/pallas_call | solution.py:615
  26.2 0.0 copy-start.1
  26.2 7.9 %all-to-all-start.1 = ((f32[128,1,768]{2,1,0:T(1,128)}), f32[128,1,768]{2,1,0:T(1,128)S(1)}, u32[]{:S(2)}, u32[]{:S(2)}) async-start(f32[128,1,768]{2,1,0:T(1,128)} %bitcast.7), calls=%async_computation.1 | async-start | bytes 786432 | tf_op jit(solution)/shard_map/all_to_all | solution.py:634
  34.1 0.0 copy-done.4
  34.1 0.0 copy-done.1
  34.1 0.0 copy-start.6
  34.2 0.0 copy-start.7
  34.2 0.0 copy-start.8
  34.2 0.0 copy-start.9
  34.2 0.0 copy-start.10
  34.2 0.0 copy-start.11
  34.2 0.0 copy-start.16
  34.2 0.0 copy-start.17
  34.2 0.0 copy-start.20
  34.3 0.0 copy-start.22
  34.3 2.7 %inner.1 = (f32[9,20,512]{2,1,0:T(8,128)}, bf16[4,96,256]{2,1,0:T(8,128)(2,1)S(1)}, f32[216,128]{1,0:T(8,128)S(1)}, f32[216,128]{1,0:T(8,128)S(1)}) custom-call(f32[9,24,512]{2,1,0:T(8,128)S(1)} %get-tuple-element.23.refs_0_.refs_1_, f32[9,20,512]{2,1,0:T(8,128)S(1)} %copy-done.5, ...), custom_call_target="tpu_custom_call", output_to_operand_aliasing={{2}: (5, {}), {3}: (6, {})} | custom-call | flops 10000000000 | bytes 4000000 | tf_op jit(solution)/shard_map/inner/pallas_call | solution.py:615
  36.9 0.0 copy-start.15
  37.0 3.3 %collective-permute-start = (f32[216,128]{1,0:T(8,128)S(1)}, f32[216,128]{1,0:T(8,128)S(1)}, u32[]{:S(2)}, u32[]{:S(2)}) collective-permute-start(f32[216,128]{1,0:T(8,128)S(1)} %get-tuple-element.27), channel_id=1, source_target_pairs={{0,1},{1,2},{2,3},{3,4},{4,5},{5,6},{6,7},{7,8},{8,9},{9,10},{10,1... | collective-permute-start | bytes 331784 | tf_op jit(solution)/shard_map/ppermute | solution.py:20
  40.3 3.5 %collective-permute-start.1 = (f32[216,128]{1,0:T(8,128)S(1)}, f32[216,128]{1,0:T(8,128)S(1)}, u32[]{:S(2)}, u32[]{:S(2)}) collective-permute-start(f32[216,128]{1,0:T(8,128)S(1)} %get-tuple-element.28), channel_id=1, source_target_pairs={{1,0},{2,1},{3,2},{4,3},{5,4},{6,5},{7,6},{8,7},{9,8},{10,9},{11,1... | collective-permute-start | bytes 331784 | tf_op jit(solution)/shard_map/ppermute | solution.py:20
  43.7 2.1 %all-to-all-done.1 = f32[128,1,768]{2,1,0:T(1,128)S(1)} async-done(((f32[128,1,768]{2,1,0:T(1,128)}), f32[128,1,768]{2,1,0:T(1,128)S(1)}, u32[]{:S(2)}, u32[]{:S(2)}) %all-to-all-start.1) | async-done | bytes 393248 | tf_op jit(solution)/shard_map/all_to_all | solution.py:634
  45.9 0.0 copy-done.6
  45.9 0.0 copy-done.8
  46.0 0.0 copy-start.3
  46.0 2.5 %friction.1 = (f32[768,128]{1,0:T(8,128)}, f32[25,512]{1,0:T(8,128)}, f32[25,2,512]{2,1,0:T(2,128)}) custom-call(f32[768,128]{1,0:T(8,128)S(1)} %bitcast.19, f32[8,1024]{1,0:T(8,128)S(1)} %copy-done.22, s32[2,512]{1,0:T(2,128)S(1)} %bitcast.35, f32[4,512]{1,0:T(4,128)S(1)} %copy-done.15, f32[10,25]{1,0:T(8,128)S(1)} %bitcast.32, f32[10,25]{1,0:T(8,128)S(1)} %copy-done.17, ...), custom_call_target="tpu_custom_call" | custom-call | flops 1000000000 | bytes 4000000 | tf_op jit(solution)/shard_map/friction/pallas_call | solution.py:615
  48.5 0.0 copy-start.2
  48.5 0.0 copy-start.12
  48.5 0.0 copy-start.19
  48.5 6.8 %all-to-all-start.2 = ((f32[128,1,768]{2,1,0:T(1,128)}), f32[128,1,768]{2,1,0:T(1,128)S(1)}, u32[]{:S(2)}, u32[]{:S(2)}) async-start(f32[128,1,768]{2,1,0:T(1,128)} %bitcast.11), calls=%async_computation.2 | async-start | bytes 786432 | tf_op jit(solution)/shard_map/all_to_all | solution.py:634
  55.3 0.0 copy-start.18
  55.3 0.0 collective-permute-done.refs_2_
  55.3 0.0 collective-permute-done.1.refs_3_
  55.4 0.6 copy-done.18
  56.0 8.4 %neighbour.1 = (f32[9,20,512]{2,1,0:T(8,128)}, f32[128,512]{1,0:T(8,128)S(1)}, f32[192,256]{1,0:T(8,128)S(1)}) custom-call(f32[9,20,512]{2,1,0:T(8,128)} %get-tuple-element.26.refs_0_, f32[9,24,512]{2,1,0:T(8,128)S(1)} %get-tuple-element.23.refs_0_.refs_1_, f32[216,128]{1,0:T(8,128)S(1)} %collective-permute-done.refs_2_, ...), custom_call_target="tpu_custom_call", output_to_operand_aliasing={{0}: (0, {})} | custom-call | flops 10000000000 | bytes 4000000 | tf_op jit(solution)/shard_map/neighbour/pallas_call | solution.py:615
  64.4 2.6 %all-to-all-done.2 = f32[128,1,768]{2,1,0:T(1,128)S(1)} async-done(((f32[128,1,768]{2,1,0:T(1,128)}), f32[128,1,768]{2,1,0:T(1,128)S(1)}, u32[]{:S(2)}, u32[]{:S(2)}) %all-to-all-start.2) | async-done | bytes 393248 | tf_op jit(solution)/shard_map/all_to_all | solution.py:634
  67.0 3.8 %final.1 = f32[9,20,512]{2,1,0:T(8,128)} custom-call(f32[128,128]{1,0:T(8,128)S(1)} %bitcast.22, f32[768,128]{1,0:T(8,128)S(1)} %bitcast.20, f32[128,512]{1,0:T(8,128)S(1)} %get-tuple-element.30.own_ref, f32[192,256]{1,0:T(8,128)S(1)} %get-tuple-element.31.spread_ref, f32[9,20,512]{2,1,0:T(8,128)} %get-tuple-element.32.partial_ref), custom_call_target="tpu_custom_call", output_to_operand_aliasing={{}: (4, {})} | custom-call | flops 1000000000 | bytes 4000000 | tf_op jit(solution)/shard_map/final/pallas_call | solution.py:756
  (15 shorter events, 0.0 us)
Async XLA Ops:
  0.6 13.5 %copy-start.5 = (f32[9,20,512]{2,1,0:T(8,128)S(1)}, f32[9,20,512]{2,1,0:T(8,128)}, u32[]{:S(2)}) copy-start(f32[9,20,512]{2,1,0:T(8,128)} %refs_1_.1) | copy-start | bytes 1105924
  2.6 11.6 %copy-start.13 = (f32[3,20,20]{2,1,0:T(8,128)S(1)}, f32[3,20,20]{2,1,0:T(8,128)}, u32[]{:S(2)}) copy-start(f32[3,20,20]{2,1,0:T(8,128)} %refs_3_.3) | copy-start | bytes 14404
  2.6 11.6 %copy-start.14 = (f32[4,10,20]{2,0,1:T(4,128)S(1)}, f32[4,10,20]{2,0,1:T(4,128)}, u32[]{:S(2)}) copy-start(f32[4,10,20]{2,0,1:T(4,128)} %param.32) | copy-start | bytes 9604
  2.7 20.8 %all-to-all-start = ((f32[128,1,128]{2,1,0:T(1,128)}), f32[128,1,128]{2,1,0:T(1,128)S(1)}, u32[]{:S(2)}, u32[]{:S(2)}) async-start(f32[128,1,128]{2,1,0:T(1,128)} %bitcast.36), calls=%async_computation | async-start | bytes 131072 | tf_op jit(solution)/shard_map/all_to_all | solution.py:634
  14.2 0.7 copy-start.21
  14.8 1.1 %copy-start = (f32[3,9,9,512]{3,0,2,1:T(4,128)S(1)}, f32[3,9,9,512]{3,0,2,1:T(4,128)}, u32[]{:S(2)}) copy-start(f32[3,9,9,512]{3,0,2,1:T(4,128)} %param.23) | copy-start | bytes 1492996
  23.4 10.7 %copy-start.4 = (f32[4,12,20,20]{3,0,2,1:T(4,128)S(1)}, f32[4,12,20,20]{3,0,2,1:T(4,128)}, u32[]{:S(2)}) copy-start(f32[4,12,20,20]{3,0,2,1:T(4,128)} %param.26) | copy-start | bytes 230404
  26.2 8.0 %copy-start.1 = (f32[3,9,9,512]{3,0,2,1:T(4,128)S(1)}, f32[3,9,9,512]{3,0,2,1:T(4,128)}, u32[]{:S(2)}) copy-start(f32[3,9,9,512]{3,0,2,1:T(4,128)} %param.23) | copy-start | bytes 1492996
  26.2 19.7 %all-to-all-start.1 = ((f32[128,1,768]{2,1,0:T(1,128)}), f32[128,1,768]{2,1,0:T(1,128)S(1)}, u32[]{:S(2)}, u32[]{:S(2)}) async-start(f32[128,1,768]{2,1,0:T(1,128)} %bitcast.7), calls=%async_computation.1 | async-start | bytes 786432 | tf_op jit(solution)/shard_map/all_to_all | solution.py:634
  34.1 11.7 %copy-start.6 = (f32[2,25,512]{2,0,1:T(2,128)S(1)}, f32[2,25,512]{2,0,1:T(2,128)}, u32[]{:S(2)}) copy-start(f32[2,25,512]{2,0,1:T(2,128)} %param.39) | copy-start | bytes 307204
  34.2 11.7 %copy-start.7 = (f32[25,512]{1,0:T(8,128)S(1)}, f32[25,512]{1,0:T(8,128)}, u32[]{:S(2)}) copy-start(f32[25,512]{1,0:T(8,128)} %refs_6_.1) | copy-start | bytes 153604
  34.2 11.7 %copy-start.8 = (f32[25,512]{1,0:T(8,128)S(1)}, f32[25,512]{1,0:T(8,128)}, u32[]{:S(2)}) copy-start(f32[25,512]{1,0:T(8,128)} %refs_8_.1) | copy-start | bytes 153604
  34.2 11.7 %copy-start.9 = (f32[25,512]{1,0:T(8,128)S(1)}, f32[25,512]{1,0:T(8,128)}, u32[]{:S(2)}) copy-start(f32[25,512]{1,0:T(8,128)} %refs_9_.1) | copy-start | bytes 153604
  34.2 11.7 %copy-start.10 = (f32[25,512]{1,0:T(8,128)S(1)}, f32[25,512]{1,0:T(8,128)}, u32[]{:S(2)}) copy-start(f32[25,512]{1,0:T(8,128)} %refs_10_.1) | copy-start | bytes 153604
  34.2 11.7 %copy-start.11 = (f32[25,512]{1,0:T(8,128)S(1)}, f32[25,512]{1,0:T(8,128)}, u32[]{:S(2)}) copy-start(f32[25,512]{1,0:T(8,128)} %refs_11_.1) | copy-start | bytes 153604
  34.2 11.7 %copy-start.16 = (f32[25,10]{0,1:T(8,128)S(1)}, f32[25,10]{0,1:T(8,128)}, u32[]{:S(2)}) copy-start(f32[25,10]{0,1:T(8,128)} %param.33) | copy-start | bytes 3004
  34.2 11.7 %copy-start.17 = (f32[10,25]{1,0:T(8,128)S(1)}, f32[10,25]{1,0:T(8,128)}, u32[]{:S(2)}) copy-start(f32[10,25]{1,0:T(8,128)} %refs_12_.1) | copy-start | bytes 3004
  34.2 11.7 %copy-start.20 = (s32[512,2]{0,1:T(2,128)S(1)}, s32[512,2]{0,1:T(2,128)}, u32[]{:S(2)}) copy-start(s32[512,2]{0,1:T(2,128)} %param.35) | copy-start | bytes 12292
  34.3 11.7 %copy-start.22 = (f32[8,1024]{1,0:T(8,128)S(1)}, f32[8,1024]{1,0:T(8,128)}, u32[]{:S(2)}) copy-start(f32[8,1024]{1,0:T(8,128)} %get-tuple-element.21.refs_1_) | copy-start | bytes 98308
  36.9 9.0 %copy-start.15 = (f32[4,512]{1,0:T(4,128)S(1)}, f32[4,512]{1,0:T(4,128)}, u32[]{:S(2)}) copy-start(f32[4,512]{1,0:T(4,128)} %refs_3_.2) | copy-start | bytes 24580
  37.0 18.3 %collective-permute-start = (f32[216,128]{1,0:T(8,128)S(1)}, f32[216,128]{1,0:T(8,128)S(1)}, u32[]{:S(2)}, u32[]{:S(2)}) collective-permute-start(f32[216,128]{1,0:T(8,128)S(1)} %get-tuple-element.27), channel_id=1, source_target_pairs={{0,1},{1,2},{2,3},{3,4},{4,5},{5,6},{6,7},{7,8},{8,9},{9,10},{10,1... | collective-permute-start | bytes 331784 | tf_op jit(solution)/shard_map/ppermute | solution.py:20
  40.3 15.0 %collective-permute-start.1 = (f32[216,128]{1,0:T(8,128)S(1)}, f32[216,128]{1,0:T(8,128)S(1)}, u32[]{:S(2)}, u32[]{:S(2)}) collective-permute-start(f32[216,128]{1,0:T(8,128)S(1)} %get-tuple-element.28), channel_id=1, source_target_pairs={{1,0},{2,1},{3,2},{4,3},{5,4},{6,5},{7,6},{8,7},{9,8},{10,9},{11,1... | collective-permute-start | bytes 331784 | tf_op jit(solution)/shard_map/ppermute | solution.py:20
  46.0 9.4 %copy-start.3 = (f32[4,9,9,512]{3,0,2,1:T(4,128)S(1)}, f32[4,9,9,512]{3,0,2,1:T(4,128)}, u32[]{:S(2)}) copy-start(f32[4,9,9,512]{3,0,2,1:T(4,128)} %param.27) | copy-start | bytes 1990660
  48.5 6.8 %copy-start.2 = (f32[4,9,9,512]{3,0,2,1:T(4,128)S(1)}, f32[4,9,9,512]{3,0,2,1:T(4,128)}, u32[]{:S(2)}) copy-start(f32[4,9,9,512]{3,0,2,1:T(4,128)} %param.28) | copy-start | bytes 1990660
  48.5 6.8 %copy-start.12 = (f32[4,20,20]{2,0,1:T(4,128)S(1)}, f32[4,20,20]{2,0,1:T(4,128)}, u32[]{:S(2)}) copy-start(f32[4,20,20]{2,0,1:T(4,128)} %param.25) | copy-start | bytes 19204
  48.5 6.8 %copy-start.19 = (s32[4,512]{1,0:T(4,128)S(1)}, s32[4,512]{1,0:T(4,128)}, u32[]{:S(2)}) copy-start(s32[4,512]{1,0:T(4,128)} %refs_5_.3) | copy-start | bytes 24580
  48.5 18.5 %all-to-all-start.2 = ((f32[128,1,768]{2,1,0:T(1,128)}), f32[128,1,768]{2,1,0:T(1,128)S(1)}, u32[]{:S(2)}, u32[]{:S(2)}) async-start(f32[128,1,768]{2,1,0:T(1,128)} %bitcast.11), calls=%async_computation.2 | async-start | bytes 786432 | tf_op jit(solution)/shard_map/all_to_all | solution.py:634
  55.3 0.7 copy-start.18
